TPU v7x, 32 devices: a whole 2x2x4 slice. The times are simulated.
32 devices in a mesh: lat: 8 (over y, x, core), lon: 4 (over z).
Axes of the slice: x: 2, y: 2, z: 4, core: 2. Of those that a mesh axis runs over, the one named last changes fastest.
Arguments:
- tracers: float32 [5, 1, 768, 512], P(None, None, 'lat', 'lon'), may hold values from 0.2 to 2
- offsets: int32 [768, 512], P('lat', 'lon'), may hold values from 0 to 255, as said below
- fraction: float32 [768, 512], P('lat', 'lon'), may hold values from 0 to 0.95
- courant_north: float32 [768, 512], P('lat', 'lon'), may hold values from 0 to 0.9
Outputs:
- advected: float32 [5, 1, 768, 512], P(None, None, 'lat', 'lon')
Inputs may be any that keep to these rules, and one draw needn't show every extreme that they name: Let k = min(r, 767 - r) for row r. Rows with k < 24 have offsets from 128 to 255, the largest reached in row 0; rows with 24 <= k < 48 have offsets at most 64, reached in row 24; all other rows have offsets at most 8, reached in row 48. Offsets of adjacent faces g and g + 1 of a row differ by at most one.
All inputs are finite; a program needn't handle non-finite values.
Results may differ from a plain program's by a relative error of at most 0.0003.
Values sent between devices are 32-bit elements; how exact they have to be, the bound alone decides.
No kernel may reach another device: no remote copies, remote signals or barrier semaphores. Data moves between devices by JAX's collectives and lax.ppermute only.
A program may use at most 64 MiB of HBM per device.

v0:
```python
import jax
import jax.numpy as jnp
from jax import lax
from jax.sharding import PartitionSpec as P

wide_weight = 7.0 / 12.0
narrow_weight = 1.0 / 12.0


def with_halo(block, sides, width, periodic):
    for axis, dim in sides:
        count = lax.axis_size(axis)
        forward = [(i, i + 1) for i in range(count - 1)]
        if periodic:
            forward.append((count - 1, 0))
        backward = [(target, source) for source, target in forward]
        low = lax.ppermute(
            lax.slice_in_dim(block, block.shape[dim] - width, None, axis=dim), axis, forward
        )
        high = lax.ppermute(lax.slice_in_dim(block, 0, width, axis=dim), axis, backward)
        block = jnp.concatenate([low, block, high], axis=dim)
    return block


def shifted(value, axis, steps):
    count = lax.axis_size(axis)
    pairs = [(source, (source + steps) % count) for source in range(count)]
    return lax.ppermute(value, axis, pairs)


def frac_flux(courant, right_edge, edge_jump, curvature):
    return courant * (
        right_edge - 0.5 * courant * (edge_jump - (1.0 - 2.0 / 3.0 * courant) * curvature)
    )


def edge_tables(extended):
    cell_count = extended.shape[2] - 4
    centre = extended[:, :, 2 : 2 + cell_count]
    left_edge = wide_weight * (extended[:, :, 1 : 1 + cell_count] + centre) - narrow_weight * (
        extended[:, :, 0:cell_count] + extended[:, :, 3 : 3 + cell_count]
    )
    right_edge = wide_weight * (centre + extended[:, :, 3 : 3 + cell_count]) - narrow_weight * (
        extended[:, :, 1 : 1 + cell_count] + extended[:, :, 4 : 4 + cell_count]
    )
    edge_jump = right_edge - left_edge
    curvature = 6.0 * (centre - 0.5 * (left_edge + right_edge))
    return (right_edge, edge_jump, curvature)


def block_tables(block):
    depth, row_total, width_padded = block.shape
    cell_count = width_padded - 4
    right_edge, edge_jump, curvature = edge_tables(block)
    inner_cells = block[:, :, 2 : 2 + cell_count]
    earlier = lax.broadcasted_iota(jnp.int32, (cell_count, cell_count), 0)
    later = lax.broadcasted_iota(jnp.int32, (cell_count, cell_count), 1)
    strictly_before = (earlier < later).astype(jnp.float32)
    prefix = jnp.dot(
        inner_cells.reshape(depth * row_total, cell_count),
        strictly_before,
        precision=lax.Precision.HIGHEST,
    ).reshape(depth, row_total, cell_count)
    return jnp.stack((prefix, right_edge, edge_jump, curvature))


def as_tables(received):
    return block_tables(received)


def rebase(table, subtract):
    return jnp.concatenate([(table[0] - subtract[:, :, None])[None], table[1:]], axis=0)


def on_device(tracers, offsets, fraction, courant_north):
    tracer_count, level_count, row_count, cells_dev = tracers.shape
    stack_depth = tracer_count * level_count
    field = tracers.reshape(stack_depth, row_count, cells_dev)
    rim_width = 2
    padded = with_halo(field, (("lon", 2),), rim_width, True)
    own_table = block_tables(padded)
    block_total = jnp.sum(field, axis=2)
    got_one, total_one = shifted((padded, block_total), "lon", 1)
    got_two, total_two = shifted((padded, block_total), "lon", 2)
    west_one = rebase(as_tables(got_one), total_one)
    west_two = rebase(as_tables(got_two), total_one + total_two)
    face_index = lax.broadcasted_iota(jnp.int32, (row_count, cells_dev), 1)
    source_index = face_index - offsets + 2 * cells_dev
    joined_width = 3 * cells_dev
    joined = jnp.concatenate([west_two, west_one, own_table], axis=3)
    block_rows = 8

    def lookup_block(block_turn, picked):
        first_row = block_turn * block_rows
        table_block = lax.dynamic_slice_in_dim(joined, first_row, block_rows, 2)
        source_block = lax.dynamic_slice_in_dim(source_index, first_row, block_rows, 0)
        column = lax.broadcasted_iota(jnp.int32, (block_rows, joined_width, cells_dev), 1)
        pick_source = (column == source_block[:, None, :]).astype(jnp.float32)
        pick_depart = (column == source_block[:, None, :] - 1).astype(jnp.float32)
        base_part = jnp.einsum(
            "drk,rkg->drg", table_block[0], pick_source, precision=lax.Precision.HIGHEST
        )
        other_parts = jnp.einsum(
            "tdrk,rkg->tdrg", table_block[1:], pick_depart, precision=lax.Precision.HIGHEST
        )
        result_block = jnp.concatenate([base_part[None], other_parts], axis=0)
        return lax.dynamic_update_slice_in_dim(picked, result_block, first_row, 2)

    picked = lax.fori_loop(
        0,
        row_count // block_rows,
        lookup_block,
        jnp.zeros((4, stack_depth, row_count, cells_dev), jnp.float32),
    )
    base_value = picked[0]
    zonal_flux = (
        own_table[0] - base_value + frac_flux(fraction[None], picked[1], picked[2], picked[3])
    )
    east_flux = shifted(zonal_flux[:, :, 0], "lon", -1)
    next_flux = jnp.concatenate([zonal_flux[:, :, 1:], east_flux[:, :, None]], axis=2)
    after_zonal = field - (next_flux - zonal_flux)
    combined = jnp.concatenate([after_zonal, courant_north[None]], axis=0)
    extended = with_halo(combined, (("lat", 1),), 3, False)
    merid_field = extended[:stack_depth]
    merid_courant = extended[stack_depth]

    def row_window(shift_by):
        return merid_field[:, 2 + shift_by : 3 + shift_by + row_count]

    merid_left = wide_weight * (row_window(-1) + row_window(0)) - narrow_weight * (
        row_window(-2) + row_window(1)
    )
    merid_right = wide_weight * (row_window(0) + row_window(1)) - narrow_weight * (
        row_window(-1) + row_window(2)
    )
    merid_jump = merid_right - merid_left
    merid_curve = 6.0 * (row_window(0) - 0.5 * (merid_left + merid_right))
    global_face = lax.axis_index("lat") * row_count + lax.broadcasted_iota(
        jnp.int32, (row_count + 1, cells_dev), 0
    )
    courant = jnp.where(global_face == 0, jnp.float32(0.0), merid_courant[3 : 4 + row_count])
    merid_flux = frac_flux(courant[None], merid_right, merid_jump, merid_curve)
    advected = after_zonal - (merid_flux[:, 1:] - merid_flux[:, :-1])
    return advected.reshape(tracer_count, level_count, row_count, cells_dev)


def solution(mesh):
    placed = (P(None, None, "lat", "lon"), P("lat", "lon"), P("lat", "lon"), P("lat", "lon"))
    return jax.shard_map(
        on_device,
        mesh=mesh,
        in_specs=placed,
        out_specs=P(None, None, "lat", "lon"),
        check_vma=False,
    )
```

profile of v0, /device:TPU:0, one launch (start us, length us, event | category | flops | bytes accessed | tf_op | source)
XLA Modules:
  0.0 103.8 jit_solution(11685828209533623773)
XLA Ops:
  0.0 1.2 %reduce_sum.9 = f32[5,96]{1,0:T(8,128)S(1)} reduce(f32[5,1,96,128]{3,2,1,0:T(8,128)} %param.6, f32[]{:T(128)} %constant.70.clone.1), dimensions={1,3}, to_apply=%region_0.0 | reduce | flops 60960 | bytes 247684 | tf_op jit(solution)/shard_map/reduce_sum | solution.py:82
  1.2 3.1 %collective-permute-start.3 = (f32[5,96]{1,0:T(8,128)S(1)}, f32[5,96]{1,0:T(8,128)S(1)}, u32[]{:S(2)}, u32[]{:S(2)}) collective-permute-start(f32[5,96]{1,0:T(8,128)S(1)} %reduce_sum.9), channel_id=1, source_target_pairs={{0,1},{1,2},{2,3},{3,0},{4,5},{5,6},{6,7},{7,4},{8,9},{9,10},{10,1... | collective-permute-start | bytes 5768 | tf_op jit(solution)/shard_map/ppermute | solution.py:28
  4.3 2.6 %collective-permute-start.4 = (f32[5,96]{1,0:T(8,128)S(1)}, f32[5,96]{1,0:T(8,128)S(1)}, u32[]{:S(2)}, u32[]{:S(2)}) collective-permute-start(f32[5,96]{1,0:T(8,128)S(1)} %reduce_sum.9), channel_id=1, source_target_pairs={{0,2},{1,3},{2,0},{3,1},{4,6},{5,7},{6,4},{7,5},{8,10},{9,11},{10,... | collective-permute-start | bytes 5768 | tf_op jit(solution)/shard_map/ppermute | solution.py:28
  6.9 1.2 %fusion.53 = (f32[5,96,2]{2,1,0:T(8,128)S(1)}, f32[5,96,2]{2,1,0:T(8,128)S(1)}) fusion(f32[5,96,128]{2,1,0:T(8,128)} %bitcast.90), kind=kLoop, calls=%fused_computation.91 | loop fusion | bytes 15360 | tf_op jit(solution)/shard_map/slice | solution.py:18
  8.2 3.7 %collective-permute-start.1 = (f32[5,96,2]{2,1,0:T(8,128)S(1)}, f32[5,96,2]{2,1,0:T(8,128)S(1)}, u32[]{:S(2)}, u32[]{:S(2)}) collective-permute-start(f32[5,96,2]{2,1,0:T(8,128)S(1)} %get-tuple-element.154), channel_id=1, source_target_pairs={{1,0},{2,1},{3,2},{0,3},{5,4},{6,5},{7,6},{4,7},{9,8},{10,9},{11,1... | collective-permute-start | bytes 11528 | tf_op jit(solution)/shard_map/ppermute | solution.py:20
  11.9 1.2 %fusion.44 = f32[128,480]{0,1:T(8,128)S(1)} fusion(f32[480,128]{1,0:T(8,128)} %bitcast.91), kind=kOutput, calls=%fused_computation.81 | convolution fusion | flops 94388224 | bytes 491520 | tf_op jit(solution)/shard_map/dot_general | solution.py:59
  13.1 1.4 %broadcast_multiply_fusion = (f32[96,128]{1,0:T(8,128)S(1)}, f32[96,128]{1,0:T(8,128)}) fusion(f32[96,128]{1,0:T(8,128)} %param.8), kind=kLoop, calls=%fused_computation.87 | loop fusion | flops 36864 | bytes 147456 | tf_op jit(solution)/shard_map/mul | solution.py:33
  14.5 1.4 %subtract_add_fusion = s32[96,128]{1,0:T(8,128)} fusion(s32[96,128]{1,0:T(8,128)} %param.7), kind=kLoop, calls=%fused_computation.86 | loop fusion | flops 24576 | bytes 98304 | tf_op jit(solution)/shard_map/add | solution.py:88
  16.0 2.8 %collective-permute-done = f32[5,96,2]{2,1,0:T(8,128)S(1)} collective-permute-done((f32[5,96,2]{2,1,0:T(8,128)S(1)}, f32[5,96,2]{2,1,0:T(8,128)S(1)}, u32[]{:S(2)}, u32[]{:S(2)}) %collective-permute-start) | collective-permute-done | bytes 3872 | tf_op jit(solution)/shard_map/ppermute | solution.py:17
  18.8 1.8 %collective-permute-done.1 = f32[5,96,2]{2,1,0:T(8,128)S(1)} collective-permute-done((f32[5,96,2]{2,1,0:T(8,128)S(1)}, f32[5,96,2]{2,1,0:T(8,128)S(1)}, u32[]{:S(2)}, u32[]{:S(2)}) %collective-permute-start.1) | collective-permute-done | bytes 3872 | tf_op jit(solution)/shard_map/ppermute | solution.py:20
  20.6 1.2 %pad_maximum_fusion.1 = f32[5,96,132]{2,1,0:T(8,128)S(1)} fusion(f32[5,96,2]{2,1,0:T(8,128)S(1)} %collective-permute-done.1, f32[5,96,128]{2,1,0:T(8,128)} %bitcast.92, f32[5,96,2]{2,1,0:T(8,128)S(1)} %collective-permute-done), kind=kLoop, calls=%fused_computation.22 | loop fusion | flops 126720 | bytes 506880 | tf_op jit(solution)/shard_map/concatenate | solution.py:21
  21.8 2.4 %collective-permute-start.2 = (f32[5,96,132]{2,1,0:T(8,128)S(1)}, f32[5,96,132]{2,1,0:T(8,128)S(1)}, u32[]{:S(2)}, u32[]{:S(2)}) collective-permute-start(f32[5,96,132]{2,1,0:T(8,128)S(1)} %pad_maximum_fusion.1), channel_id=1, source_target_pairs={{0,2},{1,3},{2,0},{3,1},{4,6},{5,7},{6,4},{7,5},{8,10},{9,11},{10,... | collective-permute-start | bytes 760328 | tf_op jit(solution)/shard_map/ppermute | solution.py:28
  24.5 0.8 subtract_bitcast_fusion
  25.4 19.3 %collective-permute-done.5 = f32[5,96,132]{2,1,0:T(8,128)S(1)} collective-permute-done((f32[5,96,132]{2,1,0:T(8,128)S(1)}, f32[5,96,132]{2,1,0:T(8,128)S(1)}, u32[]{:S(2)}, u32[]{:S(2)}) %collective-permute-start.5) | collective-permute-done | bytes 253472 | tf_op jit(solution)/shard_map/ppermute | solution.py:28
  45.3 9.8 %collective-permute-done.2 = f32[5,96,132]{2,1,0:T(8,128)S(1)} collective-permute-done((f32[5,96,132]{2,1,0:T(8,128)S(1)}, f32[5,96,132]{2,1,0:T(8,128)S(1)}, u32[]{:S(2)}, u32[]{:S(2)}) %collective-permute-start.2) | collective-permute-done | bytes 253472 | tf_op jit(solution)/shard_map/ppermute | solution.py:28
  56.4 1.1 %broadcast_in_dim.37.clone = f32[4,5,96,128]{3,2,1,0:T(8,128)} broadcast(f32[]{:T(128)} %constant.70.clone.1), dimensions={} | broadcast | bytes 983044 | tf_op jit(solution)/shard_map/broadcast_in_dim | solution.py:113
  57.4 34.6 %while.15 = (s32[]{:T(128)}, f32[4,5,96,128]{3,2,1,0:T(8,128)}, s32[96,128]{1,0:T(8,128)}, f32[4,5,96,384]{3,2,1,0:T(8,128)S(1)}, s32[]{:T(128)}, /*index=5*/s32[]{:T(128)}, s32[]{:T(128)}, s32[]{:T(128)}, s32[]{}) while((s32[]{:T(128)}, f32[4,5,96,128]{3,2,1,0:T(8,128)}, s32[96,128]{1,0:T(8,128)}, f32[4,5,96,384]{3,2,1,0:T(8,128)S(1)}, ...), condition=%wide.region_2.0_spmd, body=%wide.region_1.0_spmd.sunk | while | flops 95179784 | bytes 1167531 | solution.py:109
  79.8 0.7 copy_dynamic-update-slice_fusion.2
  91.3 0.7 copy_dynamic-update-slice_fusion.2
  92.1 1.4 %fusion.40 = f32[5,96,128]{2,1,0:T(8,128)S(1)} fusion(f32[5,96,128]{2,1,0:T(8,128)S(1)} %bitcast.95, f32[4,5,96,128]{3,2,1,0:T(8,128)} %get-tuple-element.115, f32[96,128]{1,0:T(8,128)} %get-tuple-element.156, f32[96,128]{1,0:T(8,128)S(1)} %get-tuple-element.155, f32[96,128]{1,0:T(8,128)S(1)} %copy-done.2), kind=kLoop, calls=%fused_computation.69 | loop fusion | flops 430080 | bytes 1622016 | tf_op jit(solution)/shard_map/add | solution.py:117
  93.8 3.5 %collective-permute-done.6 = f32[5,96]{1,0:T(8,128)S(1)} collective-permute-done((f32[5,96]{1,0:T(8,128)S(1)}, f32[5,96]{1,0:T(8,128)S(1)}, u32[]{:S(2)}, u32[]{:S(2)}) %collective-permute-start.6) | collective-permute-done | bytes 1952 | tf_op jit(solution)/shard_map/ppermute | solution.py:28
  97.6 1.3 %collective-permute-start.7 = (f32[6,3,128]{2,1,0:T(4,128)S(1)}, f32[6,3,128]{2,1,0:T(4,128)S(1)}, u32[]{:S(2)}, u32[]{:S(2)}) collective-permute-start(f32[6,3,128]{2,1,0:T(4,128)S(1)} %get-tuple-element.152), channel_id=1, source_target_pairs={{4,0},{8,4},{12,8},{16,12},{20,16},{24,20},{28,24},{5,1},{9,5},{13... | collective-permute-start | bytes 27656 | tf_op jit(solution)/shard_map/ppermute | solution.py:20
  98.9 3.0 %collective-permute-start.8 = (f32[6,3,128]{2,1,0:T(4,128)S(1)}, f32[6,3,128]{2,1,0:T(4,128)S(1)}, u32[]{:S(2)}, u32[]{:S(2)}) collective-permute-start(f32[6,3,128]{2,1,0:T(4,128)S(1)} %get-tuple-element.151), channel_id=1, source_target_pairs={{0,4},{4,8},{8,12},{12,16},{16,20},{20,24},{24,28},{1,5},{5,9},{9,... | collective-permute-start | bytes 27656 | tf_op jit(solution)/shard_map/ppermute | solution.py:17
  103.1 0.7 fusion.20
  (114 shorter events, 37.0 us)
Async XLA Ops:
  0.0 24.5 %copy-start = (f32[5,1,96,128]{3,2,1,0:T(8,128)S(1)}, f32[5,1,96,128]{3,2,1,0:T(8,128)}, u32[]{:S(2)}) copy-start(f32[5,1,96,128]{3,2,1,0:T(8,128)} %param.6) | copy-start | bytes 737284
  1.2 14.8 %collective-permute-start.3 = (f32[5,96]{1,0:T(8,128)S(1)}, f32[5,96]{1,0:T(8,128)S(1)}, u32[]{:S(2)}, u32[]{:S(2)}) collective-permute-start(f32[5,96]{1,0:T(8,128)S(1)} %reduce_sum.9), channel_id=1, source_target_pairs={{0,1},{1,2},{2,3},{3,0},{4,5},{5,6},{6,7},{7,4},{8,9},{9,10},{10,1... | collective-permute-start | bytes 5768 | tf_op jit(solution)/shard_map/ppermute | solution.py:28
  4.3 11.7 %collective-permute-start.4 = (f32[5,96]{1,0:T(8,128)S(1)}, f32[5,96]{1,0:T(8,128)S(1)}, u32[]{:S(2)}, u32[]{:S(2)}) collective-permute-start(f32[5,96]{1,0:T(8,128)S(1)} %reduce_sum.9), channel_id=1, source_target_pairs={{0,2},{1,3},{2,0},{3,1},{4,6},{5,7},{6,4},{7,5},{8,10},{9,11},{10,... | collective-permute-start | bytes 5768 | tf_op jit(solution)/shard_map/ppermute | solution.py:28
  8.0 10.7 %collective-permute-start = (f32[5,96,2]{2,1,0:T(8,128)S(1)}, f32[5,96,2]{2,1,0:T(8,128)S(1)}, u32[]{:S(2)}, u32[]{:S(2)}) collective-permute-start(f32[5,96,2]{2,1,0:T(8,128)S(1)} %get-tuple-element.153), channel_id=1, source_target_pairs={{0,1},{1,2},{2,3},{3,0},{4,5},{5,6},{6,7},{7,4},{8,9},{9,10},{10,1... | collective-permute-start | bytes 11528 | tf_op jit(solution)/shard_map/ppermute | solution.py:17
  8.2 12.4 %collective-permute-start.1 = (f32[5,96,2]{2,1,0:T(8,128)S(1)}, f32[5,96,2]{2,1,0:T(8,128)S(1)}, u32[]{:S(2)}, u32[]{:S(2)}) collective-permute-start(f32[5,96,2]{2,1,0:T(8,128)S(1)} %get-tuple-element.154), channel_id=1, source_target_pairs={{1,0},{2,1},{3,2},{0,3},{5,4},{6,5},{7,6},{4,7},{9,8},{10,9},{11,1... | collective-permute-start | bytes 11528 | tf_op jit(solution)/shard_map/ppermute | solution.py:20
  21.8 33.3 %collective-permute-start.2 = (f32[5,96,132]{2,1,0:T(8,128)S(1)}, f32[5,96,132]{2,1,0:T(8,128)S(1)}, u32[]{:S(2)}, u32[]{:S(2)}) collective-permute-start(f32[5,96,132]{2,1,0:T(8,128)S(1)} %pad_maximum_fusion.1), channel_id=1, source_target_pairs={{0,2},{1,3},{2,0},{3,1},{4,6},{5,7},{6,4},{7,5},{8,10},{9,11},{10,... | collective-permute-start | bytes 760328 | tf_op jit(solution)/shard_map/ppermute | solution.py:28
  24.2 20.5 %collective-permute-start.5 = (f32[5,96,132]{2,1,0:T(8,128)S(1)}, f32[5,96,132]{2,1,0:T(8,128)S(1)}, u32[]{:S(2)}, u32[]{:S(2)}) collective-permute-start(f32[5,96,132]{2,1,0:T(8,128)S(1)} %pad_maximum_fusion.1), channel_id=1, source_target_pairs={{0,1},{1,2},{2,3},{3,0},{4,5},{5,6},{6,7},{7,4},{8,9},{9,10},{10,1... | collective-permute-start | bytes 760328 | tf_op jit(solution)/shard_map/ppermute | solution.py:28
  57.4 34.6 %copy-start.2 = (f32[96,128]{1,0:T(8,128)S(1)}, f32[96,128]{1,0:T(8,128)}, u32[]{:S(2)}) copy-start(f32[96,128]{1,0:T(8,128)} %param.8) | copy-start | bytes 147460
  92.1 5.5 %copy-start.1 = (f32[96,128]{1,0:T(8,128)S(1)}, f32[96,128]{1,0:T(8,128)}, u32[]{:S(2)}) copy-start(f32[96,128]{1,0:T(8,128)} %param.9) | copy-start | bytes 147460
  93.6 3.7 %collective-permute-start.6 = (f32[5,96]{1,0:T(8,128)S(1)}, f32[5,96]{1,0:T(8,128)S(1)}, u32[]{:S(2)}, u32[]{:S(2)}) collective-permute-start(f32[5,96]{1,0:T(8,128)S(1)} %slice_reduce_fusion), channel_id=1, source_target_pairs={{0,3},{1,0},{2,1},{3,2},{4,7},{5,4},{6,5},{7,6},{8,11},{9,8},{10,9... | collective-permute-start | bytes 5768 | tf_op jit(solution)/shard_map/ppermute | solution.py:28
  97.6 4.4 %collective-permute-start.7 = (f32[6,3,128]{2,1,0:T(4,128)S(1)}, f32[6,3,128]{2,1,0:T(4,128)S(1)}, u32[]{:S(2)}, u32[]{:S(2)}) collective-permute-start(f32[6,3,128]{2,1,0:T(4,128)S(1)} %get-tuple-element.152), channel_id=1, source_target_pairs={{4,0},{8,4},{12,8},{16,12},{20,16},{24,20},{28,24},{5,1},{9,5},{13... | collective-permute-start | bytes 27656 | tf_op jit(solution)/shard_map/ppermute | solution.py:20
  98.9 3.9 %collective-permute-start.8 = (f32[6,3,128]{2,1,0:T(4,128)S(1)}, f32[6,3,128]{2,1,0:T(4,128)S(1)}, u32[]{:S(2)}, u32[]{:S(2)}) collective-permute-start(f32[6,3,128]{2,1,0:T(4,128)S(1)} %get-tuple-element.151), channel_id=1, source_target_pairs={{0,4},{4,8},{8,12},{12,16},{16,20},{20,24},{24,28},{1,5},{5,9},{9,... | collective-permute-start | bytes 27656 | tf_op jit(solution)/shard_map/ppermute | solution.py:17
where the time goes:
time: 106 us; the launch traced here: 104 us
  waiting for transfers between devices  37.9 us (36%)
  other arithmetic  18.6 us (18%)
  matrix products  18.6 us (18%)
  starting transfers between devices  16.7 us (16%)
  local copies, waits for them, and re-layouts  11.6 us (11%)
    ppermute x5, waiting for transfers between devices, shifted(): return lax.ppermute(value, axis, pairs)  32.6 us
    dot_general x12, matrix products, lookup_block(): jnp.einsum('tdrk,rkg->tdrg', table_block[1:], pick_depart, precision=lax....  8.63 us
    dynamic_update_slice x12, local copies, waits for them, and re-layouts, lookup_block(): return lax.dynamic_update_slice_in_dim(picked, result_block, first_row, 2)  8.55 us
    ppermute x5, starting transfers between devices, shifted(): return lax.ppermute(value, axis, pairs)  8.47 us
    sub x12, other arithmetic, lookup_block(): pick_depart = (column == source_block[:, None, :] - 1).astype(jnp.float32)  8.35 us
    dot_general x12, matrix products, lookup_block(): jnp.einsum('drk,rkg->drg', table_block[0], pick_source, precision=lax.Pre...  8.09 us
    ppermute x2, starting transfers between devices, with_halo(): lax.ppermute(lax.slice_in_dim(block, 0, width, axis=dim), axis, backward)  5.04 us
    ppermute x2, waiting for transfers between devices, with_halo(): lax.ppermute(lax.slice_in_dim(block, block.shape[dim] - width, None, axis...  3.5 us
  transfers between devices with their start and end apart: 9, of which 6 were waited for; matrix products, arithmetic and copies ran while one was open for 7% of the time, Pallas kernels for 0%

commit v1 on v0

v1 whole, which is shorter than its diff:
```python
import functools

import jax
import jax.numpy as jnp
from jax import lax
from jax.experimental import pallas as pl
from jax.experimental.pallas import tpu as pltpu
from jax.sharding import PartitionSpec as P

WIDE = 7.0 / 12.0
NARROW = 1.0 / 12.0
POLAR = 24
BAND = 24
SEG = 24
WEST = 11
EAST0 = 12
FAR0 = 14
OFF_LANE = 120
FRAC_LANE = 121

f32 = jnp.float32
i32 = jnp.int32
VMEM = pltpu.VMEM


def lanes(shape):
    return lax.broadcasted_iota(i32, shape, 1)


def rolled(value, steps):
    steps = steps % value.shape[1]
    return pltpu.roll(value, steps, 1) if steps else value


def pick(table, index):
    return jnp.take_along_axis(table, index, axis=1, mode="promise_in_bounds")


def parabola(c, right, left, centre):
    jump = right - left
    curve = 6.0 * centre - 3.0 * (left + right)
    return c * (right - 0.5 * c * (jump - (1.0 - (2.0 / 3.0) * c) * curve))


def running_sum(value):
    count = value.shape[1]
    shape = (count, count)
    upto = lax.broadcasted_iota(i32, shape, 0) <= lax.broadcasted_iota(i32, shape, 1)
    ones = upto.astype(jnp.bfloat16)
    high = value.astype(jnp.bfloat16)
    low = (value - high.astype(f32)).astype(jnp.bfloat16)
    return jnp.dot(high, ones, preferred_element_type=f32) + jnp.dot(
        low, ones, preferred_element_type=f32
    )


def edges(value):
    right = WIDE * (value + rolled(value, -1)) - NARROW * (rolled(value, 1) + rolled(value, -2))
    return right, rolled(right, 1)


def edges_between(value, west, east):
    lane = lanes(value.shape)
    last = value.shape[1] - 1
    back_one = jnp.where(lane < 1, rolled(west, 1), rolled(value, 1))
    back_two = jnp.where(lane < 2, rolled(west, 2), rolled(value, 2))
    on_one = jnp.where(lane > last - 1, rolled(east, -1), rolled(value, -1))
    on_two = jnp.where(lane > last - 2, rolled(east, -2), rolled(value, -2))
    right = WIDE * (value + on_one) - NARROW * (back_one + on_two)
    left = WIDE * (back_one + value) - NARROW * (back_two + on_one)
    return right, left


def pack_kernel(tracers, offsets, fraction, to_east, to_west, pole_one, pole_two):
    depth, row_count, cells = tracers.shape
    shape = (row_count, cells)
    lane = lanes(shape)
    place, tracer = lane % SEG, lane // SEG
    east_message = jnp.zeros(shape, f32)
    west_message = jnp.where(
        lane == OFF_LANE,
        rolled(offsets[...].astype(f32), OFF_LANE),
        jnp.where(lane == FRAC_LANE, rolled(fraction[...], FRAC_LANE), 0.0),
    )
    for t in range(depth):
        field = tracers[t]
        mine = tracer == t
        east_message = jnp.where(
            mine & (place < WEST), rolled(field, t * SEG + WEST - cells), east_message
        )
        near = mine & (place >= EAST0) & (place < FAR0)
        far = mine & (place >= FAR0) & (place < FAR0 + 2)
        west_message = jnp.where(near, rolled(field, t * SEG + EAST0), west_message)
        west_message = jnp.where(far, rolled(field, t * SEG + FAR0 + 2 - cells), west_message)
    to_east[...] = east_message
    to_west[...] = west_message
    south = lax.axis_index("lat") == 0
    start = pl.multiple_of(jnp.where(south, 0, row_count - POLAR - BAND), 8)
    inner = pl.multiple_of(jnp.where(south, 0, row_count - POLAR), 8)
    pole_one[...] = tracers[:, pl.ds(start, POLAR + BAND), :]
    pole_two[...] = tracers[:, pl.ds(inner, POLAR), :]


def own_kernel(tracers, offsets, fraction, flux, seam_west, seam_east, seam_offsets, seam_fraction):
    depth, row_count, cells = tracers.shape
    shape = (row_count, cells)
    lane = lanes(shape)
    place, tracer = lane % SEG, lane // SEG
    offset = offsets[...]
    courant = fraction[...]
    index = (lane - offset - 1) & (cells - 1)
    west_rows = jnp.zeros(shape, f32)
    east_rows = jnp.zeros(shape, f32)
    for t in range(depth):
        field = tracers[t]
        right, left = edges(field)
        sums = running_sum(field)
        flux[t] = (
            sums
            - field
            - pick(sums, index)
            + parabola(courant, pick(right, index), pick(left, index), pick(field, index))
        )
        mine = tracer == t
        west_rows = jnp.where(
            mine & (place >= WEST) & (place < 2 * WEST + 1), rolled(field, t * SEG + WEST), west_rows
        )
        east_rows = jnp.where(
            mine & (place < EAST0), rolled(field, t * SEG + EAST0 - cells), east_rows
        )
    seam_west[...] = west_rows
    seam_east[...] = east_rows
    first = (place - WEST) & (cells - 1)
    final = jnp.full(shape, cells - 1, i32)
    seam_offsets[0] = pick(offset, first)
    seam_offsets[1] = pick(offset, final)
    seam_fraction[0] = pick(courant, first)
    seam_fraction[1] = pick(courant, final)


def seam_flux(rows, offset, courant, place):
    cells = rows.shape[1]
    right, left = edges(rows)
    sums = rows
    for step in (1, 2, 4, 8, 16):
        sums = sums + jnp.where(place >= step, rolled(sums, step), 0.0)
    index = (lanes(rows.shape) - offset - 1) & (cells - 1)
    return (
        sums
        - rows
        - pick(sums, index)
        + parabola(courant, pick(right, index), pick(left, index), pick(rows, index))
    )


def seam_kernel(
    tracers, flux, seam_west, seam_east, seam_offsets, seam_fraction, courant_north,
    from_west, from_east, after, message_a, message_b,
):
    depth, row_count, cells = tracers.shape
    shape = (row_count, cells)
    lane = lanes(shape)
    place = lane % SEG
    west_rows = jnp.where(place < WEST, from_west[...], seam_west[...])
    west_flux = seam_flux(west_rows, seam_offsets[0], seam_fraction[0], place)
    received = from_east[...]
    east_rows = jnp.where(place < EAST0, seam_east[...], received)
    next_face = place == EAST0
    next_offset = pick(received, jnp.full(shape, OFF_LANE, i32)).astype(i32)
    next_fraction = pick(received, jnp.full(shape, FRAC_LANE, i32))
    east_flux = seam_flux(
        east_rows,
        jnp.where(next_face, next_offset, seam_offsets[1]),
        jnp.where(next_face, next_fraction, seam_fraction[1]),
        place,
    )
    even = lax.axis_index("lat") % 2 == 0
    for t in range(depth):
        west_faces = rolled(west_flux, -(t * SEG + WEST))
        east_faces = rolled(east_flux, cells - 1 - (t * SEG + EAST0 - 1))
        face = jnp.where(
            lane < WEST, west_faces, jnp.where(lane == cells - 1, east_faces, flux[t])
        )
        following = rolled(jnp.where(lane == 0, east_faces, face), -1)
        after[t] = tracers[t] - (following - face)
        top = after[t, row_count - 3 :]
        bottom = after[t, :3]
        message_a[3 * t : 3 * t + 3] = jnp.where(even, top, bottom)
        message_b[3 * t : 3 * t + 3] = jnp.where(even, bottom, top)
    message_a[3 * depth : 3 * depth + 1] = courant_north[:1]
    message_b[3 * depth : 3 * depth + 1] = courant_north[:1]


def polar_rows(own, west, west_two, near, far, offset, courant, next_offset, next_courant):
    cells = own.shape[1]
    lane = lanes(own.shape)
    right_one, left_one = edges_between(west, west_two, own)
    right_two, left_two = edges_between(west_two, far, west)
    sums = running_sum(own)
    sums_one = running_sum(west)
    sums_two = running_sum(west_two)
    total, total_one, total_two = (s[:, cells - 1 :] for s in (sums, sums_one, sums_two))
    source = lane - offset - 1
    index = source & (cells - 1)
    near_block = source >= -cells

    def both(one, two):
        return jnp.where(near_block, pick(one, index), pick(two, index))

    face = (
        sums
        - own
        + total_one
        - jnp.where(near_block, pick(sums_one, index), pick(sums_two, index) - total_two)
        + parabola(courant, both(right_one, right_two), both(left_one, left_two), both(west, west_two))
    )
    index = (cells - 1 - next_offset) & (cells - 1)
    last = (
        total
        + total_one
        - pick(sums_one, index)
        + parabola(next_courant, pick(right_one, index), pick(left_one, index), pick(west, index))
    )
    following = rolled(jnp.where(lane == 0, last, face), -1)
    return own - (following - face)


def band_rows(own, west, near, offset, courant, next_offset, next_courant):
    cells = own.shape[1]
    lane = lanes(own.shape)
    right, left = edges_between(own, west, near)
    right_one, left_one = edges_between(west, west, own)
    sums = running_sum(own)
    sums_one = running_sum(west)
    total, total_one = sums[:, cells - 1 :], sums_one[:, cells - 1 :]
    source = lane - offset - 1
    index = source & (cells - 1)
    inside = source >= 0

    def both(here, there):
        return jnp.where(inside, pick(here, index), pick(there, index))

    face = (
        sums
        - own
        - both(sums, sums_one - total_one)
        + parabola(courant, both(right, right_one), both(left, left_one), both(own, west))
    )
    index = (cells - 1 - next_offset) & (cells - 1)
    last = (
        total
        - pick(sums, index)
        + parabola(next_courant, pick(right, index), pick(left, index), pick(own, index))
    )
    following = rolled(jnp.where(lane == 0, last, face), -1)
    return own - (following - face)


def merid_kernel(
    lat_count, tracers, offsets, fraction, courant_north, after, from_east, from_far, pole_one, pole_two,
    message_a, message_b, out, wide, courant_rows,
):
    depth, row_count, cells = tracers.shape
    lat = lax.axis_index("lat")
    south, north = lat == 0, lat == lat_count - 1
    even = lat % 2 == 0
    for t in range(depth):
        wide[t, 8 : 8 + row_count] = after[t]
        below = jnp.where(even, message_b[3 * t : 3 * t + 3], message_a[3 * t : 3 * t + 3])
        above = jnp.where(even, message_a[3 * t : 3 * t + 3], message_b[3 * t : 3 * t + 3])
        wide[t, 5:8] = below
        wide[t, 8 + row_count : 11 + row_count] = above
    last = 3 * depth
    courant_rows[7 : 7 + row_count] = courant_north[...]
    courant_rows[7 + row_count : 8 + row_count] = jnp.where(
        even, message_a[last : last + 1], message_b[last : last + 1]
    )

    @pl.when(south)
    def _():
        courant_rows[7:8] = jnp.zeros((1, cells), f32)

    @pl.when(south | north)
    def _():
        def part(first, in_window, count, polar):
            rows = pl.ds(pl.multiple_of(first, 8), count)
            window = pl.ds(pl.multiple_of(in_window, 8), count)
            offset, courant = offsets[rows], fraction[rows]
            east, far_cells = from_east[rows], from_far[rows]
            shape = east.shape
            next_offset = pick(east, jnp.full(shape, OFF_LANE, i32)).astype(i32)
            next_courant = pick(east, jnp.full(shape, FRAC_LANE, i32))
            for t in range(depth):
                own = tracers[t, rows]
                near = rolled(east, -(t * SEG + EAST0))
                common = (offset, courant, next_offset, next_courant)
                if polar:
                    far = rolled(far_cells, cells - 2 - (t * SEG + FAR0))
                    result = polar_rows(own, pole_one[t, window], pole_two[t], near, far, *common)
                else:
                    result = band_rows(own, pole_one[t, window], near, *common)
                wide[t, pl.ds(pl.multiple_of(first + 8, 8), count)] = result

        base = row_count - POLAR - BAND
        part(jnp.where(south, 0, base + BAND), jnp.where(south, 0, BAND), POLAR, True)
        part(jnp.where(south, POLAR, base), jnp.where(south, POLAR, 0), BAND, False)

    courant = courant_rows[...]
    for t in range(depth):
        value = wide[t]
        size = row_count + 16
        right = WIDE * (value + pltpu.roll(value, size - 1, 0)) - NARROW * (
            pltpu.roll(value, 1, 0) + pltpu.roll(value, size - 2, 0)
        )
        left = pltpu.roll(right, 1, 0)
        face = parabola(courant, right, left, value)
        result = value - (face - pltpu.roll(face, 1, 0))
        out[t] = result[8 : 8 + row_count]


def in_vmem(*values):
    return [pltpu.with_memory_space_constraint(value, VMEM) for value in values]


def whole(count):
    return [pl.BlockSpec(memory_space=VMEM)] * count


def on_device(lat_count, lon_count, tracers, offsets, fraction, courant_north):
    tracer_count, level_count, row_count, cells = tracers.shape
    depth = tracer_count * level_count
    shape = (row_count, cells)
    field = tracers.reshape(depth, row_count, cells)
    field, offsets, fraction, courant_north = in_vmem(field, offsets, fraction, courant_north)

    def along_lon(value, steps, lats=range(lat_count)):
        pairs = [
            (l * lon_count + o, l * lon_count + (o + steps) % lon_count)
            for l in lats
            for o in range(lon_count)
        ]
        return lax.ppermute(value, ("lat", "lon"), pairs)

    def along_lat(value, first):
        pairs = []
        for l in range(first, lat_count - 1, 2):
            for o in range(lon_count):
                low, high = l * lon_count + o, (l + 1) * lon_count + o
                pairs += [(low, high), (high, low)]
        return lax.ppermute(value, ("lat", "lon"), pairs)

    to_east, to_west, pole_one, pole_two = pl.pallas_call(
        pack_kernel,
        out_shape=[
            VMEM(shape, f32),
            VMEM(shape, f32),
            VMEM((depth, POLAR + BAND, cells), f32),
            VMEM((depth, POLAR, cells), f32),
        ],
        in_specs=whole(3),
        out_specs=whole(4),
        name="pack",
    )(field, offsets, fraction)
    from_west = along_lon(to_east, 1)
    from_east = along_lon(to_west, -1)
    poles = (0, lat_count - 1)
    from_far = from_east if lon_count == 4 else along_lon(to_west, 3)
    pole_one = along_lon(pole_one, 1, poles)
    pole_two = along_lon(pole_two, 2, poles)

    own = pl.pallas_call(
        own_kernel,
        out_shape=[
            VMEM((depth, row_count, cells), f32),
            VMEM(shape, f32),
            VMEM(shape, f32),
            VMEM((2, row_count, cells), i32),
            VMEM((2, row_count, cells), f32),
        ],
        in_specs=whole(3),
        out_specs=whole(5),
        name="own",
    )(field, offsets, fraction)

    after, message_a, message_b = pl.pallas_call(
        seam_kernel,
        out_shape=[
            VMEM((depth, row_count, cells), f32),
            VMEM((3 * depth + 1, cells), f32),
            VMEM((3 * depth + 1, cells), f32),
        ],
        in_specs=whole(9),
        out_specs=whole(3),
        name="seam",
    )(field, *in_vmem(*own), courant_north, *in_vmem(from_west, from_east))
    message_b = along_lat(message_b, 1)
    message_a = along_lat(message_a, 0)

    out = pl.pallas_call(
        functools.partial(merid_kernel, lat_count),
        out_shape=jax.ShapeDtypeStruct((depth, row_count, cells), f32),
        in_specs=whole(11),
        out_specs=pl.BlockSpec(memory_space=VMEM),
        scratch_shapes=[
            VMEM((depth, row_count + 16, cells), f32),
            VMEM((row_count + 16, cells), f32),
        ],
        name="merid",
    )(
        field, offsets, fraction, courant_north,
        *in_vmem(after, from_east, from_far, pole_one, pole_two, message_a, message_b),
    )
    return out.reshape(tracers.shape)


def solution(mesh):
    placed = (P(None, None, "lat", "lon"), P("lat", "lon"), P("lat", "lon"), P("lat", "lon"))
    return jax.shard_map(
        functools.partial(on_device, mesh.shape["lat"], mesh.shape["lon"]),
        mesh=mesh,
        in_specs=placed,
        out_specs=P(None, None, "lat", "lon"),
        check_vma=False,
    )
```

time: 106 us -> 25.8 us (0.24)
  the two profiles are of different devices: /device:TPU:0 before, /device:TPU:1 now
where the time goes in v1:
time: 25.8 us; the launch traced here: 25.4 us
  starting transfers between devices  15.9 us (62%)
  Pallas kernels  3.85 us (15%)
  waiting for transfers between devices  3.04 us (12%)
  local copies, waits for them, and re-layouts  2.56 us (10%)
    ppermute x2, starting transfers between devices, along_lat(): return lax.ppermute(value, ('lat', 'lon'), pairs)  10.3 us
    ppermute x4, starting transfers between devices, along_lon(): return lax.ppermute(value, ('lat', 'lon'), pairs)  5.61 us
    ppermute x2, waiting for transfers between devices, along_lat(): return lax.ppermute(value, ('lat', 'lon'), pairs)  3.03 us
    unnamed x12, local copies, waits for them, and re-layouts  2.56 us
    pallas_call x1, Pallas kernels, on_device(): pl.pallas_call(own_kernel, out_shape=[VMEM((depth, row_count, cells), f32...  1.47 us
    pallas_call x1, Pallas kernels, on_device(): pl.pallas_call(seam_kernel, out_shape=[VMEM((depth, row_count, cells), f3...  1.11 us
    pallas_call x1, Pallas kernels, on_device(): pl.pallas_call(functools.partial(merid_kernel, lat_count), out_shape=jax....  0.98 us
  transfers between devices with their start and end apart: 6, of which 1 were waited for; matrix products, arithmetic and copies ran while one was open for 0% of the time, Pallas kernels for 10%

profile of v1, /device:TPU:1, one launch (start us, length us, event | category | flops | bytes accessed | tf_op | source)
XLA Modules:
  0.0 25.4 jit_solution(10364227831559922733)
XLA Ops:
  0.0 0.9 %copy-done = f32[5,1,96,128]{3,2,1,0:T(8,128)S(1)} copy-done((f32[5,1,96,128]{3,2,1,0:T(8,128)S(1)}, f32[5,1,96,128]{3,2,1,0:T(8,128)}, u32[]{:S(2)}) %copy-start) | copy-done | bytes 245784
  0.9 0.8 %copy-done.1 = s32[96,128]{1,0:T(8,128)S(1)} copy-done((s32[96,128]{1,0:T(8,128)S(1)}, s32[96,128]{1,0:T(8,128)}, u32[]{:S(2)}) %copy-start.1) | copy-done | bytes 49176
  1.7 0.8 %copy-done.3 = f32[96,128]{1,0:T(8,128)S(1)} copy-done((f32[96,128]{1,0:T(8,128)S(1)}, f32[96,128]{1,0:T(8,128)}, u32[]{:S(2)}) %copy-start.3) | copy-done | bytes 49176
  2.5 0.3 %pack.1 = (f32[96,128]{1,0:T(8,128)S(1)}, f32[96,128]{1,0:T(8,128)S(1)}, f32[5,48,128]{2,1,0:T(8,128)S(1)}, f32[5,24,128]{2,1,0:T(8,128)S(1)}) custom-call(f32[5,96,128]{2,1,0:T(8,128)S(1)} %bitcast.4, s32[96,128]{1,0:T(8,128)S(1)} %copy-done.1, f32[96,128]{1,0:T(8,128)S(1)} %copy-done.3), custom_call_target="tpu_custom_call" | custom-call | tf_op jit(solution)/shard_map/pack/pallas_call | solution.py:352
  2.8 0.7 %collective-permute-start.2 = (f32[5,48,128]{2,1,0:T(8,128)S(1)}, f32[5,48,128]{2,1,0:T(8,128)S(1)}, u32[]{:S(2)}, u32[]{:S(2)}) collective-permute-start(f32[5,48,128]{2,1,0:T(8,128)S(1)} %get-tuple-element.25), channel_id=1, source_target_pairs={{0,1},{1,2},{2,3},{3,0},{28,29},{29,30},{30,31},{31,28}} | collective-permute-start | bytes 368648 | tf_op jit(solution)/shard_map/ppermute | solution.py:342
  3.5 0.7 %collective-permute-start.3 = (f32[5,24,128]{2,1,0:T(8,128)S(1)}, f32[5,24,128]{2,1,0:T(8,128)S(1)}, u32[]{:S(2)}, u32[]{:S(2)}) collective-permute-start(f32[5,24,128]{2,1,0:T(8,128)S(1)} %get-tuple-element.26), channel_id=1, source_target_pairs={{0,2},{1,3},{2,0},{3,1},{28,30},{29,31},{30,28},{31,29}} | collective-permute-start | bytes 184328 | tf_op jit(solution)/shard_map/ppermute | solution.py:342
  4.2 2.2 %collective-permute-start = (f32[96,128]{1,0:T(8,128)S(1)}, f32[96,128]{1,0:T(8,128)S(1)}, u32[]{:S(2)}, u32[]{:S(2)}) collective-permute-start(f32[96,128]{1,0:T(8,128)S(1)} %get-tuple-element.22), channel_id=1, source_target_pairs={{0,1},{1,2},{2,3},{3,0},{4,5},{5,6},{6,7},{7,4},{8,9},{9,10},{10,1... | collective-permute-start | bytes 147464 | tf_op jit(solution)/shard_map/ppermute | solution.py:342
  6.4 2.1 %collective-permute-start.1 = (f32[96,128]{1,0:T(8,128)S(1)}, f32[96,128]{1,0:T(8,128)S(1)}, u32[]{:S(2)}, u32[]{:S(2)}) collective-permute-start(f32[96,128]{1,0:T(8,128)S(1)} %get-tuple-element.23), channel_id=1, source_target_pairs={{0,3},{1,0},{2,1},{3,2},{4,7},{5,4},{6,5},{7,6},{8,11},{9,8},{10,9... | collective-permute-start | bytes 147464 | tf_op jit(solution)/shard_map/ppermute | solution.py:342
  8.5 1.5 %own.1 = (f32[5,96,128]{2,1,0:T(8,128)S(1)}, f32[96,128]{1,0:T(8,128)S(1)}, f32[96,128]{1,0:T(8,128)S(1)}, s32[2,96,128]{2,1,0:T(8,128)S(1)}, f32[2,96,128]{2,1,0:T(8,128)S(1)}) custom-call(f32[5,96,128]{2,1,0:T(8,128)S(1)} %bitcast.5, s32[96,128]{1,0:T(8,128)S(1)} %copy-done.1, f32[96,128]{1,0:T(8,128)S(1)} %copy-done.3), custom_call_target="tpu_custom_call" | custom-call | tf_op jit(solution)/shard_map/own/pallas_call | solution.py:371
  9.9 0.0 collective-permute-done.from_west
  9.9 0.0 collective-permute-done.1.from_east.from_far
  10.0 0.0 copy-done.5
  10.0 0.0 copy-start.2
  10.0 0.0 copy-start.4
  10.0 1.1 %seam.1 = (f32[5,96,128]{2,1,0:T(8,128)S(1)}, f32[16,128]{1,0:T(8,128)S(1)}, f32[16,128]{1,0:T(8,128)S(1)}) custom-call(f32[5,96,128]{2,1,0:T(8,128)S(1)} %bitcast.6, f32[5,96,128]{2,1,0:T(8,128)S(1)} %get-tuple-element.17.flux, f32[96,128]{1,0:T(8,128)S(1)} %get-tuple-element.18.seam_west, f32[96,128]{1,0:T(8,128)S(1)} %get-tuple-element.19.seam_east, ...), custom_call_target="tpu_custom_call" | custom-call | tf_op jit(solution)/shard_map/seam/pallas_call | solution.py:385
  11.1 8.4 %collective-permute-start.4 = (f32[16,128]{1,0:T(8,128)S(1)}, f32[16,128]{1,0:T(8,128)S(1)}, u32[]{:S(2)}, u32[]{:S(2)}) collective-permute-start(f32[16,128]{1,0:T(8,128)S(1)} %get-tuple-element.27), channel_id=1, source_target_pairs={{0,4},{4,0},{1,5},{5,1},{2,6},{6,2},{3,7},{7,3},{8,12},{12,8},{9,1... | collective-permute-start | bytes 24584 | tf_op jit(solution)/shard_map/ppermute | solution.py:350
  19.5 1.9 %collective-permute-start.5 = (f32[16,128]{1,0:T(8,128)S(1)}, f32[16,128]{1,0:T(8,128)S(1)}, u32[]{:S(2)}, u32[]{:S(2)}) collective-permute-start(f32[16,128]{1,0:T(8,128)S(1)} %get-tuple-element.28), channel_id=1, source_target_pairs={{4,8},{8,4},{5,9},{9,5},{6,10},{10,6},{7,11},{11,7},{12,16},{16,12... | collective-permute-start | bytes 24584 | tf_op jit(solution)/shard_map/ppermute | solution.py:350
  21.4 0.0 collective-permute-done.4.message_a
  21.4 3.0 %collective-permute-done.5.message_b = f32[16,128]{1,0:T(8,128)S(1)} collective-permute-done((f32[16,128]{1,0:T(8,128)S(1)}, f32[16,128]{1,0:T(8,128)S(1)}, u32[]{:S(2)}, u32[]{:S(2)}) %collective-permute-start.5) | collective-permute-done | bytes 8224 | tf_op jit(solution)/shard_map/ppermute | solution.py:350
  24.4 0.0 collective-permute-done.3.pole_two
  24.4 0.0 collective-permute-done.2.pole_one
  24.4 0.0 copy-done.2
  24.4 0.0 copy-done.4
  24.5 1.0 %merid.1 = f32[5,96,128]{2,1,0:T(8,128)} custom-call(f32[5,96,128]{2,1,0:T(8,128)S(1)} %bitcast.7, s32[96,128]{1,0:T(8,128)S(1)} %copy-done.2, f32[96,128]{1,0:T(8,128)S(1)} %copy-done.4, f32[96,128]{1,0:T(8,128)S(1)} %copy-done.5, f32[5,96,128]{2,1,0:T(8,128)S(1)} %get-tuple-element.24.after, f32[96,128]{1,0:T(8,128)S(1)} %collective-permute-done.1.from_east.from_far, ...), custom_call_target="tpu_custom_call" | custom-call | tf_op jit(solution)/shard_map/merid/pallas_call | solution.py:399
  (4 shorter events, 0.0 us)
Async XLA Ops:
  0.0 0.9 %copy-start = (f32[5,1,96,128]{3,2,1,0:T(8,128)S(1)}, f32[5,1,96,128]{3,2,1,0:T(8,128)}, u32[]{:S(2)}) copy-start(f32[5,1,96,128]{3,2,1,0:T(8,128)} %param.4) | copy-start | bytes 737284
  0.9 0.8 %copy-start.1 = (s32[96,128]{1,0:T(8,128)S(1)}, s32[96,128]{1,0:T(8,128)}, u32[]{:S(2)}) copy-start(s32[96,128]{1,0:T(8,128)} %offsets.5) | copy-start | bytes 147460
  1.7 0.8 %copy-start.3 = (f32[96,128]{1,0:T(8,128)S(1)}, f32[96,128]{1,0:T(8,128)}, u32[]{:S(2)}) copy-start(f32[96,128]{1,0:T(8,128)} %fraction.5) | copy-start | bytes 147460
  2.8 21.6 %collective-permute-start.2 = (f32[5,48,128]{2,1,0:T(8,128)S(1)}, f32[5,48,128]{2,1,0:T(8,128)S(1)}, u32[]{:S(2)}, u32[]{:S(2)}) collective-permute-start(f32[5,48,128]{2,1,0:T(8,128)S(1)} %get-tuple-element.25), channel_id=1, source_target_pairs={{0,1},{1,2},{2,3},{3,0},{28,29},{29,30},{30,31},{31,28}} | collective-permute-start | bytes 368648 | tf_op jit(solution)/shard_map/ppermute | solution.py:342
  3.5 20.9 %collective-permute-start.3 = (f32[5,24,128]{2,1,0:T(8,128)S(1)}, f32[5,24,128]{2,1,0:T(8,128)S(1)}, u32[]{:S(2)}, u32[]{:S(2)}) collective-permute-start(f32[5,24,128]{2,1,0:T(8,128)S(1)} %get-tuple-element.26), channel_id=1, source_target_pairs={{0,2},{1,3},{2,0},{3,1},{28,30},{29,31},{30,28},{31,29}} | collective-permute-start | bytes 184328 | tf_op jit(solution)/shard_map/ppermute | solution.py:342
  4.2 5.8 %collective-permute-start = (f32[96,128]{1,0:T(8,128)S(1)}, f32[96,128]{1,0:T(8,128)S(1)}, u32[]{:S(2)}, u32[]{:S(2)}) collective-permute-start(f32[96,128]{1,0:T(8,128)S(1)} %get-tuple-element.22), channel_id=1, source_target_pairs={{0,1},{1,2},{2,3},{3,0},{4,5},{5,6},{6,7},{7,4},{8,9},{9,10},{10,1... | collective-permute-start | bytes 147464 | tf_op jit(solution)/shard_map/ppermute | solution.py:342
  6.4 3.6 %copy-start.5 = (f32[96,128]{1,0:T(8,128)S(1)}, f32[96,128]{1,0:T(8,128)}, u32[]{:S(2)}) copy-start(f32[96,128]{1,0:T(8,128)} %courant_north.3) | copy-start | bytes 147460
  6.4 3.6 %collective-permute-start.1 = (f32[96,128]{1,0:T(8,128)S(1)}, f32[96,128]{1,0:T(8,128)S(1)}, u32[]{:S(2)}, u32[]{:S(2)}) collective-permute-start(f32[96,128]{1,0:T(8,128)S(1)} %get-tuple-element.23), channel_id=1, source_target_pairs={{0,3},{1,0},{2,1},{3,2},{4,7},{5,4},{6,5},{7,6},{8,11},{9,8},{10,9... | collective-permute-start | bytes 147464 | tf_op jit(solution)/shard_map/ppermute | solution.py:342
  10.0 14.5 %copy-start.2 = (s32[96,128]{1,0:T(8,128)S(1)}, s32[96,128]{1,0:T(8,128)}, u32[]{:S(2)}) copy-start(s32[96,128]{1,0:T(8,128)} %offsets.5) | copy-start | bytes 147460
  10.0 14.5 %copy-start.4 = (f32[96,128]{1,0:T(8,128)S(1)}, f32[96,128]{1,0:T(8,128)}, u32[]{:S(2)}) copy-start(f32[96,128]{1,0:T(8,128)} %fraction.5) | copy-start | bytes 147460
  11.1 10.3 %collective-permute-start.4 = (f32[16,128]{1,0:T(8,128)S(1)}, f32[16,128]{1,0:T(8,128)S(1)}, u32[]{:S(2)}, u32[]{:S(2)}) collective-permute-start(f32[16,128]{1,0:T(8,128)S(1)} %get-tuple-element.27), channel_id=1, source_target_pairs={{0,4},{4,0},{1,5},{5,1},{2,6},{6,2},{3,7},{7,3},{8,12},{12,8},{9,1... | collective-permute-start | bytes 24584 | tf_op jit(solution)/shard_map/ppermute | solution.py:350
  19.5 5.0 %collective-permute-start.5 = (f32[16,128]{1,0:T(8,128)S(1)}, f32[16,128]{1,0:T(8,128)S(1)}, u32[]{:S(2)}, u32[]{:S(2)}) collective-permute-start(f32[16,128]{1,0:T(8,128)S(1)} %get-tuple-element.28), channel_id=1, source_target_pairs={{4,8},{8,4},{5,9},{9,5},{6,10},{10,6},{7,11},{11,7},{12,16},{16,12... | collective-permute-start | bytes 24584 | tf_op jit(solution)/shard_map/ppermute | solution.py:350

commit v2 on v0

v2 whole, which is shorter than its diff:
```python
import functools

import jax
import jax.numpy as jnp
from jax import lax
from jax.experimental import pallas as pl
from jax.experimental.pallas import tpu as pltpu
from jax.sharding import PartitionSpec as P

POLAR = 24
BAND = 24
POLE = POLAR + BAND
WEST = 12
SEG = 24
FACES = 11
OFF_LANE = 120
FRAC_LANE = 121
EDGE = 8

f32 = jnp.float32
bf16 = jnp.bfloat16
i32 = jnp.int32
VMEM = pltpu.VMEM


def lanes(shape):
    return lax.broadcasted_iota(i32, shape, 1)


def rolled(value, steps):
    steps = steps % value.shape[1]
    return pltpu.roll(value, steps, 1) if steps else value


def pick(table, index):
    return jnp.take_along_axis(table, index, axis=1, mode="promise_in_bounds")


def parabola(c, right, left, centre):
    jump = right - left
    curve = 6.0 * centre - 3.0 * (left + right)
    return c * (right - 0.5 * c * (jump - (1.0 - (2.0 / 3.0) * c) * curve))


def times(value, matrix):
    high = value.astype(bf16)
    low = (value - high.astype(f32)).astype(bf16)
    return jnp.dot(high, matrix, preferred_element_type=f32) + jnp.dot(
        low, matrix, preferred_element_type=f32
    )


def edge_weights(gap):
    def weight(gap):
        inner = (gap == 0) | (gap == 1)
        outer = (gap == -1) | (gap == 2)
        return jnp.where(inner, 7.0, jnp.where(outer, -1.0, 0.0))

    return weight(gap), weight(gap + 1)


def split(table, cells):
    return [table[:, i : i + cells] for i in range(0, table.shape[1], cells)]


def pack_kernel(
    tracers, offsets, fraction, courant, field, offset, part, north, packed, pole_one, pole_two, sems
):
    depth, row_count, cells = field.shape
    copies = [
        pltpu.make_async_copy(source, target, sems.at[i])
        for i, (source, target) in enumerate(
            ((tracers, field), (offsets, offset), (fraction, part), (courant, north))
        )
    ]
    for copy in copies:
        copy.start()
    for copy in copies[:3]:
        copy.wait()
    shape = (row_count, cells)
    lane = lanes(shape)
    message = jnp.where(
        lane == OFF_LANE,
        rolled(offset[...].astype(f32), OFF_LANE),
        jnp.where(lane == FRAC_LANE, rolled(part[...], FRAC_LANE), 0.0),
    )
    for t in range(depth):
        mine = (lane >= t * SEG) & (lane < (t + 1) * SEG)
        message = jnp.where(mine, rolled(field[t], t * SEG + WEST), message)
    packed[...] = message
    south = lax.axis_index("lat") == 0
    outer = pl.multiple_of(jnp.where(south, 0, row_count - POLE), 8)
    inner = pl.multiple_of(jnp.where(south, 0, row_count - POLAR), 8)
    pole_one[...] = field[:, pl.ds(outer, POLE), :]
    pole_two[...] = field[:, pl.ds(inner, POLAR), :]
    copies[3].wait()


def own_kernel(
    field, offset, part, flux, seam_index, seam_part, block_matrix, seam_matrix
):
    depth, row_count, cells = field.shape
    shape = (cells, cells)
    source = lax.broadcasted_iota(i32, shape, 0)
    target = lax.broadcasted_iota(i32, shape, 1)
    gap = source - target
    upto = jnp.where(gap <= 0, 1.0, 0.0)
    right, left = edge_weights(gap)
    block_matrix[cells : 2 * cells] = jnp.concatenate(
        [upto, right, left, jnp.ones(shape, f32)], axis=1
    ).astype(bf16)
    zeros = jnp.zeros(shape, f32)
    for first, away in ((0, -cells), (2 * cells, cells)):
        block_matrix[first : first + cells] = jnp.concatenate(
            [zeros, *edge_weights(gap + away), zeros], axis=1
        ).astype(bf16)
    together = source // SEG == target // SEG
    seam_matrix[...] = jnp.concatenate([jnp.where(together, upto, 0.0), right, left], axis=1).astype(bf16)

    shape = (row_count, cells)
    lane = lanes(shape)
    place = lane % SEG
    offsets = offset[...]
    courant = part[...]
    index = (lane - offsets - 1) & (cells - 1)
    own = field[...].reshape(depth * row_count, cells)
    tables = times(own, block_matrix[cells : 2 * cells, : 3 * cells])
    for t in range(depth):
        rows = slice(t * row_count, (t + 1) * row_count)
        sums, right, left = split(tables[rows], cells)
        value = field[t]
        flux[t] = (
            sums
            - value
            - pick(sums, index)
            + parabola(
                courant, pick(right, index) * (1 / 12), pick(left, index) * (1 / 12), pick(value, index)
            )
        )
    first = (place - WEST) & (cells - 1)
    final = jnp.full(shape, cells - 1, i32)
    seam_index[0] = (lane - pick(offsets, first) - 1) & (cells - 1)
    seam_index[1] = (lane - pick(offsets, final) - 1) & (cells - 1)
    seam_part[0] = pick(courant, first)
    seam_part[1] = pick(courant, final)


def rows_after(field, flux, packed, seam_index, seam_part, from_west, from_east, seam_matrix, parts):
    def take(ref, *lead):
        return jnp.concatenate([ref[(*lead, part)] for part in parts], axis=0)

    mine, west, east = take(packed), take(from_west), take(from_east)
    count, cells = mine.shape
    shape = mine.shape
    lane = lanes(shape)
    place = lane % SEG
    near = place < WEST
    rows = jnp.concatenate([jnp.where(near, west, mine), jnp.where(near, mine, east)], axis=0)
    next_face = place == WEST
    next_offset = pick(east, jnp.full(shape, OFF_LANE, i32)).astype(i32)
    next_part = pick(east, jnp.full(shape, FRAC_LANE, i32))
    next_index = (lane - next_offset - 1) & (cells - 1)
    index = jnp.concatenate(
        [take(seam_index, 0), jnp.where(next_face, next_index, take(seam_index, 1))], axis=0
    )
    courant = jnp.concatenate(
        [take(seam_part, 0), jnp.where(next_face, next_part, take(seam_part, 1))], axis=0
    )
    sums, right, left = split(times(rows, seam_matrix[...]), cells)
    faces = (
        sums
        - rows
        - pick(sums, index)
        + parabola(
            courant, pick(right, index) * (1 / 12), pick(left, index) * (1 / 12), pick(rows, index)
        )
    )
    east_faces = faces[count:]
    both = jnp.where(place == WEST - 1, east_faces, faces[:count])
    outside = (lane < FACES) | (lane == cells - 1)
    results = []
    for t in range(field.shape[0]):
        steps = -(t * SEG + WEST)
        face = jnp.where(outside, rolled(both, steps), take(flux, t))
        following = jnp.where(lane == cells - 1, rolled(east_faces, steps - 1), rolled(face, -1))
        results.append(take(field, t) - (following - face))
    return results


def edge_kernel(
    field, flux, packed, seam_index, seam_part, seam_matrix, north, from_east, from_west,
    message_a, message_b,
):
    depth, row_count, _ = field.shape
    parts = (pl.ds(0, EDGE), pl.ds(row_count - EDGE, EDGE))
    after = rows_after(
        field, flux, packed, seam_index, seam_part, from_west, from_east, seam_matrix, parts
    )
    even = lax.axis_index("lat") % 2 == 0
    for t in range(depth):
        bottom, top = after[t][:3], after[t][2 * EDGE - 3 :]
        message_a[3 * t : 3 * t + 3] = jnp.where(even, top, bottom)
        message_b[3 * t : 3 * t + 3] = jnp.where(even, bottom, top)
    message_a[3 * depth : 3 * depth + 1] = north[:1]
    message_b[3 * depth : 3 * depth + 1] = north[:1]


def polar_rows(tables, own, west, west_two, offset, courant, next_offset, next_courant):
    cells = own.shape[1]
    lane = lanes(own.shape)
    (sums, _, _, total), one, two = tables
    source = lane - offset - 1
    index = source & (cells - 1)
    close = source >= -cells

    def both(here, there):
        return jnp.where(close, pick(here, index), pick(there, index))

    face = (
        sums
        - own
        + one[3]
        - both(one[0], two[0] - two[3])
        + parabola(
            courant, both(one[1], two[1]) * (1 / 12), both(one[2], two[2]) * (1 / 12), both(west, west_two)
        )
    )
    index = (cells - 1 - next_offset) & (cells - 1)
    last = parabola(next_courant, one[1] * (1 / 12), one[2] * (1 / 12), west) - one[0]
    last = total + one[3] + pick(last, index)
    following = rolled(jnp.where(lane == 0, last, face), -1)
    return own - (following - face)


def band_rows(tables, own, west, offset, courant, next_offset, next_courant):
    cells = own.shape[1]
    lane = lanes(own.shape)
    here, one = tables
    source = lane - offset - 1
    index = source & (cells - 1)
    inside = source >= 0

    def both(inner, outer):
        return jnp.where(inside, pick(inner, index), pick(outer, index))

    face = (
        here[0]
        - own
        - both(here[0], one[0] - one[3])
        + parabola(
            courant, both(here[1], one[1]) * (1 / 12), both(here[2], one[2]) * (1 / 12), both(own, west)
        )
    )
    index = (cells - 1 - next_offset) & (cells - 1)
    last = parabola(next_courant, here[1] * (1 / 12), here[2] * (1 / 12), own) - here[0]
    last = here[3] + pick(last, index)
    following = rolled(jnp.where(lane == 0, last, face), -1)
    return own - (following - face)


def merid_flux(wide, t, courant, first, count):
    cell = [wide[t, first + k : first + k + count] for k in (-3, -2, -1, 0, 1)]
    left = (7.0 * (cell[1] + cell[2]) - (cell[0] + cell[3])) * (1 / 12)
    right = (7.0 * (cell[2] + cell[3]) - (cell[1] + cell[4])) * (1 / 12)
    return parabola(courant, right, left, cell[2])


def middle_kernel(
    lat_count, field, offset, part, north, flux, packed, seam_index, seam_part, seam_matrix, block_matrix,
    from_east, from_far, from_west, pole_one, pole_two, wide, out, result, faces, sems,
):
    depth, row_count, cells = field.shape
    lat = lax.axis_index("lat")
    south = lat == 0
    after = rows_after(
        field, flux, packed, seam_index, seam_part, from_west, from_east, seam_matrix, (pl.ds(0, row_count),)
    )
    for t in range(depth):
        wide[t] = after[t]

    @pl.when(south | (lat == lat_count - 1))
    def _():
        base = pl.multiple_of(jnp.where(south, 0, row_count - POLE), 8)
        polar = pl.multiple_of(jnp.where(south, 0, BAND), 8)
        band = pl.multiple_of(jnp.where(south, POLAR, 0), 8)
        polar_at = pl.ds(pl.multiple_of(base + polar, 8), POLAR)
        band_at = pl.ds(pl.multiple_of(base + band, 8), BAND)

        def stacked(ref, rows):
            return ref[:, rows, :].reshape(-1, cells)

        def unpacked(ref, rows, lane):
            value = ref[rows]
            return jnp.concatenate([rolled(value, lane - t * SEG) for t in range(depth)], axis=0)

        own_polar, own_band = stacked(field, polar_at), stacked(field, band_at)
        west_polar = stacked(pole_one, pl.ds(polar, POLAR))
        west_band = stacked(pole_one, pl.ds(band, BAND))
        west_two = pole_two[...].reshape(-1, cells)
        far = unpacked(from_far, polar_at, cells - WEST)
        east = unpacked(from_east, band_at, -WEST)
        rows = jnp.concatenate(
            [
                jnp.concatenate(three, axis=1)
                for three in (
                    (west_polar, own_polar, own_polar),
                    (west_two, west_polar, own_polar),
                    (far, west_two, west_polar),
                    (west_band, own_band, east),
                    (west_band, west_band, own_band),
                )
            ],
            axis=0,
        )
        tables = times(rows, block_matrix[...])

        def table(which, t):
            first = (which * depth + t) * POLAR
            return split(tables[first : first + POLAR], cells)

        for rows_at, is_polar in ((polar_at, True), (band_at, False)):
            shape = (POLAR, cells)
            beyond = from_east[rows_at]
            common = (
                offset[rows_at],
                part[rows_at],
                pick(beyond, jnp.full(shape, OFF_LANE, i32)).astype(i32),
                pick(beyond, jnp.full(shape, FRAC_LANE, i32)),
            )
            for t in range(depth):
                at = slice(t * POLAR, (t + 1) * POLAR)
                if is_polar:
                    wide[t, rows_at] = polar_rows(
                        (table(0, t), table(1, t), table(2, t)),
                        own_polar[at], west_polar[at], west_two[at], *common,
                    )
                else:
                    wide[t, rows_at] = band_rows(
                        (table(3, t), table(4, t)), own_band[at], west_band[at], *common
                    )

    count = row_count - 2 * EDGE
    copies = []
    for t in range(depth):
        faces[t, :count] = merid_flux(wide, t, north[EDGE : EDGE + count], EDGE, count)
        last = merid_flux(wide, t, north[EDGE + count : EDGE + count + 1], EDGE + count, 1)
        faces[t, count : count + 1] = last
        result[t] = wide[t, EDGE : EDGE + count] - (faces[t, 1 : 1 + count] - faces[t, :count])
        copies.append(
            pltpu.make_async_copy(result.at[t], out.at[t, pl.ds(EDGE, count)], sems.at[t])
        )
        copies[-1].start()
    for copy in copies:
        copy.wait()


def last_kernel(lat_count, wide, north, message_b, message_a, partial, out, low, high, result, sems):
    del partial
    depth, row_count, cells = wide.shape
    lat = lax.axis_index("lat")
    even = lat % 2 == 0
    south, top = lat == 0, lat == lat_count - 1
    end = 3 * depth
    north_courant = jnp.where(even, message_a[end : end + 1], message_b[end : end + 1])
    north_courant = jnp.where(top, 0.0, north_courant)
    first_row = lax.broadcasted_iota(i32, (EDGE, cells), 0)
    low_courant = jnp.where(south & (first_row == 0), 0.0, north[:EDGE])
    high_next = jnp.concatenate([north[row_count - EDGE + 1 :], north_courant], axis=0)
    for t in range(depth):
        rows = slice(3 * t, 3 * t + 3)
        from_a, from_b = message_a[rows], message_b[rows]
        low[t, EDGE - 3 : EDGE] = jnp.where(south, 0.0, jnp.where(even, from_b, from_a))
        low[t, EDGE : 3 * EDGE] = wide[t, : 2 * EDGE]
        high[t, : 2 * EDGE] = wide[t, row_count - 2 * EDGE :]
        high[t, 2 * EDGE : 2 * EDGE + 3] = jnp.where(top, 0.0, jnp.where(even, from_a, from_b))
    for t in range(depth):
        south_face = merid_flux(low, t, low_courant, EDGE, EDGE)
        north_face = merid_flux(low, t, north[1 : EDGE + 1], EDGE + 1, EDGE)
        result[0, t] = low[t, EDGE : 2 * EDGE] - (north_face - south_face)
        south_face = merid_flux(high, t, north[row_count - EDGE :], EDGE, EDGE)
        north_face = merid_flux(high, t, high_next, EDGE + 1, EDGE)
        result[1, t] = high[t, EDGE : 2 * EDGE] - (north_face - south_face)
    copies = [
        pltpu.make_async_copy(result.at[i], out.at[:, pl.ds(first, EDGE)], sems.at[i])
        for i, first in enumerate((0, row_count - EDGE))
    ]
    for copy in copies:
        copy.start()
    for copy in copies:
        copy.wait()


def cost(microseconds):
    return pl.CostEstimate(
        flops=int(microseconds * 1e8), bytes_accessed=int(microseconds * 3e6), transcendentals=0
    )


def in_vmem(*values):
    return [pltpu.with_memory_space_constraint(value, VMEM) for value in values]


def whole(count):
    return [pl.BlockSpec(memory_space=VMEM)] * count


def anywhere(count):
    return [pl.BlockSpec(memory_space=pl.ANY)] * count


def on_device(lat_count, lon_count, tracers, offsets, fraction, courant_north):
    tracer_count, level_count, row_count, cells = tracers.shape
    depth = tracer_count * level_count
    shape = (row_count, cells)
    stack = (depth, row_count, cells)
    dma = pltpu.SemaphoreType.DMA

    def along_lon(value, steps, everywhere=True):
        pairs = []
        for l in range(lat_count):
            from_pole = min(l, lat_count - 1 - l)
            for o in range(lon_count):
                if everywhere or from_pole == 0 or lat_count % 2 or lon_count % 2:
                    target = (l, (o + steps) % lon_count)
                else:
                    target = (l, o ^ 1) if from_pole == 1 else (l ^ 1, o)
                pairs.append((l * lon_count + o, target[0] * lon_count + target[1]))
        return lax.ppermute(value, ("lat", "lon"), pairs)

    def along_lat(value, first):
        pairs = []
        for l in range(first, lat_count if lat_count % 2 == 0 else lat_count - 1, 2):
            for o in range(lon_count):
                low, high = l * lon_count + o, (l + 1) % lat_count * lon_count + o
                pairs += [(low, high), (high, low)]
        return lax.ppermute(value, ("lat", "lon"), pairs)

    field, offset, part, north, packed, pole_one, pole_two = in_vmem(
        *pl.pallas_call(
            pack_kernel,
            out_shape=[
                VMEM(stack, f32),
                VMEM(shape, i32),
                VMEM(shape, f32),
                VMEM(shape, f32),
                VMEM(shape, f32),
                VMEM((depth, POLE, cells), f32),
                VMEM((depth, POLAR, cells), f32),
            ],
            in_specs=anywhere(4),
            out_specs=whole(7),
            scratch_shapes=[dma((4,))],
            cost_estimate=cost(1.0),
            name="pack",
        )(tracers.reshape(stack), offsets, fraction, courant_north)
    )
    from_west = along_lon(packed, 1)
    from_east = along_lon(packed, -1)
    from_far = from_east if lon_count == 4 else along_lon(packed, 3)

    flux, seam_index, seam_part, block_matrix, seam_matrix = in_vmem(
        *pl.pallas_call(
            own_kernel,
            out_shape=[
                VMEM(stack, f32),
                VMEM((2, *shape), i32),
                VMEM((2, *shape), f32),
                VMEM((3 * cells, 4 * cells), bf16),
                VMEM((cells, 3 * cells), bf16),
            ],
            in_specs=whole(3),
            out_specs=whole(5),
            cost_estimate=cost(2.0),
            name="own",
        )(field, offset, part)
    )
    pole_one = along_lon(pole_one, 1, False)
    pole_two = along_lon(pole_two, 2, False)
    from_west, from_east, from_far = in_vmem(from_west, from_east, from_far)

    message = (3 * depth + 1, cells)
    message_a, message_b = pl.pallas_call(
        edge_kernel,
        out_shape=[VMEM(message, f32), VMEM(message, f32)],
        in_specs=whole(9),
        out_specs=whole(2),
        cost_estimate=cost(8.0),
        name="edge",
    )(field, flux, packed, seam_index, seam_part, seam_matrix, north, from_east, from_west)
    message_a = along_lat(message_a, 0)
    message_b = along_lat(message_b, 1)

    wide, partial = pl.pallas_call(
        functools.partial(middle_kernel, lat_count),
        out_shape=[VMEM(stack, f32), jax.ShapeDtypeStruct(stack, f32)],
        in_specs=whole(15),
        out_specs=whole(1) + anywhere(1),
        scratch_shapes=[
            VMEM((depth, row_count - 2 * EDGE, cells), f32),
            VMEM((depth, row_count - EDGE, cells), f32),
            dma((depth,)),
        ],
        cost_estimate=cost(3.0),
        name="middle",
    )(
        field, offset, part, north, flux, packed, seam_index, seam_part, seam_matrix, block_matrix,
        from_east, from_far, from_west, *in_vmem(pole_one, pole_two),
    )

    out = pl.pallas_call(
        functools.partial(last_kernel, lat_count),
        out_shape=jax.ShapeDtypeStruct(stack, f32),
        in_specs=whole(4) + anywhere(1),
        out_specs=pl.BlockSpec(memory_space=pl.ANY),
        scratch_shapes=[
            VMEM((depth, 3 * EDGE, cells), f32),
            VMEM((depth, 3 * EDGE, cells), f32),
            VMEM((2, depth, EDGE, cells), f32),
            dma((2,)),
        ],
        input_output_aliases={4: 0},
        cost_estimate=cost(0.7),
        name="last",
    )(*in_vmem(wide), north, *in_vmem(message_b, message_a), partial)
    return out.reshape(tracers.shape)


def solution(mesh):
    placed = (P(None, None, "lat", "lon"), P("lat", "lon"), P("lat", "lon"), P("lat", "lon"))
    return jax.shard_map(
        functools.partial(on_device, mesh.shape["lat"], mesh.shape["lon"]),
        mesh=mesh,
        in_specs=placed,
        out_specs=P(None, None, "lat", "lon"),
        check_vma=False,
    )
```

time: 106 us -> 16.8 us (0.16); the launches traced: 104 us -> 16.6 us
  waiting for transfers between devices: 37.9 us -> 2.03 us
  matrix products: 18.6 us -> 0 us
  other arithmetic: 18.6 us -> 0 us
  local copies, waits for them, and re-layouts: 11.6 us -> 0 us
  starting transfers between devices: 16.7 us -> 8.52 us
  Pallas kernels: 0 us -> 6.01 us
    ppermute x9 -> x6, waiting for transfers between devices: 37.9 us -> 2.03 us  [the longest x4 2.03 us: along_lon(): return lax.ppermute(value, ('lat', 'lon'), pairs)]
    dot_general x27 -> x0, matrix products: 18.6 us -> none  [the longest x12 8.63 us: lookup_block(): jnp.einsum('tdrk,rkg->tdrg', table_block[1:], pick_depart, precision=lax....]
    dynamic_update_slice x12 -> x0, local copies, waits for them, and re-layouts: 8.55 us -> none  [lookup_block(): return lax.dynamic_update_slice_in_dim(picked, result_block, first_row, 2)]
    sub x13 -> x0, other arithmetic: 8.49 us -> none  [the longest x12 8.35 us: lookup_block(): pick_depart = (column == source_block[:, None, :] - 1).astype(jnp.float32)]
    ppermute x9 -> x6, starting transfers between devices: 16.7 us -> 8.52 us  [the longest x4 7.69 us: along_lon(): return lax.ppermute(value, ('lat', 'lon'), pairs)]
    pallas_call x0 -> x5, Pallas kernels: none -> 6.01 us  [the longest x1 2.88 us: on_device(): pl.pallas_call(functools.partial(middle_kernel, lat_count), out_shape=[VM...]
    add x3 -> x0, other arithmetic: 2.82 us -> none  [the longest x1 1.42 us: on_device(): source_index = face_index - offsets + 2 * cells_dev]
    concatenate x16 -> x0, other arithmetic: 1.86 us -> none  [the longest x2 1.24 us: with_halo(): block = jnp.concatenate([low, block, high], axis=dim)]
  transfers between devices with their start and end apart: 9 -> 6, of which waited for: 6 -> 2; matrix products, arithmetic and copies ran while one was open for 7% -> 0% of each run, Pallas kernels for 0% -> 25%
where the time goes in v2:
time: 16.8 us; the launch traced here: 16.6 us
  starting transfers between devices  8.52 us (51%)
  Pallas kernels  6.01 us (36%)
  waiting for transfers between devices  2.03 us (12%)
    ppermute x4, starting transfers between devices, along_lon(): return lax.ppermute(value, ('lat', 'lon'), pairs)  7.69 us
    pallas_call x1, Pallas kernels, on_device(): pl.pallas_call(functools.partial(middle_kernel, lat_count), out_shape=[VM...  2.88 us
    ppermute x4, waiting for transfers between devices, along_lon(): return lax.ppermute(value, ('lat', 'lon'), pairs)  2.03 us
    pallas_call x1, Pallas kernels, on_device(): pl.pallas_call(pack_kernel, out_shape=[VMEM(stack, f32), VMEM(shape, i32)...  1.15 us
    pallas_call x1, Pallas kernels, on_device(): pl.pallas_call(own_kernel, out_shape=[VMEM(stack, f32), VMEM((2, *shape),...  0.87 us
    ppermute x2, starting transfers between devices, along_lat(): return lax.ppermute(value, ('lat', 'lon'), pairs)  0.83 us
    pallas_call x1, Pallas kernels, on_device(): pl.pallas_call(functools.partial(last_kernel, lat_count), out_shape=jax.S...  0.72 us
    pallas_call x1, Pallas kernels, on_device(): pl.pallas_call(edge_kernel, out_shape=[VMEM(message, f32), VMEM(message,...  0.4 us
  transfers between devices with their start and end apart: 6, of which 2 were waited for; matrix products, arithmetic and copies ran while one was open for 0% of the time, Pallas kernels for 25%

profile of v2, /device:TPU:0, one launch (start us, length us, event | category | flops | bytes accessed | tf_op | source)
XLA Modules:
  0.0 16.6 jit_solution(10534383413454148126)
XLA Ops:
  0.0 1.1 %pack.1 = (f32[5,96,128]{2,1,0:T(8,128)S(1)}, s32[96,128]{1,0:T(8,128)S(1)}, f32[96,128]{1,0:T(8,128)S(1)}, f32[96,128]{1,0:T(8,128)S(1)}, f32[96,128]{1,0:T(8,1...) custom-call(f32[5,96,128]{2,1,0:T(8,128)} %bitcast.4, s32[96,128]{1,0:T(8,128)} %offsets.1, ...), custom_call_target="tpu_custom_call" | custom-call | flops 100000000 | bytes 3000000 | tf_op jit(solution)/shard_map/pack/pallas_call | solution.py:439
  1.2 3.1 %collective-permute-start.1 = (f32[96,128]{1,0:T(8,128)S(1)}, f32[96,128]{1,0:T(8,128)S(1)}, u32[]{:S(2)}, u32[]{:S(2)}) collective-permute-start(f32[96,128]{1,0:T(8,128)S(1)} %get-tuple-element.26.packed), channel_id=1, source_target_pairs={{0,1},{1,2},{2,3},{3,0},{4,5},{5,6},{6,7},{7,4},{8,9},{9,10},{10,1... | collective-permute-start | bytes 147464 | tf_op jit(solution)/shard_map/ppermute | solution.py:428
  4.2 2.1 %collective-permute-start = (f32[96,128]{1,0:T(8,128)S(1)}, f32[96,128]{1,0:T(8,128)S(1)}, u32[]{:S(2)}, u32[]{:S(2)}) collective-permute-start(f32[96,128]{1,0:T(8,128)S(1)} %get-tuple-element.26.packed), channel_id=1, source_target_pairs={{0,3},{1,0},{2,1},{3,2},{4,7},{5,4},{6,5},{7,6},{8,11},{9,8},{10,9... | collective-permute-start | bytes 147464 | tf_op jit(solution)/shard_map/ppermute | solution.py:428
  6.3 0.0 collective-permute-start.2
  6.3 2.5 %collective-permute-start.3 = (f32[5,24,128]{2,1,0:T(8,128)S(1)}, f32[5,24,128]{2,1,0:T(8,128)S(1)}, u32[]{:S(2)}, u32[]{:S(2)}) collective-permute-start(f32[5,24,128]{2,1,0:T(8,128)S(1)} %get-tuple-element.32), channel_id=1, source_target_pairs={{0,2},{1,3},{2,0},{3,1},{4,5},{5,4},{6,7},{7,6},{8,12},{9,13},{10,... | collective-permute-start | bytes 184328 | tf_op jit(solution)/shard_map/ppermute | solution.py:428
  8.8 0.9 %own.1 = (f32[5,96,128]{2,1,0:T(8,128)S(1)}, s32[2,96,128]{2,1,0:T(8,128)S(1)}, f32[2,96,128]{2,1,0:T(8,128)S(1)}, bf16[384,512]{1,0:T(8,128)(2,1)S(1)}, bf16[128,384]{1,0:T(8,128)(2,1)S(1)}) custom-call(f32[5,96,128]{2,1,0:T(8,128)S(1)} %get-tuple-element.21.field, s32[96,128]{1,0:T(8,128)S(1)} %get-tuple-element.22.offset, ...), custom_call_target="tpu_custom_call" | custom-call | flops 200000000 | bytes 6000000 | tf_op jit(solution)/shard_map/own/pallas_call | solution.py:462
  9.7 0.0 collective-permute-done.1.from_west
  9.7 0.0 collective-permute-done.from_east.from_far
  9.7 0.4 %edge.1 = (f32[16,128]{1,0:T(8,128)S(1)}, f32[16,128]{1,0:T(8,128)S(1)}) custom-call(f32[5,96,128]{2,1,0:T(8,128)S(1)} %get-tuple-element.21.field, f32[5,96,128]{2,1,0:T(8,128)S(1)} %get-tuple-element.25.flux, f32[96,128]{1,0:T(8,128)S(1)} %get-tuple-element.26.packed, s32[2,96,128]{2,1,0:T(8,128)S(1)} %get-tuple-element.27.seam_index, ...), custom_call_target="tpu_custom_call" | custom-call | flops 800000000 | bytes 24000000 | tf_op jit(solution)/shard_map/edge/pallas_call | solution.py:482
  10.1 0.8 %collective-permute-start.4 = (f32[16,128]{1,0:T(8,128)S(1)}, f32[16,128]{1,0:T(8,128)S(1)}, u32[]{:S(2)}, u32[]{:S(2)}) collective-permute-start(f32[16,128]{1,0:T(8,128)S(1)} %get-tuple-element.34), channel_id=1, source_target_pairs={{4,8},{8,4},{5,9},{9,5},{6,10},{10,6},{7,11},{11,7},{12,16},{16,12... | collective-permute-start | bytes 24584 | tf_op jit(solution)/shard_map/ppermute | solution.py:436
  11.0 0.0 collective-permute-start.5
  11.0 0.5 %collective-permute-done.3.pole_two = f32[5,24,128]{2,1,0:T(8,128)S(1)} collective-permute-done((f32[5,24,128]{2,1,0:T(8,128)S(1)}, f32[5,24,128]{2,1,0:T(8,128)S(1)}, u32[]{:S(2)}, u32[]{:S(2)}) %collective-permute-start.3) | collective-permute-done | bytes 61472 | tf_op jit(solution)/shard_map/ppermute | solution.py:428
  11.5 1.5 %collective-permute-done.2.pole_one = f32[5,48,128]{2,1,0:T(8,128)S(1)} collective-permute-done((f32[5,48,128]{2,1,0:T(8,128)S(1)}, f32[5,48,128]{2,1,0:T(8,128)S(1)}, u32[]{:S(2)}, u32[]{:S(2)}) %collective-permute-start.2) | collective-permute-done | bytes 122912 | tf_op jit(solution)/shard_map/ppermute | solution.py:428
  13.0 2.9 %middle.1 = (f32[5,96,128]{2,1,0:T(8,128)S(1)}, f32[5,96,128]{2,1,0:T(8,128)}) custom-call(f32[5,96,128]{2,1,0:T(8,128)S(1)} %get-tuple-element.21.field, s32[96,128]{1,0:T(8,128)S(1)} %get-tuple-element.22.offset, f32[96,128]{1,0:T(8,128)S(1)} %get-tuple-element.23.part, f32[96,128]{1,0:T(8,128)S(1)} %get-tuple-element.24.north, ...), custom_call_target="tpu_custom_call" | custom-call | flops 300000000 | bytes 9000000 | tf_op jit(solution)/shard_map/middle/pallas_call | solution.py:493
  15.9 0.0 collective-permute-done.4.message_b
  15.9 0.0 collective-permute-done.5.message_a
  15.9 0.7 %last.1 = f32[5,96,128]{2,1,0:T(8,128)} custom-call(f32[5,96,128]{2,1,0:T(8,128)S(1)} %get-tuple-element.33.wide, f32[96,128]{1,0:T(8,128)S(1)} %get-tuple-element.24.north, f32[16,128]{1,0:T(8,128)S(1)} %collective-permute-done.4.message_b, f32[16,128]{1,0:T(8,128)S(1)} %collective-permute-done.5.message_a, ...), custom_call_target="tpu_custom_call", output_to_operand_aliasing={{}: (4, {})} | custom-call | flops 70000000 | bytes 2100000 | tf_op jit(solution)/shard_map/last/pallas_call | solution.py:510
Async XLA Ops:
  1.2 8.6 %collective-permute-start.1 = (f32[96,128]{1,0:T(8,128)S(1)}, f32[96,128]{1,0:T(8,128)S(1)}, u32[]{:S(2)}, u32[]{:S(2)}) collective-permute-start(f32[96,128]{1,0:T(8,128)S(1)} %get-tuple-element.26.packed), channel_id=1, source_target_pairs={{0,1},{1,2},{2,3},{3,0},{4,5},{5,6},{6,7},{7,4},{8,9},{9,10},{10,1... | collective-permute-start | bytes 147464 | tf_op jit(solution)/shard_map/ppermute | solution.py:428
  4.2 5.5 %collective-permute-start = (f32[96,128]{1,0:T(8,128)S(1)}, f32[96,128]{1,0:T(8,128)S(1)}, u32[]{:S(2)}, u32[]{:S(2)}) collective-permute-start(f32[96,128]{1,0:T(8,128)S(1)} %get-tuple-element.26.packed), channel_id=1, source_target_pairs={{0,3},{1,0},{2,1},{3,2},{4,7},{5,4},{6,5},{7,6},{8,11},{9,8},{10,9... | collective-permute-start | bytes 147464 | tf_op jit(solution)/shard_map/ppermute | solution.py:428
  6.3 6.7 %collective-permute-start.2 = (f32[5,48,128]{2,1,0:T(8,128)S(1)}, f32[5,48,128]{2,1,0:T(8,128)S(1)}, u32[]{:S(2)}, u32[]{:S(2)}) collective-permute-start(f32[5,48,128]{2,1,0:T(8,128)S(1)} %get-tuple-element.31), channel_id=1, source_target_pairs={{0,1},{1,2},{2,3},{3,0},{4,5},{5,4},{6,7},{7,6},{8,12},{9,13},{10,... | collective-permute-start | bytes 368648 | tf_op jit(solution)/shard_map/ppermute | solution.py:428
  6.3 5.2 %collective-permute-start.3 = (f32[5,24,128]{2,1,0:T(8,128)S(1)}, f32[5,24,128]{2,1,0:T(8,128)S(1)}, u32[]{:S(2)}, u32[]{:S(2)}) collective-permute-start(f32[5,24,128]{2,1,0:T(8,128)S(1)} %get-tuple-element.32), channel_id=1, source_target_pairs={{0,2},{1,3},{2,0},{3,1},{4,5},{5,4},{6,7},{7,6},{8,12},{9,13},{10,... | collective-permute-start | bytes 184328 | tf_op jit(solution)/shard_map/ppermute | solution.py:428
  10.1 5.7 %collective-permute-start.4 = (f32[16,128]{1,0:T(8,128)S(1)}, f32[16,128]{1,0:T(8,128)S(1)}, u32[]{:S(2)}, u32[]{:S(2)}) collective-permute-start(f32[16,128]{1,0:T(8,128)S(1)} %get-tuple-element.34), channel_id=1, source_target_pairs={{4,8},{8,4},{5,9},{9,5},{6,10},{10,6},{7,11},{11,7},{12,16},{16,12... | collective-permute-start | bytes 24584 | tf_op jit(solution)/shard_map/ppermute | solution.py:436
  11.0 4.9 %collective-permute-start.5 = (f32[16,128]{1,0:T(8,128)S(1)}, f32[16,128]{1,0:T(8,128)S(1)}, u32[]{:S(2)}, u32[]{:S(2)}) collective-permute-start(f32[16,128]{1,0:T(8,128)S(1)} %get-tuple-element.35), channel_id=1, source_target_pairs={{0,4},{4,0},{1,5},{5,1},{2,6},{6,2},{3,7},{7,3},{8,12},{12,8},{9,1... | collective-permute-start | bytes 24584 | tf_op jit(solution)/shard_map/ppermute | solution.py:436

commit v3 on v2

--- a/solution.py
+++ b/solution.py
@@ -64,7 +64,8 @@
 
 
 def pack_kernel(
-    tracers, offsets, fraction, courant, field, offset, part, north, packed, pole_one, pole_two, sems
+    lat_count, tracers, offsets, fraction, courant,
+    field, offset, part, north, packed, to_east, pole_one, pole_two, sems,
 ):
     depth, row_count, cells = field.shape
     copies = [
@@ -88,16 +89,53 @@
         mine = (lane >= t * SEG) & (lane < (t + 1) * SEG)
         message = jnp.where(mine, rolled(field[t], t * SEG + WEST), message)
     packed[...] = message
-    south = lax.axis_index("lat") == 0
-    outer = pl.multiple_of(jnp.where(south, 0, row_count - POLE), 8)
-    inner = pl.multiple_of(jnp.where(south, 0, row_count - POLAR), 8)
-    pole_one[...] = field[:, pl.ds(outer, POLE), :]
-    pole_two[...] = field[:, pl.ds(inner, POLAR), :]
+    to_east[...] = message
+    lat = lax.axis_index("lat")
+    south = lat == 0
+
+    @pl.when(south | (lat == lat_count - 1))
+    def _():
+        base = pl.multiple_of(jnp.where(south, 0, row_count - POLE), 8)
+        band = pl.multiple_of(jnp.where(south, POLAR, row_count - POLE), 8)
+        polar = pl.multiple_of(jnp.where(south, 0, row_count - POLAR), 8)
+        rows = [field[t, pl.ds(band, BAND)] for t in range(depth)]
+        lane = lanes(rows[0].shape)
+        half = cells // 2
+        halves = []
+        for t in range(0, depth, 2):
+            other = rolled(rows[t + 1], half) if t + 1 < depth else jnp.zeros(lane.shape, f32)
+            halves.append(jnp.where(lane >= half, rows[t], other))
+        rest = halves.pop()
+        for t in range(depth):
+            mine = (lane >= 3 * t) & (lane < 3 * t + 3)
+            rest = jnp.where(mine, rolled(rows[t], 3 * t + 3 - half), rest)
+        for i, value in enumerate(halves):
+            to_east[pl.ds(pl.multiple_of(base + i * BAND, 8), BAND)] = value
+        pole_one[:BAND] = rest
+        for t in range(depth):
+            value = field[t, pl.ds(polar, POLAR)]
+            pole_one[BAND + t * POLAR : BAND + (t + 1) * POLAR] = value
+            pole_two[t * POLAR : (t + 1) * POLAR] = value
+
     copies[3].wait()
 
 
+def pieces(row_count):
+    return [(0, POLE), (POLE, row_count - 2 * POLE), (row_count - POLE, POLE)]
+
+
+def each_mid_piece(lat_count, row_count, body):
+    lat = lax.axis_index("lat")
+    conditions = (lat > 0, None, lat < lat_count - 1)
+    for (first, count), condition in zip(pieces(row_count), conditions):
+        if count and condition is None:
+            body(first, count)
+        elif count:
+            pl.when(condition)(functools.partial(body, first, count))
+
+
 def own_kernel(
-    field, offset, part, flux, seam_index, seam_part, block_matrix, seam_matrix
+    lat_count, field, offset, part, flux, seam_index, seam_part, block_matrix, seam_matrix
 ):
     depth, row_count, cells = field.shape
     shape = (cells, cells)
@@ -106,43 +144,42 @@
     gap = source - target
     upto = jnp.where(gap <= 0, 1.0, 0.0)
     right, left = edge_weights(gap)
-    block_matrix[cells : 2 * cells] = jnp.concatenate(
-        [upto, right, left, jnp.ones(shape, f32)], axis=1
-    ).astype(bf16)
+    block_matrix[:cells] = jnp.concatenate([upto, right, left, jnp.ones(shape, f32)], axis=1).astype(bf16)
     zeros = jnp.zeros(shape, f32)
-    for first, away in ((0, -cells), (2 * cells, cells)):
-        block_matrix[first : first + cells] = jnp.concatenate(
-            [zeros, *edge_weights(gap + away), zeros], axis=1
-        ).astype(bf16)
+    beyond = gap + jnp.where(source < cells // 2, cells, -cells)
+    block_matrix[cells:] = jnp.concatenate([zeros, *edge_weights(beyond), zeros], axis=1).astype(bf16)
     together = source // SEG == target // SEG
     seam_matrix[...] = jnp.concatenate([jnp.where(together, upto, 0.0), right, left], axis=1).astype(bf16)
 
-    shape = (row_count, cells)
-    lane = lanes(shape)
-    place = lane % SEG
-    offsets = offset[...]
-    courant = part[...]
-    index = (lane - offsets - 1) & (cells - 1)
-    own = field[...].reshape(depth * row_count, cells)
-    tables = times(own, block_matrix[cells : 2 * cells, : 3 * cells])
-    for t in range(depth):
-        rows = slice(t * row_count, (t + 1) * row_count)
-        sums, right, left = split(tables[rows], cells)
-        value = field[t]
-        flux[t] = (
-            sums
-            - value
-            - pick(sums, index)
-            + parabola(
-                courant, pick(right, index) * (1 / 12), pick(left, index) * (1 / 12), pick(value, index)
+    def step(first_row, count):
+        at = pl.ds(first_row, count)
+        shape = (count, cells)
+        lane = lanes(shape)
+        place = lane % SEG
+        offsets = offset[at]
+        courant = part[at]
+        index = (lane - offsets - 1) & (cells - 1)
+        own = field[:, at].reshape(depth * count, cells)
+        tables = times(own, block_matrix[:cells, : 3 * cells])
+        for t in range(depth):
+            sums, right, left = split(tables[t * count : (t + 1) * count], cells)
+            value = field[t, at]
+            flux[t, at] = (
+                sums
+                - value
+                - pick(sums, index)
+                + parabola(
+                    courant, pick(right, index) * (1 / 12), pick(left, index) * (1 / 12), pick(value, index)
+                )
             )
-        )
-    first = (place - WEST) & (cells - 1)
-    final = jnp.full(shape, cells - 1, i32)
-    seam_index[0] = (lane - pick(offsets, first) - 1) & (cells - 1)
-    seam_index[1] = (lane - pick(offsets, final) - 1) & (cells - 1)
-    seam_part[0] = pick(courant, first)
-    seam_part[1] = pick(courant, final)
+        first = (place - WEST) & (cells - 1)
+        final = jnp.full(shape, cells - 1, i32)
+        seam_index[0, at] = (lane - pick(offsets, first) - 1) & (cells - 1)
+        seam_index[1, at] = (lane - pick(offsets, final) - 1) & (cells - 1)
+        seam_part[0, at] = pick(courant, first)
+        seam_part[1, at] = pick(courant, final)
+
+    each_mid_piece(lat_count, row_count, step)
 
 
 def rows_after(field, flux, packed, seam_index, seam_part, from_west, from_east, seam_matrix, parts):
@@ -266,100 +303,150 @@
 
 
 def middle_kernel(
-    lat_count, field, offset, part, north, flux, packed, seam_index, seam_part, seam_matrix, block_matrix,
-    from_east, from_far, from_west, pole_one, pole_two, wide, out, result, faces, sems,
+    lat_count, field, north, flux, packed, seam_index, seam_part, seam_matrix, from_east, from_west,
+    wide, out, result, faces, sems,
 ):
     depth, row_count, cells = field.shape
+
+    def step(first, count):
+        after = rows_after(
+            field, flux, packed, seam_index, seam_part, from_west, from_east, seam_matrix,
+            (pl.ds(first, count),),
+        )
+        for t in range(depth):
+            wide[t, first : first + count] = after[t]
+
+    each_mid_piece(lat_count, row_count, step)
     lat = lax.axis_index("lat")
-    south = lat == 0
-    after = rows_after(
-        field, flux, packed, seam_index, seam_part, from_west, from_east, seam_matrix, (pl.ds(0, row_count),)
-    )
-    for t in range(depth):
-        wide[t] = after[t]
-
-    @pl.when(south | (lat == lat_count - 1))
+
+    @pl.when((lat > 0) & (lat < lat_count - 1))
     def _():
-        base = pl.multiple_of(jnp.where(south, 0, row_count - POLE), 8)
-        polar = pl.multiple_of(jnp.where(south, 0, BAND), 8)
-        band = pl.multiple_of(jnp.where(south, POLAR, 0), 8)
-        polar_at = pl.ds(pl.multiple_of(base + polar, 8), POLAR)
-        band_at = pl.ds(pl.multiple_of(base + band, 8), BAND)
-
-        def stacked(ref, rows):
-            return ref[:, rows, :].reshape(-1, cells)
-
-        def unpacked(ref, rows, lane):
-            value = ref[rows]
-            return jnp.concatenate([rolled(value, lane - t * SEG) for t in range(depth)], axis=0)
-
-        own_polar, own_band = stacked(field, polar_at), stacked(field, band_at)
-        west_polar = stacked(pole_one, pl.ds(polar, POLAR))
-        west_band = stacked(pole_one, pl.ds(band, BAND))
-        west_two = pole_two[...].reshape(-1, cells)
-        far = unpacked(from_far, polar_at, cells - WEST)
-        east = unpacked(from_east, band_at, -WEST)
-        rows = jnp.concatenate(
-            [
-                jnp.concatenate(three, axis=1)
-                for three in (
-                    (west_polar, own_polar, own_polar),
-                    (west_two, west_polar, own_polar),
-                    (far, west_two, west_polar),
-                    (west_band, own_band, east),
-                    (west_band, west_band, own_band),
-                )
-            ],
-            axis=0,
-        )
-        tables = times(rows, block_matrix[...])
-
-        def table(which, t):
-            first = (which * depth + t) * POLAR
-            return split(tables[first : first + POLAR], cells)
-
-        for rows_at, is_polar in ((polar_at, True), (band_at, False)):
-            shape = (POLAR, cells)
-            beyond = from_east[rows_at]
-            common = (
-                offset[rows_at],
-                part[rows_at],
-                pick(beyond, jnp.full(shape, OFF_LANE, i32)).astype(i32),
-                pick(beyond, jnp.full(shape, FRAC_LANE, i32)),
-            )
-            for t in range(depth):
-                at = slice(t * POLAR, (t + 1) * POLAR)
-                if is_polar:
-                    wide[t, rows_at] = polar_rows(
-                        (table(0, t), table(1, t), table(2, t)),
-                        own_polar[at], west_polar[at], west_two[at], *common,
-                    )
-                else:
-                    wide[t, rows_at] = band_rows(
-                        (table(3, t), table(4, t)), own_band[at], west_band[at], *common
-                    )
-
-    count = row_count - 2 * EDGE
-    copies = []
+        copies = [
+            pltpu.make_async_copy(result.at[t], out.at[t, pl.ds(EDGE, result.shape[1])], sems.at[t])
+            for t in range(depth)
+        ]
+        inner_rows(wide, north, faces, result, copies)
+        for copy in copies:
+            copy.wait()
+
+
+def inner_rows(wide, north, faces, result, copies=()):
+    depth, count, _ = result.shape
     for t in range(depth):
         faces[t, :count] = merid_flux(wide, t, north[EDGE : EDGE + count], EDGE, count)
         last = merid_flux(wide, t, north[EDGE + count : EDGE + count + 1], EDGE + count, 1)
         faces[t, count : count + 1] = last
         result[t] = wide[t, EDGE : EDGE + count] - (faces[t, 1 : 1 + count] - faces[t, :count])
-        copies.append(
-            pltpu.make_async_copy(result.at[t], out.at[t, pl.ds(EDGE, count)], sems.at[t])
+        if copies:
+            copies[t].start()
+
+
+def poles_kernel(
+    lat_count, field, offset, part, north, block_matrix, from_east, from_far, from_west, pole_one, pole_two,
+    given, wide, inner, faces,
+):
+    del given
+    depth, row_count, cells = field.shape
+    lat = lax.axis_index("lat")
+    south = lat == 0
+
+    @pl.when(south | (lat == lat_count - 1))
+    def _():
+        pole_rows_step(
+            south, field, offset, part, from_east, from_far, from_west, pole_one, pole_two, block_matrix, wide
         )
-        copies[-1].start()
-    for copy in copies:
-        copy.wait()
-
-
-def last_kernel(lat_count, wide, north, message_b, message_a, partial, out, low, high, result, sems):
+        inner_rows(wide, north, faces, inner)
+
+
+def pole_rows_step(
+    south, field, offset, part, from_east, from_far, from_west, pole_one, pole_two, block_matrix, wide
+):
+    depth, row_count, cells = field.shape
+    base = pl.multiple_of(jnp.where(south, 0, row_count - POLE), 8)
+    polar_at = pl.ds(pl.multiple_of(jnp.where(south, 0, row_count - POLAR), 8), POLAR)
+    band_at = pl.ds(pl.multiple_of(jnp.where(south, POLAR, row_count - POLE), 8), BAND)
+
+    def stacked(ref, rows):
+        return ref[:, rows, :].reshape(-1, cells)
+
+    def unpacked(ref, rows, lane):
+        value = ref[rows]
+        return jnp.concatenate([rolled(value, lane - t * SEG) for t in range(depth)], axis=0)
+
+    own_polar, own_band = stacked(field, polar_at), stacked(field, band_at)
+    west_polar = pole_one[BAND:]
+    west_two = pole_two[...]
+    far = unpacked(from_far, polar_at, cells - WEST)
+    east = unpacked(from_east, band_at, -WEST)
+    rest = pole_one[:BAND]
+    lane = lanes(rest.shape)
+    half = cells // 2
+    west_band = []
+    for t in range(depth):
+        value = rest
+        if t // 2 < (depth - 1) // 2:
+            value = from_west[pl.ds(pl.multiple_of(base + t // 2 * BAND, 8), BAND)]
+        value = rolled(value, half) if t % 2 else value
+        inner = jnp.where(lane >= half - 3, rolled(rest, half - 3 - 3 * t), 0.0)
+        west_band.append(jnp.where(lane >= half, value, inner))
+    west_band = jnp.concatenate(west_band, axis=0)
+
+    def with_sides(west, own, east):
+        beside = jnp.where(lanes(own.shape) < half, east, west)
+        return jnp.concatenate([own, beside], axis=1)
+
+    rows = jnp.concatenate(
+        [
+            with_sides(own_polar, own_polar, own_polar),
+            with_sides(west_two, west_polar, own_polar),
+            with_sides(far, west_two, west_polar),
+            with_sides(west_band, own_band, east),
+            with_sides(west_band, west_band, own_band),
+        ],
+        axis=0,
+    )
+    tables = times(rows, block_matrix[...])
+
+    def table(which, t):
+        first = (which * depth + t) * POLAR
+        return split(tables[first : first + POLAR], cells)
+
+    for rows_at, is_polar in ((polar_at, True), (band_at, False)):
+        shape = (POLAR, cells)
+        beyond = from_east[rows_at]
+        common = (
+            offset[rows_at],
+            part[rows_at],
+            pick(beyond, jnp.full(shape, OFF_LANE, i32)).astype(i32),
+            pick(beyond, jnp.full(shape, FRAC_LANE, i32)),
+        )
+        for t in range(depth):
+            at = slice(t * POLAR, (t + 1) * POLAR)
+            if is_polar:
+                wide[t, rows_at] = polar_rows(
+                    (table(0, t), table(1, t), table(2, t)), own_polar[at], west_polar[at], west_two[at], *common
+                )
+            else:
+                wide[t, rows_at] = band_rows(
+                    (table(3, t), table(4, t)), own_band[at], west_band[at], *common
+                )
+
+
+def last_kernel(
+    lat_count, wide, inner, north, message_b, message_a, partial, out, low, high, result, sems
+):
     del partial
     depth, row_count, cells = wide.shape
+    count = row_count - 2 * EDGE
     lat = lax.axis_index("lat")
     even = lat % 2 == 0
     south, top = lat == 0, lat == lat_count - 1
+    inner_copy = pltpu.make_async_copy(inner, out.at[:, pl.ds(EDGE, count)], sems.at[2])
+
+    @pl.when(south | top)
+    def _():
+        inner_copy.start()
+
     end = 3 * depth
     north_courant = jnp.where(even, message_a[end : end + 1], message_b[end : end + 1])
     north_courant = jnp.where(top, 0.0, north_courant)
@@ -389,6 +476,10 @@
     for copy in copies:
         copy.wait()
 
+    @pl.when(south | top)
+    def _():
+        inner_copy.wait()
+
 
 def cost(microseconds):
     return pl.CostEstimate(
@@ -435,37 +526,40 @@
                 pairs += [(low, high), (high, low)]
         return lax.ppermute(value, ("lat", "lon"), pairs)
 
-    field, offset, part, north, packed, pole_one, pole_two = in_vmem(
+    field, offset, part, north, packed, to_east, pole_one, pole_two = in_vmem(
         *pl.pallas_call(
-            pack_kernel,
+            functools.partial(pack_kernel, lat_count),
             out_shape=[
                 VMEM(stack, f32),
                 VMEM(shape, i32),
                 VMEM(shape, f32),
                 VMEM(shape, f32),
                 VMEM(shape, f32),
-                VMEM((depth, POLE, cells), f32),
-                VMEM((depth, POLAR, cells), f32),
+                VMEM(shape, f32),
+                VMEM((BAND + depth * POLAR, cells), f32),
+                VMEM((depth * POLAR, cells), f32),
             ],
             in_specs=anywhere(4),
-            out_specs=whole(7),
+            out_specs=whole(8),
             scratch_shapes=[dma((4,))],
             cost_estimate=cost(1.0),
             name="pack",
         )(tracers.reshape(stack), offsets, fraction, courant_north)
     )
-    from_west = along_lon(packed, 1)
+    from_west = along_lon(to_east, 1)
     from_east = along_lon(packed, -1)
     from_far = from_east if lon_count == 4 else along_lon(packed, 3)
+    pole_one = along_lon(pole_one, 1, False)
+    pole_two = along_lon(pole_two, 2, False)
 
     flux, seam_index, seam_part, block_matrix, seam_matrix = in_vmem(
         *pl.pallas_call(
-            own_kernel,
+            functools.partial(own_kernel, lat_count),
             out_shape=[
                 VMEM(stack, f32),
                 VMEM((2, *shape), i32),
                 VMEM((2, *shape), f32),
-                VMEM((3 * cells, 4 * cells), bf16),
+                VMEM((2 * cells, 4 * cells), bf16),
                 VMEM((cells, 3 * cells), bf16),
             ],
             in_specs=whole(3),
@@ -474,9 +568,9 @@
             name="own",
         )(field, offset, part)
     )
-    pole_one = along_lon(pole_one, 1, False)
-    pole_two = along_lon(pole_two, 2, False)
-    from_west, from_east, from_far = in_vmem(from_west, from_east, from_far)
+    from_west, from_east, from_far, pole_one, pole_two = in_vmem(
+        from_west, from_east, from_far, pole_one, pole_two
+    )
 
     message = (3 * depth + 1, cells)
     message_a, message_b = pl.pallas_call(
@@ -484,7 +578,7 @@
         out_shape=[VMEM(message, f32), VMEM(message, f32)],
         in_specs=whole(9),
         out_specs=whole(2),
-        cost_estimate=cost(8.0),
+        cost_estimate=cost(2.0),
         name="edge",
     )(field, flux, packed, seam_index, seam_part, seam_matrix, north, from_east, from_west)
     message_a = along_lat(message_a, 0)
@@ -493,7 +587,7 @@
     wide, partial = pl.pallas_call(
         functools.partial(middle_kernel, lat_count),
         out_shape=[VMEM(stack, f32), jax.ShapeDtypeStruct(stack, f32)],
-        in_specs=whole(15),
+        in_specs=whole(9),
         out_specs=whole(1) + anywhere(1),
         scratch_shapes=[
             VMEM((depth, row_count - 2 * EDGE, cells), f32),
@@ -502,26 +596,39 @@
         ],
         cost_estimate=cost(3.0),
         name="middle",
+    )(field, north, flux, packed, seam_index, seam_part, seam_matrix, from_east, from_west)
+
+    inner = (depth, row_count - 2 * EDGE, cells)
+    faces = VMEM((depth, row_count - EDGE, cells), f32)
+    wide, inner = pl.pallas_call(
+        functools.partial(poles_kernel, lat_count),
+        out_shape=[VMEM(stack, f32), VMEM(inner, f32)],
+        in_specs=whole(11),
+        out_specs=whole(2),
+        scratch_shapes=[faces],
+        input_output_aliases={10: 0},
+        cost_estimate=cost(3.0),
+        name="poles",
     )(
-        field, offset, part, north, flux, packed, seam_index, seam_part, seam_matrix, block_matrix,
-        from_east, from_far, from_west, *in_vmem(pole_one, pole_two),
+        field, offset, part, north, block_matrix, from_east, from_far, from_west, pole_one, pole_two,
+        *in_vmem(wide),
     )
 
     out = pl.pallas_call(
         functools.partial(last_kernel, lat_count),
         out_shape=jax.ShapeDtypeStruct(stack, f32),
-        in_specs=whole(4) + anywhere(1),
+        in_specs=whole(5) + anywhere(1),
         out_specs=pl.BlockSpec(memory_space=pl.ANY),
         scratch_shapes=[
             VMEM((depth, 3 * EDGE, cells), f32),
             VMEM((depth, 3 * EDGE, cells), f32),
             VMEM((2, depth, EDGE, cells), f32),
-            dma((2,)),
+            dma((3,)),
         ],
-        input_output_aliases={4: 0},
+        input_output_aliases={5: 0},
         cost_estimate=cost(0.7),
         name="last",
-    )(*in_vmem(wide), north, *in_vmem(message_b, message_a), partial)
+    )(*in_vmem(wide, inner), north, *in_vmem(message_b, message_a), partial)
     return out.reshape(tracers.shape)
 
 

time: 16.8 us -> 14.8 us (0.88)
  Pallas kernels: 6.01 us -> 4.59 us
  waiting for transfers between devices: 2.03 us -> 1.34 us
  starting transfers between devices: 8.52 us -> 8.7 us
    pallas_call x1, Pallas kernels: 2.88 us -> 0.55 us  [on_device(): pl.pallas_call(functools.partial(middle_kernel, lat_count), out_shape=[VM...]
    ppermute x4, waiting for transfers between devices: 2.03 us -> 1.09 us  [along_lon(): return lax.ppermute(value, ('lat', 'lon'), pairs)]
    pallas_call x2 -> x3, Pallas kernels: 2.02 us -> 2.92 us  [the longest x1 1.23 us: on_device(): pl.pallas_call(functools.partial(pack_kernel, lat_count), out_shape=[VMEM...]
    ppermute x2, waiting for transfers between devices: 0.01 us -> 0.25 us  [along_lat(): return lax.ppermute(value, ('lat', 'lon'), pairs)]
    ppermute x2, starting transfers between devices: 0.83 us -> 1 us  [along_lat(): return lax.ppermute(value, ('lat', 'lon'), pairs)]
  transfers between devices with their start and end apart: 6 -> 6, of which waited for: 2 -> 3; matrix products, arithmetic and copies ran while one was open for 0% -> 0% of each run, Pallas kernels for 25% -> 18%
where the time goes in v3:
time: 14.8 us; the launch traced here: 14.7 us
  starting transfers between devices  8.7 us (59%)
  Pallas kernels  4.59 us (31%)
  waiting for transfers between devices  1.34 us (9%)
    ppermute x4, starting transfers between devices, along_lon(): return lax.ppermute(value, ('lat', 'lon'), pairs)  7.69 us
    pallas_call x1, Pallas kernels, on_device(): pl.pallas_call(functools.partial(pack_kernel, lat_count), out_shape=[VMEM...  1.23 us
    pallas_call x1, Pallas kernels, on_device(): pl.pallas_call(functools.partial(poles_kernel, lat_count), out_shape=[VME...  1.15 us
    ppermute x4, waiting for transfers between devices, along_lon(): return lax.ppermute(value, ('lat', 'lon'), pairs)  1.09 us
    ppermute x2, starting transfers between devices, along_lat(): return lax.ppermute(value, ('lat', 'lon'), pairs)  1 us
    pallas_call x1, Pallas kernels, on_device(): pl.pallas_call(functools.partial(last_kernel, lat_count), out_shape=jax.S...  0.72 us
    pallas_call x1, Pallas kernels, on_device(): pl.pallas_call(functools.partial(own_kernel, lat_count), out_shape=[VMEM(...  0.55 us
    pallas_call x1, Pallas kernels, on_device(): pl.pallas_call(functools.partial(middle_kernel, lat_count), out_shape=[VM...  0.55 us
  transfers between devices with their start and end apart: 6, of which 3 were waited for; matrix products, arithmetic and copies ran while one was open for 0% of the time, Pallas kernels for 18%

profile of v3, /device:TPU:0, one launch (start us, length us, event | category | flops | bytes accessed | tf_op | source)
XLA Modules:
  0.0 14.7 jit_solution(13045133183802875597)
XLA Ops:
  0.0 1.2 %pack.1 = (f32[5,96,128]{2,1,0:T(8,128)S(1)}, s32[96,128]{1,0:T(8,128)S(1)}, f32[96,128]{1,0:T(8,128)S(1)}, f32[96,128]{1,0:T(8,128)S(1)}, f32[96,128]{1,0:T(8,1...) custom-call(f32[5,96,128]{2,1,0:T(8,128)} %bitcast.4, s32[96,128]{1,0:T(8,128)} %offsets.1, ...), custom_call_target="tpu_custom_call" | custom-call | flops 100000000 | bytes 3000000 | tf_op jit(solution)/shard_map/pack/pallas_call | solution.py:530
  1.2 3.1 %collective-permute-start.1 = (f32[96,128]{1,0:T(8,128)S(1)}, f32[96,128]{1,0:T(8,128)S(1)}, u32[]{:S(2)}, u32[]{:S(2)}) collective-permute-start(f32[96,128]{1,0:T(8,128)S(1)} %get-tuple-element.30), channel_id=1, source_target_pairs={{0,1},{1,2},{2,3},{3,0},{4,5},{5,6},{6,7},{7,4},{8,9},{9,10},{10,1... | collective-permute-start | bytes 147464 | tf_op jit(solution)/shard_map/ppermute | solution.py:519
  4.3 2.1 %collective-permute-start = (f32[96,128]{1,0:T(8,128)S(1)}, f32[96,128]{1,0:T(8,128)S(1)}, u32[]{:S(2)}, u32[]{:S(2)}) collective-permute-start(f32[96,128]{1,0:T(8,128)S(1)} %get-tuple-element.29.packed), channel_id=1, source_target_pairs={{0,3},{1,0},{2,1},{3,2},{4,7},{5,4},{6,5},{7,6},{8,11},{9,8},{10,9... | collective-permute-start | bytes 147464 | tf_op jit(solution)/shard_map/ppermute | solution.py:519
  6.4 0.0 collective-permute-start.2
  6.4 2.5 %collective-permute-start.3 = (f32[120,128]{1,0:T(8,128)S(1)}, f32[120,128]{1,0:T(8,128)S(1)}, u32[]{:S(2)}, u32[]{:S(2)}) collective-permute-start(f32[120,128]{1,0:T(8,128)S(1)} %get-tuple-element.32), channel_id=1, source_target_pairs={{0,2},{1,3},{2,0},{3,1},{4,5},{5,4},{6,7},{7,6},{8,12},{9,13},{10,... | collective-permute-start | bytes 184328 | tf_op jit(solution)/shard_map/ppermute | solution.py:519
  8.9 0.5 %own.1 = (f32[5,96,128]{2,1,0:T(8,128)S(1)}, s32[2,96,128]{2,1,0:T(8,128)S(1)}, f32[2,96,128]{2,1,0:T(8,128)S(1)}, bf16[256,512]{1,0:T(8,128)(2,1)S(1)}, bf16[128,384]{1,0:T(8,128)(2,1)S(1)}) custom-call(f32[5,96,128]{2,1,0:T(8,128)S(1)} %get-tuple-element.24.field, s32[96,128]{1,0:T(8,128)S(1)} %get-tuple-element.25.offset, ...), custom_call_target="tpu_custom_call" | custom-call | flops 200000000 | bytes 6000000 | tf_op jit(solution)/shard_map/own/pallas_call | solution.py:556
  9.5 0.0 collective-permute-done.1.from_west
  9.5 0.0 collective-permute-done.from_east.from_far
  9.5 0.4 %edge.1 = (f32[16,128]{1,0:T(8,128)S(1)}, f32[16,128]{1,0:T(8,128)S(1)}) custom-call(f32[5,96,128]{2,1,0:T(8,128)S(1)} %get-tuple-element.24.field, f32[5,96,128]{2,1,0:T(8,128)S(1)} %get-tuple-element.33.flux, f32[96,128]{1,0:T(8,128)S(1)} %get-tuple-element.29.packed, s32[2,96,128]{2,1,0:T(8,128)S(1)} %get-tuple-element.34.seam_index, ...), custom_call_target="tpu_custom_call" | custom-call | flops 200000000 | bytes 6000000 | tf_op jit(solution)/shard_map/edge/pallas_call | solution.py:576
  9.9 0.8 %collective-permute-start.4 = (f32[16,128]{1,0:T(8,128)S(1)}, f32[16,128]{1,0:T(8,128)S(1)}, u32[]{:S(2)}, u32[]{:S(2)}) collective-permute-start(f32[16,128]{1,0:T(8,128)S(1)} %get-tuple-element.40), channel_id=1, source_target_pairs={{4,8},{8,4},{5,9},{9,5},{6,10},{10,6},{7,11},{11,7},{12,16},{16,12... | collective-permute-start | bytes 24584 | tf_op jit(solution)/shard_map/ppermute | solution.py:527
  10.7 0.2 %collective-permute-start.5 = (f32[16,128]{1,0:T(8,128)S(1)}, f32[16,128]{1,0:T(8,128)S(1)}, u32[]{:S(2)}, u32[]{:S(2)}) collective-permute-start(f32[16,128]{1,0:T(8,128)S(1)} %get-tuple-element.41), channel_id=1, source_target_pairs={{0,4},{4,0},{1,5},{5,1},{2,6},{6,2},{3,7},{7,3},{8,12},{12,8},{9,1... | collective-permute-start | bytes 24584 | tf_op jit(solution)/shard_map/ppermute | solution.py:527
  10.9 0.5 %middle.1 = (f32[5,96,128]{2,1,0:T(8,128)S(1)}, f32[5,96,128]{2,1,0:T(8,128)}) custom-call(f32[5,96,128]{2,1,0:T(8,128)S(1)} %get-tuple-element.24.field, f32[96,128]{1,0:T(8,128)S(1)} %get-tuple-element.27.north, f32[5,96,128]{2,1,0:T(8,128)S(1)} %get-tuple-element.33.flux, f32[96,128]{1,0:T(8,128)S(1)} %get-tuple-element.29.packed, ...), custom_call_target="tpu_custom_call" | custom-call | flops 300000000 | bytes 9000000 | tf_op jit(solution)/shard_map/middle/pallas_call | solution.py:587
  11.5 0.1 collective-permute-done.3.pole_two
  11.5 1.0 %collective-permute-done.2.pole_one = f32[144,128]{1,0:T(8,128)S(1)} collective-permute-done((f32[144,128]{1,0:T(8,128)S(1)}, f32[144,128]{1,0:T(8,128)S(1)}, u32[]{:S(2)}, u32[]{:S(2)}) %collective-permute-start.2) | collective-permute-done | bytes 73760 | tf_op jit(solution)/shard_map/ppermute | solution.py:519
  12.6 1.1 %poles.1 = (f32[5,96,128]{2,1,0:T(8,128)S(1)}, f32[5,80,128]{2,1,0:T(8,128)S(1)}) custom-call(f32[5,96,128]{2,1,0:T(8,128)S(1)} %get-tuple-element.24.field, s32[96,128]{1,0:T(8,128)S(1)} %get-tuple-element.25.offset, f32[96,128]{1,0:T(8,128)S(1)} %get-tuple-element.26.part, ...), custom_call_target="tpu_custom_call", output_to_operand_aliasing={{0}: (10, {})} | custom-call | flops 300000000 | bytes 9000000 | tf_op jit(solution)/shard_map/poles/pallas_call | solution.py:603
  13.7 0.2 %collective-permute-done.4.message_b = f32[16,128]{1,0:T(8,128)S(1)} collective-permute-done((f32[16,128]{1,0:T(8,128)S(1)}, f32[16,128]{1,0:T(8,128)S(1)}, u32[]{:S(2)}, u32[]{:S(2)}) %collective-permute-start.4) | collective-permute-done | bytes 8224 | tf_op jit(solution)/shard_map/ppermute | solution.py:527
  14.0 0.0 collective-permute-done.5.message_a
  14.0 0.7 %last.1 = f32[5,96,128]{2,1,0:T(8,128)} custom-call(f32[5,96,128]{2,1,0:T(8,128)S(1)} %get-tuple-element.38.wide, f32[5,80,128]{2,1,0:T(8,128)S(1)} %get-tuple-element.39.inner, f32[96,128]{1,0:T(8,128)S(1)} %get-tuple-element.27.north, f32[16,128]{1,0:T(8,128)S(1)} %collective-permute-done.4.message_b, ...), custom_call_target="tpu_custom_call", output_to_operand_aliasing={{}: (5, {})} | custom-call | flops 70000000 | bytes 2100000 | tf_op jit(solution)/shard_map/last/pallas_call | solution.py:617
Async XLA Ops:
  1.2 8.2 %collective-permute-start.1 = (f32[96,128]{1,0:T(8,128)S(1)}, f32[96,128]{1,0:T(8,128)S(1)}, u32[]{:S(2)}, u32[]{:S(2)}) collective-permute-start(f32[96,128]{1,0:T(8,128)S(1)} %get-tuple-element.30), channel_id=1, source_target_pairs={{0,1},{1,2},{2,3},{3,0},{4,5},{5,6},{6,7},{7,4},{8,9},{9,10},{10,1... | collective-permute-start | bytes 147464 | tf_op jit(solution)/shard_map/ppermute | solution.py:519
  4.3 5.2 %collective-permute-start = (f32[96,128]{1,0:T(8,128)S(1)}, f32[96,128]{1,0:T(8,128)S(1)}, u32[]{:S(2)}, u32[]{:S(2)}) collective-permute-start(f32[96,128]{1,0:T(8,128)S(1)} %get-tuple-element.29.packed), channel_id=1, source_target_pairs={{0,3},{1,0},{2,1},{3,2},{4,7},{5,4},{6,5},{7,6},{8,11},{9,8},{10,9... | collective-permute-start | bytes 147464 | tf_op jit(solution)/shard_map/ppermute | solution.py:519
  6.4 6.2 %collective-permute-start.2 = (f32[144,128]{1,0:T(8,128)S(1)}, f32[144,128]{1,0:T(8,128)S(1)}, u32[]{:S(2)}, u32[]{:S(2)}) collective-permute-start(f32[144,128]{1,0:T(8,128)S(1)} %get-tuple-element.31), channel_id=1, source_target_pairs={{0,1},{1,2},{2,3},{3,0},{4,5},{5,4},{6,7},{7,6},{8,12},{9,13},{10,... | collective-permute-start | bytes 221192 | tf_op jit(solution)/shard_map/ppermute | solution.py:519
  6.4 5.1 %collective-permute-start.3 = (f32[120,128]{1,0:T(8,128)S(1)}, f32[120,128]{1,0:T(8,128)S(1)}, u32[]{:S(2)}, u32[]{:S(2)}) collective-permute-start(f32[120,128]{1,0:T(8,128)S(1)} %get-tuple-element.32), channel_id=1, source_target_pairs={{0,2},{1,3},{2,0},{3,1},{4,5},{5,4},{6,7},{7,6},{8,12},{9,13},{10,... | collective-permute-start | bytes 184328 | tf_op jit(solution)/shard_map/ppermute | solution.py:519
  9.9 4.0 %collective-permute-start.4 = (f32[16,128]{1,0:T(8,128)S(1)}, f32[16,128]{1,0:T(8,128)S(1)}, u32[]{:S(2)}, u32[]{:S(2)}) collective-permute-start(f32[16,128]{1,0:T(8,128)S(1)} %get-tuple-element.40), channel_id=1, source_target_pairs={{4,8},{8,4},{5,9},{9,5},{6,10},{10,6},{7,11},{11,7},{12,16},{16,12... | collective-permute-start | bytes 24584 | tf_op jit(solution)/shard_map/ppermute | solution.py:527
  10.7 3.2 %collective-permute-start.5 = (f32[16,128]{1,0:T(8,128)S(1)}, f32[16,128]{1,0:T(8,128)S(1)}, u32[]{:S(2)}, u32[]{:S(2)}) collective-permute-start(f32[16,128]{1,0:T(8,128)S(1)} %get-tuple-element.41), channel_id=1, source_target_pairs={{0,4},{4,0},{1,5},{5,1},{2,6},{6,2},{3,7},{7,3},{8,12},{12,8},{9,1... | collective-permute-start | bytes 24584 | tf_op jit(solution)/shard_map/ppermute | solution.py:527

commit v4 on v2

v4 whole, which is shorter than its diff:
```python
import functools

import jax
import jax.numpy as jnp
from jax import lax
from jax.experimental import pallas as pl
from jax.experimental.pallas import tpu as pltpu
from jax.sharding import PartitionSpec as P

POLAR = 24
BAND = 24
POLE = POLAR + BAND
WEST = 12
SEG = 24
FACES = 11
OFF_LANE = 120
FRAC_LANE = 121
PAIR = 4
EDGE = 8

f32 = jnp.float32
bf16 = jnp.bfloat16
i32 = jnp.int32
VMEM = pltpu.VMEM


def lanes(shape):
    return lax.broadcasted_iota(i32, shape, 1)


def rolled(value, steps):
    steps = steps % value.shape[1]
    return pltpu.roll(value, steps, 1) if steps else value


def pick(table, index):
    return jnp.take_along_axis(table, index, axis=1, mode="promise_in_bounds")


def parabola(c, right, left, centre):
    jump = right - left
    curve = 6.0 * centre - 3.0 * (left + right)
    return c * (right - 0.5 * c * (jump - (1.0 - (2.0 / 3.0) * c) * curve))


def times(value, matrix):
    high = value.astype(bf16)
    low = (value - high.astype(f32)).astype(bf16)
    return jnp.dot(high, matrix, preferred_element_type=f32) + jnp.dot(
        low, matrix, preferred_element_type=f32
    )


def for_west(packed):
    half, cells = packed.shape[0] // 2, packed.shape[1]
    lane = lanes((half, cells))
    place = lane % SEG
    first = (lane >= OFF_LANE) & (lane < OFF_LANE + 2)
    first = first | ((lane < OFF_LANE) & (place >= WEST - 2) & (place < WEST + 2))
    return jnp.where(first, packed[:half], rolled(packed[half:], PAIR))


def edge_weights(gap):
    def weight(gap):
        inner = (gap == 0) | (gap == 1)
        outer = (gap == -1) | (gap == 2)
        return jnp.where(inner, 7.0, jnp.where(outer, -1.0, 0.0))

    return weight(gap), weight(gap + 1)


def split(table, cells):
    return [table[:, i : i + cells] for i in range(0, table.shape[1], cells)]


def pack_kernel(
    lat_count, tracers, offsets, fraction, courant,
    field, offset, part, north, packed, to_east, to_west, pole, sems,
):
    depth, row_count, cells = field.shape
    copies = [
        pltpu.make_async_copy(source, target, sems.at[i])
        for i, (source, target) in enumerate(
            ((tracers, field), (offsets, offset), (fraction, part), (courant, north))
        )
    ]
    for copy in copies:
        copy.start()
    for copy in copies[:3]:
        copy.wait()
    shape = (row_count, cells)
    lane = lanes(shape)
    message = jnp.where(
        lane == OFF_LANE,
        rolled(offset[...].astype(f32), OFF_LANE),
        jnp.where(lane == FRAC_LANE, rolled(part[...], FRAC_LANE), 0.0),
    )
    for t in range(depth):
        mine = (lane >= t * SEG) & (lane < (t + 1) * SEG)
        message = jnp.where(mine, rolled(field[t], t * SEG + WEST), message)
    packed[...] = message
    to_east[:row_count] = message
    to_west[...] = for_west(message)
    lat = lax.axis_index("lat")
    south = lat == 0

    @pl.when(south | (lat == lat_count - 1))
    def _():
        base, band, polar, mid = pole_places(south, row_count)
        rows = [field[t, pl.ds(band, BAND)] for t in range(depth)]
        lane = lanes(rows[0].shape)
        half = cells // 2
        for t in range(0, depth - 1, 2):
            value = jnp.where(lane >= half, rows[t], rolled(rows[t + 1], half))
            to_east[pl.ds(pl.multiple_of(base + t // 2 * BAND, 8), BAND)] = value
        rest = rolled(rows[depth - 1], OFF_LANE - cells)
        for t in range(depth):
            mine = (lane >= 3 * t) & (lane < 3 * t + 3)
            rest = jnp.where(mine, rolled(rows[t], 3 * t + 3 - half), rest)
        kept = (lane % SEG < WEST) | (lane >= OFF_LANE)
        for i, value in enumerate((rest, rolled(rest, WEST))):
            at = pl.ds(pl.multiple_of(mid + i * BAND, 8), BAND)
            to_east[at] = jnp.where(kept, to_east[at], value)
        for t in range(depth):
            value = field[t, pl.ds(polar, POLAR)]
            first = row_count + t * POLAR
            to_east[first : first + POLAR] = value
            pole[t * POLAR : (t + 1) * POLAR] = value
    copies[3].wait()


def pole_places(south, row_count):
    places = (
        jnp.where(south, 0, row_count - POLE),
        jnp.where(south, POLAR, row_count - POLE),
        jnp.where(south, 0, row_count - POLAR),
        jnp.where(south, POLE, 0),
    )
    return [pl.multiple_of(place, 8) for place in places]


def by_place(lat_count, away, south, north):
    lat = lax.axis_index("lat")
    if away is not None:
        pl.when((lat > 0) & (lat < lat_count - 1))(away)
    pl.when(lat == 0)(south)
    pl.when(lat == lat_count - 1)(north)


def pieces(row_count):
    middle = [(POLE, row_count - 2 * POLE)] if row_count > 2 * POLE else []
    return [(0, POLE), *middle, (row_count - POLE, POLE)]


def mid_pieces(row_count):
    return pieces(row_count), pieces(row_count)[1:], pieces(row_count)[:-1]


def own_faces(first_row, count, field, offset, part, block_matrix, flux, seam_index, seam_part):
    depth, _, cells = field.shape
    at = pl.ds(first_row, count)
    shape = (count, cells)
    lane = lanes(shape)
    place = lane % SEG
    offsets = offset[at]
    courant = part[at]
    index = (lane - offsets - 1) & (cells - 1)
    own = field[:, at].reshape(depth * count, cells)
    tables = times(own, block_matrix[:cells, : 3 * cells])
    for t in range(depth):
        sums, right, left = split(tables[t * count : (t + 1) * count], cells)
        value = field[t, at]
        flux[t, at] = (
            sums
            - value
            - pick(sums, index)
            + parabola(
                courant, pick(right, index) * (1 / 12), pick(left, index) * (1 / 12), pick(value, index)
            )
        )
    first = (place - WEST) & (cells - 1)
    final = jnp.full(shape, cells - 1, i32)
    seam_index[0, at] = (lane - pick(offsets, first) - 1) & (cells - 1)
    seam_index[1, at] = (lane - pick(offsets, final) - 1) & (cells - 1)
    seam_part[0, at] = pick(courant, first)
    seam_part[1, at] = pick(courant, final)


def own_kernel(lat_count, field, offset, part, flux, seam_index, seam_part, block_matrix, seam_matrix):
    _, row_count, cells = field.shape
    shape = (cells, cells)
    source = lax.broadcasted_iota(i32, shape, 0)
    target = lax.broadcasted_iota(i32, shape, 1)
    gap = source - target
    upto = jnp.where(gap <= 0, 1.0, 0.0)
    right, left = edge_weights(gap)
    block_matrix[:cells] = jnp.concatenate([upto, right, left, jnp.ones(shape, f32)], axis=1).astype(bf16)
    zeros = jnp.zeros(shape, f32)
    beyond = gap + jnp.where(source < cells // 2, cells, -cells)
    block_matrix[cells:] = jnp.concatenate([zeros, *edge_weights(beyond), zeros], axis=1).astype(bf16)
    together = source // SEG == target // SEG
    seam_matrix[...] = jnp.concatenate([jnp.where(together, upto, 0.0), right, left], axis=1).astype(bf16)

    def step(parts):
        for first, count in parts:
            own_faces(first, count, field, offset, part, block_matrix, flux, seam_index, seam_part)

    by_place(lat_count, *(functools.partial(step, parts) for parts in mid_pieces(row_count)))


def rows_after(field, flux, packed, seam_index, seam_part, from_west, from_east, seam_matrix, parts):
    def take(ref, *lead):
        return jnp.concatenate([ref[(*lead, part)] for part in parts], axis=0)

    mine, west = take(packed), take(from_west)
    east = from_east if isinstance(from_east, jax.Array) else take(from_east)
    count, cells = mine.shape
    shape = mine.shape
    lane = lanes(shape)
    place = lane % SEG
    near = place < WEST
    rows = jnp.concatenate([jnp.where(near, west, mine), jnp.where(near, mine, east)], axis=0)
    next_face = place == WEST
    next_offset = pick(east, jnp.full(shape, OFF_LANE, i32)).astype(i32)
    next_part = pick(east, jnp.full(shape, FRAC_LANE, i32))
    next_index = (lane - next_offset - 1) & (cells - 1)
    index = jnp.concatenate(
        [take(seam_index, 0), jnp.where(next_face, next_index, take(seam_index, 1))], axis=0
    )
    courant = jnp.concatenate(
        [take(seam_part, 0), jnp.where(next_face, next_part, take(seam_part, 1))], axis=0
    )
    sums, right, left = split(times(rows, seam_matrix[...]), cells)
    faces = (
        sums
        - rows
        - pick(sums, index)
        + parabola(
            courant, pick(right, index) * (1 / 12), pick(left, index) * (1 / 12), pick(rows, index)
        )
    )
    east_faces = faces[count:]
    both = jnp.where(place == WEST - 1, east_faces, faces[:count])
    outside = (lane < FACES) | (lane == cells - 1)
    results = []
    for t in range(field.shape[0]):
        steps = -(t * SEG + WEST)
        face = jnp.where(outside, rolled(both, steps), take(flux, t))
        following = jnp.where(lane == cells - 1, rolled(east_faces, steps - 1), rolled(face, -1))
        results.append(take(field, t) - (following - face))
    return results


def edge_kernel(
    lat_count, field, flux, packed, seam_index, seam_part, seam_matrix, north, from_east, from_west,
    message_a, message_b, wide, east,
):
    depth, row_count, _ = field.shape
    half = row_count // 2
    even = lax.axis_index("lat") % 2 == 0

    def step(parts, beyond):
        return rows_after(
            field, flux, packed, seam_index, seam_part, from_west, beyond, seam_matrix, parts
        )

    def send(t, top, bottom):
        rows = slice(3 * t, 3 * t + 3)
        message_a[rows] = jnp.where(even, top, bottom)
        message_b[rows] = jnp.where(even, bottom, top)

    def away():
        beyond = jnp.concatenate(
            [from_east[:EDGE], rolled(from_east[half - EDGE :], -PAIR)], axis=0
        )
        after = step((pl.ds(0, EDGE), pl.ds(row_count - EDGE, EDGE)), beyond)
        for t in range(depth):
            send(t, after[t][2 * EDGE - 3 :], after[t][:3])

    def polar_device(parts):
        east[:half] = from_east[...]
        east[half:] = rolled(from_east[...], -PAIR)
        for first, count in parts:
            after = step((pl.ds(first, count),), east)
            for t in range(depth):
                wide[t, first : first + count] = after[t]
        for t in range(depth):
            send(t, wide[t, row_count - 3 :], wide[t, :3])

    by_place(
        lat_count, away, *(functools.partial(polar_device, parts) for parts in mid_pieces(row_count)[1:])
    )
    message_a[3 * depth : 3 * depth + 1] = north[:1]
    message_b[3 * depth : 3 * depth + 1] = north[:1]


def polar_rows(tables, own, west, west_two, offset, courant, next_offset, next_courant):
    cells = own.shape[1]
    lane = lanes(own.shape)
    (sums, _, _, total), one, two = tables
    source = lane - offset - 1
    index = source & (cells - 1)
    close = source >= -cells

    def both(here, there):
        return jnp.where(close, pick(here, index), pick(there, index))

    face = (
        sums
        - own
        + one[3]
        - both(one[0], two[0] - two[3])
        + parabola(
            courant, both(one[1], two[1]) * (1 / 12), both(one[2], two[2]) * (1 / 12), both(west, west_two)
        )
    )
    index = (cells - 1 - next_offset) & (cells - 1)
    last = parabola(next_courant, one[1] * (1 / 12), one[2] * (1 / 12), west) - one[0]
    last = total + one[3] + pick(last, index)
    following = rolled(jnp.where(lane == 0, last, face), -1)
    return own - (following - face)


def band_rows(tables, own, west, offset, courant, next_offset, next_courant):
    cells = own.shape[1]
    lane = lanes(own.shape)
    here, one = tables
    source = lane - offset - 1
    index = source & (cells - 1)
    inside = source >= 0

    def both(inner, outer):
        return jnp.where(inside, pick(inner, index), pick(outer, index))

    face = (
        here[0]
        - own
        - both(here[0], one[0] - one[3])
        + parabola(
            courant, both(here[1], one[1]) * (1 / 12), both(here[2], one[2]) * (1 / 12), both(own, west)
        )
    )
    index = (cells - 1 - next_offset) & (cells - 1)
    last = parabola(next_courant, here[1] * (1 / 12), here[2] * (1 / 12), own) - here[0]
    last = here[3] + pick(last, index)
    following = rolled(jnp.where(lane == 0, last, face), -1)
    return own - (following - face)


def merid_flux(wide, t, courant, first, count):
    cell = [wide[t, first + k : first + k + count] for k in (-3, -2, -1, 0, 1)]
    left = (7.0 * (cell[1] + cell[2]) - (cell[0] + cell[3])) * (1 / 12)
    right = (7.0 * (cell[2] + cell[3]) - (cell[1] + cell[4])) * (1 / 12)
    return parabola(courant, right, left, cell[2])


def middle_kernel(
    lat_count, field, offset, part, north, flux, packed, seam_index, seam_part, seam_matrix, block_matrix,
    from_east, from_far, from_west, given_wide, given_east, wide, east, inner, far, faces,
):
    del given_wide, given_east
    depth, row_count, cells = field.shape
    half = row_count // 2
    far[:half] = from_far[...]
    far[half:] = rolled(from_far[...], -PAIR)

    def away():
        east[:half] = from_east[...]
        east[half:] = rolled(from_east[...], -PAIR)
        for first, count in pieces(row_count):
            after = rows_after(
                field, flux, packed, seam_index, seam_part, from_west, east, seam_matrix, (pl.ds(first, count),)
            )
            for t in range(depth):
                wide[t, first : first + count] = after[t]
        inner_rows(wide, north, faces, inner, EDGE, row_count - 2 * EDGE)

    def polar_device(south):
        band_step(south, field, offset, part, east, from_west, block_matrix, wide)
        first, _ = near_pole(south, row_count)
        inner_rows(
            wide, north, faces, inner, first + POLAR if south else EDGE, row_count - 2 * EDGE - POLAR
        )

    by_place(
        lat_count, away, functools.partial(polar_device, True), functools.partial(polar_device, False)
    )


def near_pole(south, row_count):
    return (EDGE, POLAR) if south else (row_count - EDGE - POLAR, POLAR)


def inner_rows(wide, north, faces, result, first, count):
    for t in range(wide.shape[0]):
        faces[t, :count] = merid_flux(wide, t, north[first : first + count], first, count)
        end = first + count
        faces[t, count : count + 1] = merid_flux(wide, t, north[end : end + 1], end, 1)
        result[t, first - EDGE : end - EDGE] = wide[t, first:end] - (
            faces[t, 1 : 1 + count] - faces[t, :count]
        )


def with_sides(west, own, east):
    beside = jnp.where(lanes(own.shape) < own.shape[1] // 2, east, west)
    return jnp.concatenate([own, beside], axis=1)


def unpacked(ref, rows, lane, depth):
    value = ref[rows]
    return jnp.concatenate([rolled(value, lane - t * SEG) for t in range(depth)], axis=0)


def stacked(ref, rows):
    return ref[:, rows, :].reshape(-1, ref.shape[2])


def row_values(offset, part, east, rows):
    beyond = east[rows]
    return (
        offset[rows],
        part[rows],
        pick(beyond, jnp.full(beyond.shape, OFF_LANE, i32)).astype(i32),
        pick(beyond, jnp.full(beyond.shape, FRAC_LANE, i32)),
    )


def band_step(south, field, offset, part, east, from_west, block_matrix, wide):
    depth, row_count, cells = field.shape
    base, band, _, mid = (int(place) for place in static_places(south, row_count))
    rows = pl.ds(band, BAND)
    own = stacked(field, rows)
    half = cells // 2
    pair = from_west[mid : mid + BAND], from_west[mid + BAND : mid + 2 * BAND]
    lane = lanes(pair[0].shape)
    rest = jnp.where(lane % SEG >= WEST, pair[0], rolled(pair[1], -WEST))
    west = []
    for t in range(depth):
        if t < depth - 1:
            value = from_west[base + t // 2 * BAND : base + (t // 2 + 1) * BAND]
            value = rolled(value, half) if t % 2 else value
        else:
            value = rolled(rest, cells - OFF_LANE)
        inner = jnp.where(lane >= half - 3, rolled(rest, half - 3 - 3 * t), 0.0)
        west.append(jnp.where(lane >= half, value, inner))
    west = jnp.concatenate(west, axis=0)
    beyond = unpacked(east, rows, -WEST, depth)
    tables = jnp.concatenate([with_sides(west, own, beyond), with_sides(west, west, own)], axis=0)
    tables = times(tables, block_matrix[...])
    common = row_values(offset, part, east, rows)
    for t in range(depth):
        at = slice(t * BAND, (t + 1) * BAND)
        both = [split(tables[first : first + BAND], cells) for first in (t * BAND, (depth + t) * BAND)]
        wide[t, rows] = band_rows(both, own[at], west[at], *common)


def static_places(south, row_count):
    return (0, POLAR, 0, POLE) if south else (row_count - POLE, row_count - POLE, row_count - POLAR, 0)


def edge_rows(lat_count, wide, north, message_b, message_a, low, high, result):
    depth, row_count, cells = wide.shape
    lat = lax.axis_index("lat")
    even = lat % 2 == 0
    south, top = lat == 0, lat == lat_count - 1
    end = 3 * depth
    north_courant = jnp.where(even, message_a[end : end + 1], message_b[end : end + 1])
    north_courant = jnp.where(top, 0.0, north_courant)
    first_row = lax.broadcasted_iota(i32, (EDGE, cells), 0)
    low_courant = jnp.where(south & (first_row == 0), 0.0, north[:EDGE])
    high_next = jnp.concatenate([north[row_count - EDGE + 1 :], north_courant], axis=0)
    for t in range(depth):
        rows = slice(3 * t, 3 * t + 3)
        from_a, from_b = message_a[rows], message_b[rows]
        low[t, EDGE - 3 : EDGE] = jnp.where(south, 0.0, jnp.where(even, from_b, from_a))
        low[t, EDGE : 3 * EDGE] = wide[t, : 2 * EDGE]
        high[t, : 2 * EDGE] = wide[t, row_count - 2 * EDGE :]
        high[t, 2 * EDGE : 2 * EDGE + 3] = jnp.where(top, 0.0, jnp.where(even, from_a, from_b))
    for t in range(depth):
        south_face = merid_flux(low, t, low_courant, EDGE, EDGE)
        north_face = merid_flux(low, t, north[1 : EDGE + 1], EDGE + 1, EDGE)
        result[0, t] = low[t, EDGE : 2 * EDGE] - (north_face - south_face)
        south_face = merid_flux(high, t, north[row_count - EDGE :], EDGE, EDGE)
        north_face = merid_flux(high, t, high_next, EDGE + 1, EDGE)
        result[1, t] = high[t, EDGE : 2 * EDGE] - (north_face - south_face)


def copy_edges(result, out, sems):
    row_count = out.shape[1]
    return [
        pltpu.make_async_copy(result.at[i], out.at[:, pl.ds(first, EDGE)], sems.at[i])
        for i, first in enumerate((0, row_count - EDGE))
    ]


def poles_kernel(
    lat_count, field, offset, part, north, block_matrix, east, far, from_west, pole_two, message_b, message_a,
    given_wide, given_inner, wide, inner, out, faces, low, high, result, sems,
):
    del given_wide, given_inner

    def polar_device(south):
        depth, row_count, cells = field.shape
        near, beside = near_pole(south, row_count)
        done = near + POLAR if south else EDGE
        count = row_count - 2 * EDGE - POLAR
        copies = [
            pltpu.make_async_copy(
                inner.at[:, pl.ds(first - EDGE, size)], out.at[:, pl.ds(first, size)], sems.at[2 + i]
            )
            for i, (first, size) in enumerate(((done, count), (near, beside)))
        ]
        copies[0].start()
        first = static_places(south, row_count)[2]
        rows = pl.ds(first, POLAR)
        own, west, west_two = stacked(field, rows), from_west[row_count:], pole_two[...]
        beyond = unpacked(far, rows, cells - WEST, depth)
        tables = jnp.concatenate(
            [with_sides(west_two, west, own), with_sides(beyond, west_two, west)], axis=0
        )
        tables = times(tables, block_matrix[...])
        own_tables = times(own, block_matrix[:cells])
        common = row_values(offset, part, east, rows)
        for t in range(depth):
            at = slice(t * POLAR, (t + 1) * POLAR)
            one, two = (
                split(tables[start : start + POLAR], cells) for start in (t * POLAR, (depth + t) * POLAR)
            )
            wide[t, rows] = polar_rows(
                (split(own_tables[at], cells), one, two), own[at], west[at], west_two[at], *common
            )
        inner_rows(wide, north, faces, inner, near, beside)
        copies[1].start()
        edge_rows(lat_count, wide, north, message_b, message_a, low, high, result)
        copies += copy_edges(result, out, sems)
        for copy in copies[2:]:
            copy.start()
        for copy in copies:
            copy.wait()

    by_place(
        lat_count, None, functools.partial(polar_device, True), functools.partial(polar_device, False)
    )


def last_kernel(
    lat_count, wide, inner, north, message_b, message_a, given_out, out, low, high, result, sems
):
    del given_out

    def away():
        count = inner.shape[1]
        inner_copy = pltpu.make_async_copy(inner, out.at[:, pl.ds(EDGE, count)], sems.at[2])
        inner_copy.start()
        edge_rows(lat_count, wide, north, message_b, message_a, low, high, result)
        copies = copy_edges(result, out, sems)
        for copy in copies:
            copy.start()
        for copy in (inner_copy, *copies):
            copy.wait()

    lat = lax.axis_index("lat")
    pl.when((lat > 0) & (lat < lat_count - 1))(away)


def cost(microseconds):
    return pl.CostEstimate(
        flops=int(microseconds * 1e8), bytes_accessed=int(microseconds * 3e6), transcendentals=0
    )


def in_vmem(*values):
    return [pltpu.with_memory_space_constraint(value, VMEM) for value in values]


def whole(count):
    return [pl.BlockSpec(memory_space=VMEM)] * count


def anywhere(count):
    return [pl.BlockSpec(memory_space=pl.ANY)] * count


def on_device(lat_count, lon_count, tracers, offsets, fraction, courant_north):
    tracer_count, level_count, row_count, cells = tracers.shape
    depth = tracer_count * level_count
    shape = (row_count, cells)
    stack = (depth, row_count, cells)
    dma = pltpu.SemaphoreType.DMA

    partner = {l: l ^ 1 for l in range(2, lat_count - 2)}
    if lat_count % 2 == 0 and lat_count >= 8:
        for l, other in ((1, 3), (2, lat_count - 2)):
            partner[l], partner[other] = other, l

    def along_lon(value, steps, everywhere=True):
        pairs = []
        for l in range(lat_count):
            for o in range(lon_count):
                if everywhere or len(partner) < lat_count - 2 or l in (0, lat_count - 1):
                    target = (l, (o + steps) % lon_count)
                else:
                    target = (partner[l], o)
                pairs.append((l * lon_count + o, target[0] * lon_count + target[1]))
        return lax.ppermute(value, ("lat", "lon"), pairs)

    def along_lat(value, first):
        pairs = []
        for l in range(lat_count):
            other = l + 1 if (l - first) % 2 == 0 else l - 1
            for o in range(lon_count):
                if 0 <= other < lat_count:
                    target = (other, o)
                else:
                    target = (l, (o + 1) % lon_count if lon_count % 2 else o ^ 1)
                pairs.append((l * lon_count + o, target[0] * lon_count + target[1]))
        return lax.ppermute(value, ("lat", "lon"), pairs)

    field, offset, part, north, packed, to_east, to_west, pole = in_vmem(
        *pl.pallas_call(
            functools.partial(pack_kernel, lat_count),
            out_shape=[
                VMEM(stack, f32),
                VMEM(shape, i32),
                VMEM(shape, f32),
                VMEM(shape, f32),
                VMEM(shape, f32),
                VMEM((row_count + depth * POLAR, cells), f32),
                VMEM((row_count // 2, cells), f32),
                VMEM((depth * POLAR, cells), f32),
            ],
            in_specs=anywhere(4),
            out_specs=whole(8),
            scratch_shapes=[dma((4,))],
            cost_estimate=cost(1.0),
            name="pack",
        )(tracers.reshape(stack), offsets, fraction, courant_north)
    )
    from_west = along_lon(to_east, 1)
    from_east = along_lon(to_west, -1)
    from_far = from_east if lon_count == 4 else along_lon(to_west, 3)
    pole_two = along_lon(pole, 2, False)

    flux, seam_index, seam_part, block_matrix, seam_matrix = in_vmem(
        *pl.pallas_call(
            functools.partial(own_kernel, lat_count),
            out_shape=[
                VMEM(stack, f32),
                VMEM((2, *shape), i32),
                VMEM((2, *shape), f32),
                VMEM((2 * cells, 4 * cells), bf16),
                VMEM((cells, 3 * cells), bf16),
            ],
            in_specs=whole(3),
            out_specs=whole(5),
            cost_estimate=cost(2.0),
            name="own",
        )(field, offset, part)
    )
    from_west, from_east, from_far, pole_two = in_vmem(from_west, from_east, from_far, pole_two)

    message = (3 * depth + 1, cells)
    longer = 56
    message_a, message_b, wide, east = in_vmem(
        *pl.pallas_call(
            functools.partial(edge_kernel, lat_count),
            out_shape=[VMEM(message, f32), VMEM((longer, cells), f32), VMEM(stack, f32), VMEM(shape, f32)],
            in_specs=whole(9),
            out_specs=whole(4),
            cost_estimate=cost(4.0),
            name="edge",
        )(field, flux, packed, seam_index, seam_part, seam_matrix, north, from_east, from_west)
    )
    message_a = along_lat(message_a, 0)
    message_b = along_lat(message_b, 1)

    inner = VMEM((depth, row_count - 2 * EDGE, cells), f32)
    faces = VMEM((depth, row_count - EDGE, cells), f32)
    wide, east, inner_part, far = in_vmem(
        *pl.pallas_call(
            functools.partial(middle_kernel, lat_count),
            out_shape=[VMEM(stack, f32), VMEM(shape, f32), inner, VMEM(shape, f32)],
            in_specs=whole(15),
            out_specs=whole(4),
            scratch_shapes=[faces],
            input_output_aliases={13: 0, 14: 1},
            cost_estimate=cost(3.0),
            name="middle",
        )(
            field, offset, part, north, flux, packed, seam_index, seam_part, seam_matrix, block_matrix,
            from_east, from_far, from_west, wide, east,
        )
    )

    message_a, message_b = in_vmem(message_a, message_b)
    scratch = [
        VMEM((depth, 3 * EDGE, cells), f32),
        VMEM((depth, 3 * EDGE, cells), f32),
        VMEM((2, depth, EDGE, cells), f32),
        dma((4,)),
    ]
    polar_b = message_b if lat_count % 2 else message_a
    wide, inner, out = pl.pallas_call(
        functools.partial(poles_kernel, lat_count),
        out_shape=[VMEM(stack, f32), inner, jax.ShapeDtypeStruct(stack, f32)],
        in_specs=whole(13),
        out_specs=whole(2) + anywhere(1),
        scratch_shapes=[faces, *scratch],
        input_output_aliases={11: 0, 12: 1},
        cost_estimate=cost(0.0),
        name="poles",
    )(
        field, offset, part, north, block_matrix, east, far, from_west, pole_two, polar_b, message_a,
        wide, inner_part,
    )

    out = pl.pallas_call(
        functools.partial(last_kernel, lat_count),
        out_shape=jax.ShapeDtypeStruct(stack, f32),
        in_specs=whole(5) + anywhere(1),
        out_specs=pl.BlockSpec(memory_space=pl.ANY),
        scratch_shapes=scratch,
        input_output_aliases={5: 0},
        cost_estimate=cost(0.7),
        name="last",
    )(*in_vmem(wide, inner), north, message_b, message_a, out)
    return out.reshape(tracers.shape)


def solution(mesh):
    placed = (P(None, None, "lat", "lon"), P("lat", "lon"), P("lat", "lon"), P("lat", "lon"))
    return jax.shard_map(
        functools.partial(on_device, mesh.shape["lat"], mesh.shape["lon"]),
        mesh=mesh,
        in_specs=placed,
        out_specs=P(None, None, "lat", "lon"),
        check_vma=False,
    )
```

time: 16.8 us -> 14.3 us (0.85)
  Pallas kernels: 6.01 us -> 4.71 us
  starting transfers between devices: 8.52 us -> 7.7 us
  waiting for transfers between devices: 2.03 us -> 1.73 us
    pallas_call x1, Pallas kernels: 2.88 us -> 0.86 us  [on_device(): pl.pallas_call(functools.partial(middle_kernel, lat_count), out_shape=[VM...]
    ppermute x4 -> x3, starting transfers between devices: 7.69 us -> 6.11 us  [along_lon(): return lax.ppermute(value, ('lat', 'lon'), pairs)]
    pallas_call x3 -> x4, Pallas kernels: 2.42 us -> 3.81 us  [the longest x1 1.38 us: on_device(): pl.pallas_call(functools.partial(poles_kernel, lat_count), out_shape=[VME...]
    ppermute x2, starting transfers between devices: 0.83 us -> 1.58 us  [along_lat(): return lax.ppermute(value, ('lat', 'lon'), pairs)]
    pallas_call x1, Pallas kernels: 0.72 us -> 0.04 us  [on_device(): pl.pallas_call(functools.partial(last_kernel, lat_count), out_shape=jax.S...]
    ppermute x4 -> x3, waiting for transfers between devices: 2.03 us -> 1.66 us  [along_lon(): return lax.ppermute(value, ('lat', 'lon'), pairs)]
  transfers between devices with their start and end apart: 6 -> 5, of which waited for: 2 -> 3; matrix products, arithmetic and copies ran while one was open for 0% -> 0% of each run, Pallas kernels for 25% -> 24%
where the time goes in v4:
time: 14.3 us; the launch traced here: 14.2 us
  starting transfers between devices  7.7 us (54%)
  Pallas kernels  4.71 us (33%)
  waiting for transfers between devices  1.73 us (12%)
    ppermute x3, starting transfers between devices, along_lon(): return lax.ppermute(value, ('lat', 'lon'), pairs)  6.11 us
    ppermute x3, waiting for transfers between devices, along_lon(): return lax.ppermute(value, ('lat', 'lon'), pairs)  1.66 us
    ppermute x2, starting transfers between devices, along_lat(): return lax.ppermute(value, ('lat', 'lon'), pairs)  1.58 us
    pallas_call x1, Pallas kernels, on_device(): pl.pallas_call(functools.partial(poles_kernel, lat_count), out_shape=[VME...  1.38 us
    pallas_call x1, Pallas kernels, on_device(): pl.pallas_call(functools.partial(pack_kernel, lat_count), out_shape=[VMEM...  1.33 us
    pallas_call x1, Pallas kernels, on_device(): pl.pallas_call(functools.partial(middle_kernel, lat_count), out_shape=[VM...  0.86 us
    pallas_call x1, Pallas kernels, on_device(): pl.pallas_call(functools.partial(own_kernel, lat_count), out_shape=[VMEM(...  0.55 us
    pallas_call x1, Pallas kernels, on_device(): pl.pallas_call(functools.partial(edge_kernel, lat_count), out_shape=[VMEM...  0.55 us
  transfers between devices with their start and end apart: 5, of which 3 were waited for; matrix products, arithmetic and copies ran while one was open for 0% of the time, Pallas kernels for 24%

profile of v4, /device:TPU:0, one launch (start us, length us, event | category | flops | bytes accessed | tf_op | source)
XLA Modules:
  0.0 14.2 jit_solution(17785999006728487501)
XLA Ops:
  0.0 1.3 %pack.1 = (f32[5,96,128]{2,1,0:T(8,128)S(1)}, s32[96,128]{1,0:T(8,128)S(1)}, f32[96,128]{1,0:T(8,128)S(1)}, f32[96,128]{1,0:T(8,128)S(1)}, f32[96,128]{1,0:T(8,1...) custom-call(f32[5,96,128]{2,1,0:T(8,128)} %bitcast.4, s32[96,128]{1,0:T(8,128)} %offsets.1, ...), custom_call_target="tpu_custom_call" | custom-call | flops 100000000 | bytes 3000000 | tf_op jit(solution)/shard_map/pack/pallas_call | solution.py:620
  1.3 3.1 %collective-permute-start.1 = (f32[216,128]{1,0:T(8,128)S(1)}, f32[216,128]{1,0:T(8,128)S(1)}, u32[]{:S(2)}, u32[]{:S(2)}) collective-permute-start(f32[216,128]{1,0:T(8,128)S(1)} %get-tuple-element.40), channel_id=1, source_target_pairs={{0,1},{1,2},{2,3},{3,0},{4,5},{5,6},{6,7},{7,4},{8,9},{9,10},{10,1... | collective-permute-start | bytes 331784 | tf_op jit(solution)/shard_map/ppermute | solution.py:605
  4.4 2.1 %collective-permute-start = (f32[48,128]{1,0:T(8,128)S(1)}, f32[48,128]{1,0:T(8,128)S(1)}, u32[]{:S(2)}, u32[]{:S(2)}) collective-permute-start(f32[48,128]{1,0:T(8,128)S(1)} %get-tuple-element.39), channel_id=1, source_target_pairs={{0,3},{1,0},{2,1},{3,2},{4,7},{5,4},{6,5},{7,6},{8,11},{9,8},{10,9... | collective-permute-start | bytes 73736 | tf_op jit(solution)/shard_map/ppermute | solution.py:605
  6.5 0.9 %collective-permute-start.2 = (f32[120,128]{1,0:T(8,128)S(1)}, f32[120,128]{1,0:T(8,128)S(1)}, u32[]{:S(2)}, u32[]{:S(2)}) collective-permute-start(f32[120,128]{1,0:T(8,128)S(1)} %get-tuple-element.45), channel_id=1, source_target_pairs={{0,2},{1,3},{2,0},{3,1},{4,12},{5,13},{6,14},{7,15},{8,24},{9,25},... | collective-permute-start | bytes 184328 | tf_op jit(solution)/shard_map/ppermute | solution.py:605
  7.5 0.5 %own.1 = (f32[5,96,128]{2,1,0:T(8,128)S(1)}, s32[2,96,128]{2,1,0:T(8,128)S(1)}, f32[2,96,128]{2,1,0:T(8,128)S(1)}, bf16[256,512]{1,0:T(8,128)(2,1)S(1)}, bf16[128,384]{1,0:T(8,128)(2,1)S(1)}) custom-call(f32[5,96,128]{2,1,0:T(8,128)S(1)} %get-tuple-element.29.field, s32[96,128]{1,0:T(8,128)S(1)} %get-tuple-element.30.offset, ...), custom_call_target="tpu_custom_call" | custom-call | flops 200000000 | bytes 6000000 | tf_op jit(solution)/shard_map/own/pallas_call | solution.py:645
  8.0 1.5 %collective-permute-done.from_east.from_far = f32[48,128]{1,0:T(8,128)S(1)} collective-permute-done((f32[48,128]{1,0:T(8,128)S(1)}, f32[48,128]{1,0:T(8,128)S(1)}, u32[]{:S(2)}, u32[]{:S(2)}) %collective-permute-start) | collective-permute-done | bytes 24608 | tf_op jit(solution)/shard_map/ppermute | solution.py:605
  9.5 0.2 %collective-permute-done.1.from_west = f32[216,128]{1,0:T(8,128)S(1)} collective-permute-done((f32[216,128]{1,0:T(8,128)S(1)}, f32[216,128]{1,0:T(8,128)S(1)}, u32[]{:S(2)}, u32[]{:S(2)}) %collective-permute-start.1) | collective-permute-done | bytes 110624 | tf_op jit(solution)/shard_map/ppermute | solution.py:605
  9.7 0.5 %edge.1 = (f32[16,128]{1,0:T(8,128)S(1)}, f32[56,128]{1,0:T(8,128)S(1)}, f32[5,96,128]{2,1,0:T(8,128)S(1)}, f32[96,128]{1,0:T(8,128)S(1)}) custom-call(f32[5,96,128]{2,1,0:T(8,128)S(1)} %get-tuple-element.29.field, f32[5,96,128]{2,1,0:T(8,128)S(1)} %get-tuple-element.34.flux, f32[96,128]{1,0:T(8,128)S(1)} %get-tuple-element.35.packed, ...), custom_call_target="tpu_custom_call" | custom-call | flops 400000000 | bytes 12000000 | tf_op jit(solution)/shard_map/edge/pallas_call | solution.py:665
  10.2 0.8 %collective-permute-start.4 = (f32[56,128]{1,0:T(8,128)S(1)}, f32[56,128]{1,0:T(8,128)S(1)}, u32[]{:S(2)}, u32[]{:S(2)}) collective-permute-start(f32[56,128]{1,0:T(8,128)S(1)} %get-tuple-element.51), channel_id=1, source_target_pairs={{0,1},{1,0},{2,3},{3,2},{4,8},{5,9},{6,10},{7,11},{8,4},{9,5},{10,... | collective-permute-start | bytes 86024 | tf_op jit(solution)/shard_map/ppermute | solution.py:617
  11.1 0.7 %collective-permute-start.3 = (f32[16,128]{1,0:T(8,128)S(1)}, f32[16,128]{1,0:T(8,128)S(1)}, u32[]{:S(2)}, u32[]{:S(2)}) collective-permute-start(f32[16,128]{1,0:T(8,128)S(1)} %get-tuple-element.46), channel_id=1, source_target_pairs={{0,4},{1,5},{2,6},{3,7},{4,0},{5,1},{6,2},{7,3},{8,12},{9,13},{10,... | collective-permute-start | bytes 24584 | tf_op jit(solution)/shard_map/ppermute | solution.py:617
  11.8 0.9 %middle.1 = (f32[5,96,128]{2,1,0:T(8,128)S(1)}, f32[96,128]{1,0:T(8,128)S(1)}, f32[5,80,128]{2,1,0:T(8,128)S(1)}, f32[96,128]{1,0:T(8,128)S(1)}) custom-call(f32[5,96,128]{2,1,0:T(8,128)S(1)} %get-tuple-element.29.field, s32[96,128]{1,0:T(8,128)S(1)} %get-tuple-element.30.offset, ...), custom_call_target="tpu_custom_call", output_to_operand_aliasing={{0}: (13, {}), {1}: (14, {})} | custom-call | flops 300000000 | bytes 9000000 | tf_op jit(solution)/shard_map/middle/pallas_call | solution.py:680
  12.7 0.0 collective-permute-done.2.pole_two
  12.7 0.0 collective-permute-done.3.message_b.message_a
  12.7 1.4 %poles.1 = (f32[5,96,128]{2,1,0:T(8,128)S(1)}, f32[5,80,128]{2,1,0:T(8,128)S(1)}, f32[5,96,128]{2,1,0:T(8,128)}) custom-call(f32[5,96,128]{2,1,0:T(8,128)S(1)} %get-tuple-element.29.field, s32[96,128]{1,0:T(8,128)S(1)} %get-tuple-element.30.offset, f32[96,128]{1,0:T(8,128)S(1)} %get-tuple-element.31.part, ...), custom_call_target="tpu_custom_call", output_to_operand_aliasing={{0}: (11, {}), {1}: (12, {})} | custom-call | tf_op jit(solution)/shard_map/poles/pallas_call | solution.py:703
  14.1 0.1 collective-permute-done.4.message_b
  (1 shorter events, 0.0 us)
Async XLA Ops:
  1.3 8.3 %collective-permute-start.1 = (f32[216,128]{1,0:T(8,128)S(1)}, f32[216,128]{1,0:T(8,128)S(1)}, u32[]{:S(2)}, u32[]{:S(2)}) collective-permute-start(f32[216,128]{1,0:T(8,128)S(1)} %get-tuple-element.40), channel_id=1, source_target_pairs={{0,1},{1,2},{2,3},{3,0},{4,5},{5,6},{6,7},{7,4},{8,9},{9,10},{10,1... | collective-permute-start | bytes 331784 | tf_op jit(solution)/shard_map/ppermute | solution.py:605
  4.4 5.1 %collective-permute-start = (f32[48,128]{1,0:T(8,128)S(1)}, f32[48,128]{1,0:T(8,128)S(1)}, u32[]{:S(2)}, u32[]{:S(2)}) collective-permute-start(f32[48,128]{1,0:T(8,128)S(1)} %get-tuple-element.39), channel_id=1, source_target_pairs={{0,3},{1,0},{2,1},{3,2},{4,7},{5,4},{6,5},{7,6},{8,11},{9,8},{10,9... | collective-permute-start | bytes 73736 | tf_op jit(solution)/shard_map/ppermute | solution.py:605
  6.5 6.2 %collective-permute-start.2 = (f32[120,128]{1,0:T(8,128)S(1)}, f32[120,128]{1,0:T(8,128)S(1)}, u32[]{:S(2)}, u32[]{:S(2)}) collective-permute-start(f32[120,128]{1,0:T(8,128)S(1)} %get-tuple-element.45), channel_id=1, source_target_pairs={{0,2},{1,3},{2,0},{3,1},{4,12},{5,13},{6,14},{7,15},{8,24},{9,25},... | collective-permute-start | bytes 184328 | tf_op jit(solution)/shard_map/ppermute | solution.py:605
  10.2 3.9 %collective-permute-start.4 = (f32[56,128]{1,0:T(8,128)S(1)}, f32[56,128]{1,0:T(8,128)S(1)}, u32[]{:S(2)}, u32[]{:S(2)}) collective-permute-start(f32[56,128]{1,0:T(8,128)S(1)} %get-tuple-element.51), channel_id=1, source_target_pairs={{0,1},{1,0},{2,3},{3,2},{4,8},{5,9},{6,10},{7,11},{8,4},{9,5},{10,... | collective-permute-start | bytes 86024 | tf_op jit(solution)/shard_map/ppermute | solution.py:617
  11.1 1.6 %collective-permute-start.3 = (f32[16,128]{1,0:T(8,128)S(1)}, f32[16,128]{1,0:T(8,128)S(1)}, u32[]{:S(2)}, u32[]{:S(2)}) collective-permute-start(f32[16,128]{1,0:T(8,128)S(1)} %get-tuple-element.46), channel_id=1, source_target_pairs={{0,4},{1,5},{2,6},{3,7},{4,0},{5,1},{6,2},{7,3},{8,12},{9,13},{10,... | collective-permute-start | bytes 24584 | tf_op jit(solution)/shard_map/ppermute | solution.py:617

commit v5 on v4

--- a/solution.py
+++ b/solution.py
@@ -39,16 +39,14 @@
 
 def parabola(c, right, left, centre):
     jump = right - left
-    curve = 6.0 * centre - 3.0 * (left + right)
-    return c * (right - 0.5 * c * (jump - (1.0 - (2.0 / 3.0) * c) * curve))
+    curve = 72.0 * centre - 3.0 * (left + right)
+    return c * (1 / 12) * (right - 0.5 * c * (jump - (1.0 - (2.0 / 3.0) * c) * curve))
 
 
 def times(value, matrix):
     high = value.astype(bf16)
     low = (value - high.astype(f32)).astype(bf16)
-    return jnp.dot(high, matrix, preferred_element_type=f32) + jnp.dot(
-        low, matrix, preferred_element_type=f32
-    )
+    return jnp.dot(jnp.concatenate([high, low], axis=1), matrix, preferred_element_type=f32)
 
 
 def for_west(packed):
@@ -99,7 +97,7 @@
         mine = (lane >= t * SEG) & (lane < (t + 1) * SEG)
         message = jnp.where(mine, rolled(field[t], t * SEG + WEST), message)
     packed[...] = message
-    to_east[:row_count] = message
+    to_east[...] = message
     to_west[...] = for_west(message)
     lat = lax.axis_index("lat")
     south = lat == 0
@@ -122,10 +120,7 @@
             at = pl.ds(pl.multiple_of(mid + i * BAND, 8), BAND)
             to_east[at] = jnp.where(kept, to_east[at], value)
         for t in range(depth):
-            value = field[t, pl.ds(polar, POLAR)]
-            first = row_count + t * POLAR
-            to_east[first : first + POLAR] = value
-            pole[t * POLAR : (t + 1) * POLAR] = value
+            pole[t * POLAR : (t + 1) * POLAR] = field[t, pl.ds(polar, POLAR)]
     copies[3].wait()
 
 
@@ -156,7 +151,7 @@
     return pieces(row_count), pieces(row_count)[1:], pieces(row_count)[:-1]
 
 
-def own_faces(first_row, count, field, offset, part, block_matrix, flux, seam_index, seam_part):
+def own_faces(first_row, count, field, offset, part, own_matrix, flux, seam_index, seam_part):
     depth, _, cells = field.shape
     at = pl.ds(first_row, count)
     shape = (count, cells)
@@ -166,7 +161,7 @@
     courant = part[at]
     index = (lane - offsets - 1) & (cells - 1)
     own = field[:, at].reshape(depth * count, cells)
-    tables = times(own, block_matrix[:cells, : 3 * cells])
+    tables = times(own, own_matrix[...])
     for t in range(depth):
         sums, right, left = split(tables[t * count : (t + 1) * count], cells)
         value = field[t, at]
@@ -175,7 +170,7 @@
             - value
             - pick(sums, index)
             + parabola(
-                courant, pick(right, index) * (1 / 12), pick(left, index) * (1 / 12), pick(value, index)
+                courant, pick(right, index), pick(left, index), pick(value, index)
             )
         )
     first = (place - WEST) & (cells - 1)
@@ -186,7 +181,9 @@
     seam_part[1, at] = pick(courant, final)
 
 
-def own_kernel(lat_count, field, offset, part, flux, seam_index, seam_part, block_matrix, seam_matrix):
+def own_kernel(
+    lat_count, field, offset, part, flux, seam_index, seam_part, block_matrix, seam_matrix, own_matrix
+):
     _, row_count, cells = field.shape
     shape = (cells, cells)
     source = lax.broadcasted_iota(i32, shape, 0)
@@ -194,16 +191,21 @@
     gap = source - target
     upto = jnp.where(gap <= 0, 1.0, 0.0)
     right, left = edge_weights(gap)
-    block_matrix[:cells] = jnp.concatenate([upto, right, left, jnp.ones(shape, f32)], axis=1).astype(bf16)
+    own = jnp.concatenate([upto, right, left, upto - 1.0], axis=1).astype(bf16)
     zeros = jnp.zeros(shape, f32)
     beyond = gap + jnp.where(source < cells // 2, cells, -cells)
-    block_matrix[cells:] = jnp.concatenate([zeros, *edge_weights(beyond), zeros], axis=1).astype(bf16)
+    beside = jnp.concatenate([zeros, *edge_weights(beyond), zeros], axis=1).astype(bf16)
     together = source // SEG == target // SEG
-    seam_matrix[...] = jnp.concatenate([jnp.where(together, upto, 0.0), right, left], axis=1).astype(bf16)
+    seam = jnp.concatenate([jnp.where(together, upto, 0.0), right, left], axis=1).astype(bf16)
+    for i in range(2):
+        block_matrix[2 * i * cells : (2 * i + 1) * cells] = own
+        block_matrix[(2 * i + 1) * cells : (2 * i + 2) * cells] = beside
+        own_matrix[i * cells : (i + 1) * cells] = own[:, : 3 * cells]
+        seam_matrix[i * cells : (i + 1) * cells] = seam
 
     def step(parts):
         for first, count in parts:
-            own_faces(first, count, field, offset, part, block_matrix, flux, seam_index, seam_part)
+            own_faces(first, count, field, offset, part, own_matrix, flux, seam_index, seam_part)
 
     by_place(lat_count, *(functools.partial(step, parts) for parts in mid_pieces(row_count)))
 
@@ -236,7 +238,7 @@
         - rows
         - pick(sums, index)
         + parabola(
-            courant, pick(right, index) * (1 / 12), pick(left, index) * (1 / 12), pick(rows, index)
+            courant, pick(right, index), pick(left, index), pick(rows, index)
         )
     )
     east_faces = faces[count:]
@@ -294,63 +296,28 @@
     message_b[3 * depth : 3 * depth + 1] = north[:1]
 
 
-def polar_rows(tables, own, west, west_two, offset, courant, next_offset, next_courant):
-    cells = own.shape[1]
-    lane = lanes(own.shape)
-    (sums, _, _, total), one, two = tables
+def rows_between(near, far, near_field, far_field, first, offset, courant, next_offset, next_courant):
+    cells = near_field.shape[1]
+    lane = lanes(near_field.shape)
     source = lane - offset - 1
     index = source & (cells - 1)
-    close = source >= -cells
+    close = source >= first
 
     def both(here, there):
         return jnp.where(close, pick(here, index), pick(there, index))
 
-    face = (
-        sums
-        - own
-        + one[3]
-        - both(one[0], two[0] - two[3])
-        + parabola(
-            courant, both(one[1], two[1]) * (1 / 12), both(one[2], two[2]) * (1 / 12), both(west, west_two)
-        )
-    )
-    index = (cells - 1 - next_offset) & (cells - 1)
-    last = parabola(next_courant, one[1] * (1 / 12), one[2] * (1 / 12), west) - one[0]
-    last = total + one[3] + pick(last, index)
-    following = rolled(jnp.where(lane == 0, last, face), -1)
-    return own - (following - face)
-
-
-def band_rows(tables, own, west, offset, courant, next_offset, next_courant):
-    cells = own.shape[1]
-    lane = lanes(own.shape)
-    here, one = tables
-    source = lane - offset - 1
-    index = source & (cells - 1)
-    inside = source >= 0
-
-    def both(inner, outer):
-        return jnp.where(inside, pick(inner, index), pick(outer, index))
-
-    face = (
-        here[0]
-        - own
-        - both(here[0], one[0] - one[3])
-        + parabola(
-            courant, both(here[1], one[1]) * (1 / 12), both(here[2], one[2]) * (1 / 12), both(own, west)
-        )
-    )
-    index = (cells - 1 - next_offset) & (cells - 1)
-    last = parabola(next_courant, here[1] * (1 / 12), here[2] * (1 / 12), own) - here[0]
-    last = here[3] + pick(last, index)
-    following = rolled(jnp.where(lane == 0, last, face), -1)
-    return own - (following - face)
+    face = both(near[0], far[3]) - parabola(
+        courant, both(near[1], far[1]), both(near[2], far[2]), both(near_field, far_field)
+    )
+    last = near[0] - parabola(next_courant, near[1], near[2], near_field)
+    last = pick(last, (cells - 1 - next_offset) & (cells - 1))
+    return rolled(jnp.where(lane == 0, last, face), -1) - face
 
 
 def merid_flux(wide, t, courant, first, count):
     cell = [wide[t, first + k : first + k + count] for k in (-3, -2, -1, 0, 1)]
-    left = (7.0 * (cell[1] + cell[2]) - (cell[0] + cell[3])) * (1 / 12)
-    right = (7.0 * (cell[2] + cell[3]) - (cell[1] + cell[4])) * (1 / 12)
+    left = 7.0 * (cell[1] + cell[2]) - (cell[0] + cell[3])
+    right = 7.0 * (cell[2] + cell[3]) - (cell[1] + cell[4])
     return parabola(courant, right, left, cell[2])
 
 
@@ -451,7 +418,7 @@
     for t in range(depth):
         at = slice(t * BAND, (t + 1) * BAND)
         both = [split(tables[first : first + BAND], cells) for first in (t * BAND, (depth + t) * BAND)]
-        wide[t, rows] = band_rows(both, own[at], west[at], *common)
+        wide[t, rows] = rows_between(*both, own[at], west[at], 0, *common)
 
 
 def static_places(south, row_count):
@@ -494,7 +461,7 @@
 
 
 def poles_kernel(
-    lat_count, field, offset, part, north, block_matrix, east, far, from_west, pole_two, message_b, message_a,
+    lat_count, field, offset, part, north, block_matrix, east, far, pole_one, pole_two, message_b, message_a,
     given_wide, given_inner, wide, inner, out, faces, low, high, result, sems,
 ):
     del given_wide, given_inner
@@ -513,22 +480,17 @@
         copies[0].start()
         first = static_places(south, row_count)[2]
         rows = pl.ds(first, POLAR)
-        own, west, west_two = stacked(field, rows), from_west[row_count:], pole_two[...]
+        own, west, west_two = stacked(field, rows), pole_one[...], pole_two[...]
         beyond = unpacked(far, rows, cells - WEST, depth)
         tables = jnp.concatenate(
             [with_sides(west_two, west, own), with_sides(beyond, west_two, west)], axis=0
         )
         tables = times(tables, block_matrix[...])
-        own_tables = times(own, block_matrix[:cells])
         common = row_values(offset, part, east, rows)
         for t in range(depth):
             at = slice(t * POLAR, (t + 1) * POLAR)
-            one, two = (
-                split(tables[start : start + POLAR], cells) for start in (t * POLAR, (depth + t) * POLAR)
-            )
-            wide[t, rows] = polar_rows(
-                (split(own_tables[at], cells), one, two), own[at], west[at], west_two[at], *common
-            )
+            both = [split(tables[start : start + POLAR], cells) for start in (t * POLAR, (depth + t) * POLAR)]
+            wide[t, rows] = rows_between(*both, west[at], west_two[at], -cells, *common)
         inner_rows(wide, north, faces, inner, near, beside)
         copies[1].start()
         edge_rows(lat_count, wide, north, message_b, message_a, low, high, result)
@@ -606,13 +568,18 @@
 
     def along_lat(value, first):
         pairs = []
+        last_lat, last_lon = lat_count - 1, lon_count - 1
         for l in range(lat_count):
             other = l + 1 if (l - first) % 2 == 0 else l - 1
             for o in range(lon_count):
                 if 0 <= other < lat_count:
                     target = (other, o)
+                elif lat_count % 2:
+                    target = (l, (o + 1) % lon_count)
+                elif l == 0:
+                    target = (0, o - 1) if o else (last_lat, 0)
                 else:
-                    target = (l, (o + 1) % lon_count if lon_count % 2 else o ^ 1)
+                    target = (last_lat, o + 1) if o < last_lon else (0, last_lon)
                 pairs.append((l * lon_count + o, target[0] * lon_count + target[1]))
         return lax.ppermute(value, ("lat", "lon"), pairs)
 
@@ -625,7 +592,7 @@
                 VMEM(shape, f32),
                 VMEM(shape, f32),
                 VMEM(shape, f32),
-                VMEM((row_count + depth * POLAR, cells), f32),
+                VMEM(shape, f32),
                 VMEM((row_count // 2, cells), f32),
                 VMEM((depth * POLAR, cells), f32),
             ],
@@ -639,6 +606,7 @@
     from_west = along_lon(to_east, 1)
     from_east = along_lon(to_west, -1)
     from_far = from_east if lon_count == 4 else along_lon(to_west, 3)
+    pole_one = along_lon(pole, 1, False)
     pole_two = along_lon(pole, 2, False)
 
     flux, seam_index, seam_part, block_matrix, seam_matrix = in_vmem(
@@ -648,19 +616,22 @@
                 VMEM(stack, f32),
                 VMEM((2, *shape), i32),
                 VMEM((2, *shape), f32),
-                VMEM((2 * cells, 4 * cells), bf16),
-                VMEM((cells, 3 * cells), bf16),
+                VMEM((4 * cells, 4 * cells), bf16),
+                VMEM((2 * cells, 3 * cells), bf16),
             ],
             in_specs=whole(3),
             out_specs=whole(5),
+            scratch_shapes=[VMEM((2 * cells, 3 * cells), bf16)],
             cost_estimate=cost(2.0),
             name="own",
         )(field, offset, part)
     )
-    from_west, from_east, from_far, pole_two = in_vmem(from_west, from_east, from_far, pole_two)
+    from_west, from_east, from_far, pole_one, pole_two = in_vmem(
+        from_west, from_east, from_far, pole_one, pole_two
+    )
 
     message = (3 * depth + 1, cells)
-    longer = 56
+    longer = 64
     message_a, message_b, wide, east = in_vmem(
         *pl.pallas_call(
             functools.partial(edge_kernel, lat_count),
@@ -710,7 +681,7 @@
         cost_estimate=cost(0.0),
         name="poles",
     )(
-        field, offset, part, north, block_matrix, east, far, from_west, pole_two, polar_b, message_a,
+        field, offset, part, north, block_matrix, east, far, pole_one, pole_two, polar_b, message_a,
         wide, inner_part,
     )
 

time: 14.3 us -> 14.2 us (level)
  starting transfers between devices: 7.7 us -> 9.17 us
  waiting for transfers between devices: 1.73 us -> 0.3 us
    ppermute x3 -> x4, starting transfers between devices: 6.11 us -> 7.69 us  [along_lon(): return lax.ppermute(value, ('lat', 'lon'), pairs)]
    ppermute x3 -> x4, waiting for transfers between devices: 1.66 us -> 0.1 us  [along_lon(): return lax.ppermute(value, ('lat', 'lon'), pairs)]
  transfers between devices with their start and end apart: 5 -> 6, of which waited for: 3 -> 2; matrix products, arithmetic and copies ran while one was open for 0% -> 0% of each run, Pallas kernels for 24% -> 23%
where the time goes in v5:
time: 14.2 us; the launch traced here: 14.1 us
  starting transfers between devices  9.17 us (65%)
  Pallas kernels  4.57 us (32%)
  waiting for transfers between devices  0.3 us (2%)
    ppermute x4, starting transfers between devices, along_lon(): return lax.ppermute(value, ('lat', 'lon'), pairs)  7.69 us
    ppermute x2, starting transfers between devices, along_lat(): return lax.ppermute(value, ('lat', 'lon'), pairs)  1.48 us
    pallas_call x1, Pallas kernels, on_device(): pl.pallas_call(functools.partial(poles_kernel, lat_count), out_shape=[VME...  1.34 us
    pallas_call x1, Pallas kernels, on_device(): pl.pallas_call(functools.partial(pack_kernel, lat_count), out_shape=[VMEM...  1.33 us
    pallas_call x1, Pallas kernels, on_device(): pl.pallas_call(functools.partial(middle_kernel, lat_count), out_shape=[VM...  0.84 us
    pallas_call x1, Pallas kernels, on_device(): pl.pallas_call(functools.partial(own_kernel, lat_count), out_shape=[VMEM(...  0.53 us
    pallas_call x1, Pallas kernels, on_device(): pl.pallas_call(functools.partial(edge_kernel, lat_count), out_shape=[VMEM...  0.5 us
  transfers between devices with their start and end apart: 6, of which 2 were waited for; matrix products, arithmetic and copies ran while one was open for 0% of the time, Pallas kernels for 23%

profile of v5, /device:TPU:0, one launch (start us, length us, event | category | flops | bytes accessed | tf_op | source)
XLA Modules:
  0.0 14.1 jit_solution(9582999525874844277)
XLA Ops:
  0.0 1.3 %pack.1 = (f32[5,96,128]{2,1,0:T(8,128)S(1)}, s32[96,128]{1,0:T(8,128)S(1)}, f32[96,128]{1,0:T(8,128)S(1)}, f32[96,128]{1,0:T(8,128)S(1)}, f32[96,128]{1,0:T(8,1...) custom-call(f32[5,96,128]{2,1,0:T(8,128)} %bitcast.4, s32[96,128]{1,0:T(8,128)} %offsets.1, ...), custom_call_target="tpu_custom_call" | custom-call | flops 100000000 | bytes 3000000 | tf_op jit(solution)/shard_map/pack/pallas_call | solution.py:587
  1.3 3.1 %collective-permute-start.1 = (f32[96,128]{1,0:T(8,128)S(1)}, f32[96,128]{1,0:T(8,128)S(1)}, u32[]{:S(2)}, u32[]{:S(2)}) collective-permute-start(f32[96,128]{1,0:T(8,128)S(1)} %get-tuple-element.40), channel_id=1, source_target_pairs={{0,1},{1,2},{2,3},{3,0},{4,5},{5,6},{6,7},{7,4},{8,9},{9,10},{10,1... | collective-permute-start | bytes 147464 | tf_op jit(solution)/shard_map/ppermute | solution.py:567
  4.4 2.1 %collective-permute-start = (f32[48,128]{1,0:T(8,128)S(1)}, f32[48,128]{1,0:T(8,128)S(1)}, u32[]{:S(2)}, u32[]{:S(2)}) collective-permute-start(f32[48,128]{1,0:T(8,128)S(1)} %get-tuple-element.39), channel_id=1, source_target_pairs={{0,3},{1,0},{2,1},{3,2},{4,7},{5,4},{6,5},{7,6},{8,11},{9,8},{10,9... | collective-permute-start | bytes 73736 | tf_op jit(solution)/shard_map/ppermute | solution.py:567
  6.5 0.0 collective-permute-start.2
  6.5 2.5 %collective-permute-start.3 = (f32[120,128]{1,0:T(8,128)S(1)}, f32[120,128]{1,0:T(8,128)S(1)}, u32[]{:S(2)}, u32[]{:S(2)}) collective-permute-start(f32[120,128]{1,0:T(8,128)S(1)} %get-tuple-element.45), channel_id=1, source_target_pairs={{0,2},{1,3},{2,0},{3,1},{4,12},{5,13},{6,14},{7,15},{8,24},{9,25},... | collective-permute-start | bytes 184328 | tf_op jit(solution)/shard_map/ppermute | solution.py:567
  9.0 0.5 %own.1 = (f32[5,96,128]{2,1,0:T(8,128)S(1)}, s32[2,96,128]{2,1,0:T(8,128)S(1)}, f32[2,96,128]{2,1,0:T(8,128)S(1)}, bf16[512,512]{1,0:T(8,128)(2,1)S(1)}, bf16[256,384]{1,0:T(8,128)(2,1)S(1)}) custom-call(f32[5,96,128]{2,1,0:T(8,128)S(1)} %get-tuple-element.29.field, s32[96,128]{1,0:T(8,128)S(1)} %get-tuple-element.30.offset, ...), custom_call_target="tpu_custom_call" | custom-call | flops 200000000 | bytes 6000000 | tf_op jit(solution)/shard_map/own/pallas_call | solution.py:613
  9.6 0.0 collective-permute-done.from_east.from_far
  9.6 0.0 collective-permute-done.1.from_west
  9.6 0.5 %edge.1 = (f32[16,128]{1,0:T(8,128)S(1)}, f32[64,128]{1,0:T(8,128)S(1)}, f32[5,96,128]{2,1,0:T(8,128)S(1)}, f32[96,128]{1,0:T(8,128)S(1)}) custom-call(f32[5,96,128]{2,1,0:T(8,128)S(1)} %get-tuple-element.29.field, f32[5,96,128]{2,1,0:T(8,128)S(1)} %get-tuple-element.34.flux, f32[96,128]{1,0:T(8,128)S(1)} %get-tuple-element.35.packed, ...), custom_call_target="tpu_custom_call" | custom-call | flops 400000000 | bytes 12000000 | tf_op jit(solution)/shard_map/edge/pallas_call | solution.py:636
  10.1 0.8 %collective-permute-start.5 = (f32[64,128]{1,0:T(8,128)S(1)}, f32[64,128]{1,0:T(8,128)S(1)}, u32[]{:S(2)}, u32[]{:S(2)}) collective-permute-start(f32[64,128]{1,0:T(8,128)S(1)} %get-tuple-element.51), channel_id=1, source_target_pairs={{0,28},{1,0},{2,1},{3,2},{4,8},{5,9},{6,10},{7,11},{8,4},{9,5},{10... | collective-permute-start | bytes 98312 | tf_op jit(solution)/shard_map/ppermute | solution.py:584
  10.9 0.7 %collective-permute-start.4 = (f32[16,128]{1,0:T(8,128)S(1)}, f32[16,128]{1,0:T(8,128)S(1)}, u32[]{:S(2)}, u32[]{:S(2)}) collective-permute-start(f32[16,128]{1,0:T(8,128)S(1)} %get-tuple-element.46), channel_id=1, source_target_pairs={{0,4},{1,5},{2,6},{3,7},{4,0},{5,1},{6,2},{7,3},{8,12},{9,13},{10,... | collective-permute-start | bytes 24584 | tf_op jit(solution)/shard_map/ppermute | solution.py:584
  11.6 0.8 %middle.1 = (f32[5,96,128]{2,1,0:T(8,128)S(1)}, f32[96,128]{1,0:T(8,128)S(1)}, f32[5,80,128]{2,1,0:T(8,128)S(1)}, f32[96,128]{1,0:T(8,128)S(1)}) custom-call(f32[5,96,128]{2,1,0:T(8,128)S(1)} %get-tuple-element.29.field, s32[96,128]{1,0:T(8,128)S(1)} %get-tuple-element.30.offset, ...), custom_call_target="tpu_custom_call", output_to_operand_aliasing={{0}: (13, {}), {1}: (14, {})} | custom-call | flops 300000000 | bytes 9000000 | tf_op jit(solution)/shard_map/middle/pallas_call | solution.py:651
  12.4 0.0 collective-permute-done.4.message_b.message_a
  12.4 0.1 collective-permute-done.2.pole_one
  12.5 0.0 collective-permute-done.3.pole_two
  12.5 1.3 %poles.1 = (f32[5,96,128]{2,1,0:T(8,128)S(1)}, f32[5,80,128]{2,1,0:T(8,128)S(1)}, f32[5,96,128]{2,1,0:T(8,128)}) custom-call(f32[5,96,128]{2,1,0:T(8,128)S(1)} %get-tuple-element.29.field, s32[96,128]{1,0:T(8,128)S(1)} %get-tuple-element.30.offset, f32[96,128]{1,0:T(8,128)S(1)} %get-tuple-element.31.part, ...), custom_call_target="tpu_custom_call", output_to_operand_aliasing={{0}: (11, {}), {1}: (12, {})} | custom-call | tf_op jit(solution)/shard_map/poles/pallas_call | solution.py:674
  13.9 0.2 %collective-permute-done.5.message_b = f32[64,128]{1,0:T(8,128)S(1)} collective-permute-done((f32[64,128]{1,0:T(8,128)S(1)}, f32[64,128]{1,0:T(8,128)S(1)}, u32[]{:S(2)}, u32[]{:S(2)}) %collective-permute-start.5) | collective-permute-done | bytes 32800 | tf_op jit(solution)/shard_map/ppermute | solution.py:584
  (1 shorter events, 0.0 us)
Async XLA Ops:
  1.3 8.2 %collective-permute-start.1 = (f32[96,128]{1,0:T(8,128)S(1)}, f32[96,128]{1,0:T(8,128)S(1)}, u32[]{:S(2)}, u32[]{:S(2)}) collective-permute-start(f32[96,128]{1,0:T(8,128)S(1)} %get-tuple-element.40), channel_id=1, source_target_pairs={{0,1},{1,2},{2,3},{3,0},{4,5},{5,6},{6,7},{7,4},{8,9},{9,10},{10,1... | collective-permute-start | bytes 147464 | tf_op jit(solution)/shard_map/ppermute | solution.py:567
  4.4 5.2 %collective-permute-start = (f32[48,128]{1,0:T(8,128)S(1)}, f32[48,128]{1,0:T(8,128)S(1)}, u32[]{:S(2)}, u32[]{:S(2)}) collective-permute-start(f32[48,128]{1,0:T(8,128)S(1)} %get-tuple-element.39), channel_id=1, source_target_pairs={{0,3},{1,0},{2,1},{3,2},{4,7},{5,4},{6,5},{7,6},{8,11},{9,8},{10,9... | collective-permute-start | bytes 73736 | tf_op jit(solution)/shard_map/ppermute | solution.py:567
  6.5 6.0 %collective-permute-start.2 = (f32[120,128]{1,0:T(8,128)S(1)}, f32[120,128]{1,0:T(8,128)S(1)}, u32[]{:S(2)}, u32[]{:S(2)}) collective-permute-start(f32[120,128]{1,0:T(8,128)S(1)} %get-tuple-element.45), channel_id=1, source_target_pairs={{0,1},{1,2},{2,3},{3,0},{4,12},{5,13},{6,14},{7,15},{8,24},{9,25},... | collective-permute-start | bytes 184328 | tf_op jit(solution)/shard_map/ppermute | solution.py:567
  6.5 6.0 %collective-permute-start.3 = (f32[120,128]{1,0:T(8,128)S(1)}, f32[120,128]{1,0:T(8,128)S(1)}, u32[]{:S(2)}, u32[]{:S(2)}) collective-permute-start(f32[120,128]{1,0:T(8,128)S(1)} %get-tuple-element.45), channel_id=1, source_target_pairs={{0,2},{1,3},{2,0},{3,1},{4,12},{5,13},{6,14},{7,15},{8,24},{9,25},... | collective-permute-start | bytes 184328 | tf_op jit(solution)/shard_map/ppermute | solution.py:567
  10.1 4.0 %collective-permute-start.5 = (f32[64,128]{1,0:T(8,128)S(1)}, f32[64,128]{1,0:T(8,128)S(1)}, u32[]{:S(2)}, u32[]{:S(2)}) collective-permute-start(f32[64,128]{1,0:T(8,128)S(1)} %get-tuple-element.51), channel_id=1, source_target_pairs={{0,28},{1,0},{2,1},{3,2},{4,8},{5,9},{6,10},{7,11},{8,4},{9,5},{10... | collective-permute-start | bytes 98312 | tf_op jit(solution)/shard_map/ppermute | solution.py:584
  10.9 1.5 %collective-permute-start.4 = (f32[16,128]{1,0:T(8,128)S(1)}, f32[16,128]{1,0:T(8,128)S(1)}, u32[]{:S(2)}, u32[]{:S(2)}) collective-permute-start(f32[16,128]{1,0:T(8,128)S(1)} %get-tuple-element.46), channel_id=1, source_target_pairs={{0,4},{1,5},{2,6},{3,7},{4,0},{5,1},{6,2},{7,3},{8,12},{9,13},{10,... | collective-permute-start | bytes 24584 | tf_op jit(solution)/shard_map/ppermute | solution.py:584

commit v6 on v5

--- a/solution.py
+++ b/solution.py
@@ -631,7 +631,7 @@
     )
 
     message = (3 * depth + 1, cells)
-    longer = 64
+    longer = 24
     message_a, message_b, wide, east = in_vmem(
         *pl.pallas_call(
             functools.partial(edge_kernel, lat_count),
@@ -655,7 +655,7 @@
             out_specs=whole(4),
             scratch_shapes=[faces],
             input_output_aliases={13: 0, 14: 1},
-            cost_estimate=cost(3.0),
+            cost_estimate=cost(0.0),
             name="middle",
         )(
             field, offset, part, north, flux, packed, seam_index, seam_part, seam_matrix, block_matrix,

time: 14.2 us -> 14.1 us (level)
  waiting for transfers between devices: 0.3 us -> 0.1 us
    ppermute x2, waiting for transfers between devices: 0.2 us -> 0.01 us  [along_lat(): return lax.ppermute(value, ('lat', 'lon'), pairs)]
  transfers between devices with their start and end apart: 6 -> 6, of which waited for: 2 -> 1; matrix products, arithmetic and copies ran while one was open for 0% -> 0% of each run, Pallas kernels for 23% -> 23%
where the time goes in v6:
time: 14.1 us; the launch traced here: 13.9 us
  starting transfers between devices  9.16 us (65%)
  Pallas kernels  4.6 us (33%)
    ppermute x4, starting transfers between devices, along_lon(): return lax.ppermute(value, ('lat', 'lon'), pairs)  7.69 us
    ppermute x2, starting transfers between devices, along_lat(): return lax.ppermute(value, ('lat', 'lon'), pairs)  1.47 us
    pallas_call x1, Pallas kernels, on_device(): pl.pallas_call(functools.partial(poles_kernel, lat_count), out_shape=[VME...  1.34 us
    pallas_call x1, Pallas kernels, on_device(): pl.pallas_call(functools.partial(pack_kernel, lat_count), out_shape=[VMEM...  1.33 us
    pallas_call x1, Pallas kernels, on_device(): pl.pallas_call(functools.partial(middle_kernel, lat_count), out_shape=[VM...  0.84 us
    pallas_call x1, Pallas kernels, on_device(): pl.pallas_call(functools.partial(own_kernel, lat_count), out_shape=[VMEM(...  0.53 us
    pallas_call x1, Pallas kernels, on_device(): pl.pallas_call(functools.partial(edge_kernel, lat_count), out_shape=[VMEM...  0.51 us
  transfers between devices with their start and end apart: 6, of which 1 were waited for; matrix products, arithmetic and copies ran while one was open for 0% of the time, Pallas kernels for 23%

profile of v6, /device:TPU:0, one launch (start us, length us, event | category | flops | bytes accessed | tf_op | source)
XLA Modules:
  0.0 13.9 jit_solution(10265821379750356683)
XLA Ops:
  0.0 1.3 %pack.1 = (f32[5,96,128]{2,1,0:T(8,128)S(1)}, s32[96,128]{1,0:T(8,128)S(1)}, f32[96,128]{1,0:T(8,128)S(1)}, f32[96,128]{1,0:T(8,128)S(1)}, f32[96,128]{1,0:T(8,1...) custom-call(f32[5,96,128]{2,1,0:T(8,128)} %bitcast.4, s32[96,128]{1,0:T(8,128)} %offsets.1, ...), custom_call_target="tpu_custom_call" | custom-call | flops 100000000 | bytes 3000000 | tf_op jit(solution)/shard_map/pack/pallas_call | solution.py:587
  1.3 3.1 %collective-permute-start.1 = (f32[96,128]{1,0:T(8,128)S(1)}, f32[96,128]{1,0:T(8,128)S(1)}, u32[]{:S(2)}, u32[]{:S(2)}) collective-permute-start(f32[96,128]{1,0:T(8,128)S(1)} %get-tuple-element.40), channel_id=1, source_target_pairs={{0,1},{1,2},{2,3},{3,0},{4,5},{5,6},{6,7},{7,4},{8,9},{9,10},{10,1... | collective-permute-start | bytes 147464 | tf_op jit(solution)/shard_map/ppermute | solution.py:567
  4.4 2.1 %collective-permute-start = (f32[48,128]{1,0:T(8,128)S(1)}, f32[48,128]{1,0:T(8,128)S(1)}, u32[]{:S(2)}, u32[]{:S(2)}) collective-permute-start(f32[48,128]{1,0:T(8,128)S(1)} %get-tuple-element.39), channel_id=1, source_target_pairs={{0,3},{1,0},{2,1},{3,2},{4,7},{5,4},{6,5},{7,6},{8,11},{9,8},{10,9... | collective-permute-start | bytes 73736 | tf_op jit(solution)/shard_map/ppermute | solution.py:567
  6.5 0.0 collective-permute-start.2
  6.5 2.5 %collective-permute-start.3 = (f32[120,128]{1,0:T(8,128)S(1)}, f32[120,128]{1,0:T(8,128)S(1)}, u32[]{:S(2)}, u32[]{:S(2)}) collective-permute-start(f32[120,128]{1,0:T(8,128)S(1)} %get-tuple-element.45), channel_id=1, source_target_pairs={{0,2},{1,3},{2,0},{3,1},{4,12},{5,13},{6,14},{7,15},{8,24},{9,25},... | collective-permute-start | bytes 184328 | tf_op jit(solution)/shard_map/ppermute | solution.py:567
  9.0 0.5 %own.1 = (f32[5,96,128]{2,1,0:T(8,128)S(1)}, s32[2,96,128]{2,1,0:T(8,128)S(1)}, f32[2,96,128]{2,1,0:T(8,128)S(1)}, bf16[512,512]{1,0:T(8,128)(2,1)S(1)}, bf16[256,384]{1,0:T(8,128)(2,1)S(1)}) custom-call(f32[5,96,128]{2,1,0:T(8,128)S(1)} %get-tuple-element.29.field, s32[96,128]{1,0:T(8,128)S(1)} %get-tuple-element.30.offset, ...), custom_call_target="tpu_custom_call" | custom-call | flops 200000000 | bytes 6000000 | tf_op jit(solution)/shard_map/own/pallas_call | solution.py:613
  9.6 0.0 collective-permute-done.from_east.from_far
  9.6 0.0 collective-permute-done.1.from_west
  9.6 0.5 %edge.1 = (f32[16,128]{1,0:T(8,128)S(1)}, f32[24,128]{1,0:T(8,128)S(1)}, f32[5,96,128]{2,1,0:T(8,128)S(1)}, f32[96,128]{1,0:T(8,128)S(1)}) custom-call(f32[5,96,128]{2,1,0:T(8,128)S(1)} %get-tuple-element.29.field, f32[5,96,128]{2,1,0:T(8,128)S(1)} %get-tuple-element.34.flux, f32[96,128]{1,0:T(8,128)S(1)} %get-tuple-element.35.packed, ...), custom_call_target="tpu_custom_call" | custom-call | flops 400000000 | bytes 12000000 | tf_op jit(solution)/shard_map/edge/pallas_call | solution.py:636
  10.1 0.8 %collective-permute-start.5 = (f32[24,128]{1,0:T(8,128)S(1)}, f32[24,128]{1,0:T(8,128)S(1)}, u32[]{:S(2)}, u32[]{:S(2)}) collective-permute-start(f32[24,128]{1,0:T(8,128)S(1)} %get-tuple-element.51), channel_id=1, source_target_pairs={{0,28},{1,0},{2,1},{3,2},{4,8},{5,9},{6,10},{7,11},{8,4},{9,5},{10... | collective-permute-start | bytes 36872 | tf_op jit(solution)/shard_map/ppermute | solution.py:584
  10.9 0.7 %collective-permute-start.4 = (f32[16,128]{1,0:T(8,128)S(1)}, f32[16,128]{1,0:T(8,128)S(1)}, u32[]{:S(2)}, u32[]{:S(2)}) collective-permute-start(f32[16,128]{1,0:T(8,128)S(1)} %get-tuple-element.46), channel_id=1, source_target_pairs={{0,4},{1,5},{2,6},{3,7},{4,0},{5,1},{6,2},{7,3},{8,12},{9,13},{10,... | collective-permute-start | bytes 24584 | tf_op jit(solution)/shard_map/ppermute | solution.py:584
  11.6 0.8 %middle.1 = (f32[5,96,128]{2,1,0:T(8,128)S(1)}, f32[96,128]{1,0:T(8,128)S(1)}, f32[5,80,128]{2,1,0:T(8,128)S(1)}, f32[96,128]{1,0:T(8,128)S(1)}) custom-call(f32[5,96,128]{2,1,0:T(8,128)S(1)} %get-tuple-element.29.field, s32[96,128]{1,0:T(8,128)S(1)} %get-tuple-element.30.offset, ...), custom_call_target="tpu_custom_call", output_to_operand_aliasing={{0}: (13, {}), {1}: (14, {})} | custom-call | tf_op jit(solution)/shard_map/middle/pallas_call | solution.py:651
  12.4 0.0 collective-permute-done.4.message_b.message_a
  12.4 0.1 collective-permute-done.2.pole_one
  12.5 0.0 collective-permute-done.3.pole_two
  12.5 1.3 %poles.1 = (f32[5,96,128]{2,1,0:T(8,128)S(1)}, f32[5,80,128]{2,1,0:T(8,128)S(1)}, f32[5,96,128]{2,1,0:T(8,128)}) custom-call(f32[5,96,128]{2,1,0:T(8,128)S(1)} %get-tuple-element.29.field, s32[96,128]{1,0:T(8,128)S(1)} %get-tuple-element.30.offset, f32[96,128]{1,0:T(8,128)S(1)} %get-tuple-element.31.part, ...), custom_call_target="tpu_custom_call", output_to_operand_aliasing={{0}: (11, {}), {1}: (12, {})} | custom-call | tf_op jit(solution)/shard_map/poles/pallas_call | solution.py:674
  13.9 0.0 collective-permute-done.5.message_b
  13.9 0.1 last.1
Async XLA Ops:
  1.3 8.2 %collective-permute-start.1 = (f32[96,128]{1,0:T(8,128)S(1)}, f32[96,128]{1,0:T(8,128)S(1)}, u32[]{:S(2)}, u32[]{:S(2)}) collective-permute-start(f32[96,128]{1,0:T(8,128)S(1)} %get-tuple-element.40), channel_id=1, source_target_pairs={{0,1},{1,2},{2,3},{3,0},{4,5},{5,6},{6,7},{7,4},{8,9},{9,10},{10,1... | collective-permute-start | bytes 147464 | tf_op jit(solution)/shard_map/ppermute | solution.py:567
  4.4 5.2 %collective-permute-start = (f32[48,128]{1,0:T(8,128)S(1)}, f32[48,128]{1,0:T(8,128)S(1)}, u32[]{:S(2)}, u32[]{:S(2)}) collective-permute-start(f32[48,128]{1,0:T(8,128)S(1)} %get-tuple-element.39), channel_id=1, source_target_pairs={{0,3},{1,0},{2,1},{3,2},{4,7},{5,4},{6,5},{7,6},{8,11},{9,8},{10,9... | collective-permute-start | bytes 73736 | tf_op jit(solution)/shard_map/ppermute | solution.py:567
  6.5 6.0 %collective-permute-start.2 = (f32[120,128]{1,0:T(8,128)S(1)}, f32[120,128]{1,0:T(8,128)S(1)}, u32[]{:S(2)}, u32[]{:S(2)}) collective-permute-start(f32[120,128]{1,0:T(8,128)S(1)} %get-tuple-element.45), channel_id=1, source_target_pairs={{0,1},{1,2},{2,3},{3,0},{4,12},{5,13},{6,14},{7,15},{8,24},{9,25},... | collective-permute-start | bytes 184328 | tf_op jit(solution)/shard_map/ppermute | solution.py:567
  6.5 6.0 %collective-permute-start.3 = (f32[120,128]{1,0:T(8,128)S(1)}, f32[120,128]{1,0:T(8,128)S(1)}, u32[]{:S(2)}, u32[]{:S(2)}) collective-permute-start(f32[120,128]{1,0:T(8,128)S(1)} %get-tuple-element.45), channel_id=1, source_target_pairs={{0,2},{1,3},{2,0},{3,1},{4,12},{5,13},{6,14},{7,15},{8,24},{9,25},... | collective-permute-start | bytes 184328 | tf_op jit(solution)/shard_map/ppermute | solution.py:567
  10.1 3.8 %collective-permute-start.5 = (f32[24,128]{1,0:T(8,128)S(1)}, f32[24,128]{1,0:T(8,128)S(1)}, u32[]{:S(2)}, u32[]{:S(2)}) collective-permute-start(f32[24,128]{1,0:T(8,128)S(1)} %get-tuple-element.51), channel_id=1, source_target_pairs={{0,28},{1,0},{2,1},{3,2},{4,8},{5,9},{6,10},{7,11},{8,4},{9,5},{10... | collective-permute-start | bytes 36872 | tf_op jit(solution)/shard_map/ppermute | solution.py:584
  10.9 1.5 %collective-permute-start.4 = (f32[16,128]{1,0:T(8,128)S(1)}, f32[16,128]{1,0:T(8,128)S(1)}, u32[]{:S(2)}, u32[]{:S(2)}) collective-permute-start(f32[16,128]{1,0:T(8,128)S(1)} %get-tuple-element.46), channel_id=1, source_target_pairs={{0,4},{1,5},{2,6},{3,7},{4,0},{5,1},{6,2},{7,3},{8,12},{9,13},{10,... | collective-permute-start | bytes 24584 | tf_op jit(solution)/shard_map/ppermute | solution.py:584

commit v7 on v6

--- a/solution.py
+++ b/solution.py
@@ -16,6 +16,7 @@
 OFF_LANE = 120
 FRAC_LANE = 121
 PAIR = 4
+WITH_WEST = 2
 EDGE = 8
 
 f32 = jnp.float32
@@ -73,7 +74,8 @@
 
 def pack_kernel(
     lat_count, tracers, offsets, fraction, courant,
-    field, offset, part, north, packed, to_east, to_west, pole, sems,
+    field, offset, part, north, packed, to_east, to_west, pole, pole_rest, flux, seam_index, seam_part, block_matrix,
+    seam_matrix, own_matrix, sems,
 ):
     depth, row_count, cells = field.shape
     copies = [
@@ -97,7 +99,7 @@
         mine = (lane >= t * SEG) & (lane < (t + 1) * SEG)
         message = jnp.where(mine, rolled(field[t], t * SEG + WEST), message)
     packed[...] = message
-    to_east[...] = message
+    to_east[:row_count] = message
     to_west[...] = for_west(message)
     lat = lax.axis_index("lat")
     south = lat == 0
@@ -120,7 +122,17 @@
             at = pl.ds(pl.multiple_of(mid + i * BAND, 8), BAND)
             to_east[at] = jnp.where(kept, to_east[at], value)
         for t in range(depth):
-            pole[t * POLAR : (t + 1) * POLAR] = field[t, pl.ds(polar, POLAR)]
+            value = field[t, pl.ds(polar, POLAR)]
+            pole[t * POLAR : (t + 1) * POLAR] = value
+            if t < WITH_WEST:
+                to_east[row_count + t * POLAR : row_count + (t + 1) * POLAR] = value
+            else:
+                pole_rest[(t - WITH_WEST) * POLAR : (t - WITH_WEST + 1) * POLAR] = value
+    pl.when(goes_early())(
+        lambda: own_work(
+            lat_count, field, offset, part, flux, seam_index, seam_part, block_matrix, seam_matrix, own_matrix
+        )
+    )
     copies[3].wait()
 
 
@@ -181,7 +193,24 @@
     seam_part[1, at] = pick(courant, final)
 
 
+def goes_early():
+    lat, lon = lax.axis_index("lat"), lax.axis_index("lon")
+    return (lon == 0) & (lat < 2)
+
+
 def own_kernel(
+    lat_count, field, offset, part, flux_given, index_given, part_given, block_given, seam_given,
+    flux, seam_index, seam_part, block_matrix, seam_matrix, own_matrix,
+):
+    del flux_given, index_given, part_given, block_given, seam_given
+    pl.when(~goes_early())(
+        lambda: own_work(
+            lat_count, field, offset, part, flux, seam_index, seam_part, block_matrix, seam_matrix, own_matrix
+        )
+    )
+
+
+def own_work(
     lat_count, field, offset, part, flux, seam_index, seam_part, block_matrix, seam_matrix, own_matrix
 ):
     _, row_count, cells = field.shape
@@ -460,6 +489,13 @@
     ]
 
 
+def join_kernel(from_west, rest, after, joined):
+    del after
+    count = joined.shape[0] - rest.shape[0]
+    joined[:count] = from_west[from_west.shape[0] - count :]
+    joined[count:] = rest[...]
+
+
 def poles_kernel(
     lat_count, field, offset, part, north, block_matrix, east, far, pole_one, pole_two, message_b, message_a,
     given_wide, given_inner, wide, inner, out, faces, low, high, result, sems,
@@ -550,19 +586,15 @@
     stack = (depth, row_count, cells)
     dma = pltpu.SemaphoreType.DMA
 
-    partner = {l: l ^ 1 for l in range(2, lat_count - 2)}
-    if lat_count % 2 == 0 and lat_count >= 8:
-        for l, other in ((1, 3), (2, lat_count - 2)):
-            partner[l], partner[other] = other, l
-
     def along_lon(value, steps, everywhere=True):
         pairs = []
         for l in range(lat_count):
+            from_pole = min(l, lat_count - 1 - l)
             for o in range(lon_count):
-                if everywhere or len(partner) < lat_count - 2 or l in (0, lat_count - 1):
+                if everywhere or from_pole == 0 or lat_count % 2 or lon_count % 2:
                     target = (l, (o + steps) % lon_count)
                 else:
-                    target = (partner[l], o)
+                    target = (l, o ^ 1) if from_pole == 1 else (l ^ 1, o)
                 pairs.append((l * lon_count + o, target[0] * lon_count + target[1]))
         return lax.ppermute(value, ("lat", "lon"), pairs)
 
@@ -583,7 +615,15 @@
                 pairs.append((l * lon_count + o, target[0] * lon_count + target[1]))
         return lax.ppermute(value, ("lat", "lon"), pairs)
 
-    field, offset, part, north, packed, to_east, to_west, pole = in_vmem(
+    own_shapes = [
+        VMEM(stack, f32),
+        VMEM((2, *shape), i32),
+        VMEM((2, *shape), f32),
+        VMEM((4 * cells, 4 * cells), bf16),
+        VMEM((2 * cells, 3 * cells), bf16),
+    ]
+    own_matrix = VMEM((2 * cells, 3 * cells), bf16)
+    field, offset, part, north, packed, to_east, to_west, pole, pole_rest, *own = in_vmem(
         *pl.pallas_call(
             functools.partial(pack_kernel, lat_count),
             out_shape=[
@@ -592,13 +632,15 @@
                 VMEM(shape, f32),
                 VMEM(shape, f32),
                 VMEM(shape, f32),
-                VMEM(shape, f32),
+                VMEM((row_count + WITH_WEST * POLAR, cells), f32),
                 VMEM((row_count // 2, cells), f32),
                 VMEM((depth * POLAR, cells), f32),
+                VMEM(((depth - WITH_WEST) * POLAR, cells), f32),
+                *own_shapes,
             ],
             in_specs=anywhere(4),
-            out_specs=whole(8),
-            scratch_shapes=[dma((4,))],
+            out_specs=whole(14),
+            scratch_shapes=[own_matrix, dma((4,))],
             cost_estimate=cost(1.0),
             name="pack",
         )(tracers.reshape(stack), offsets, fraction, courant_north)
@@ -606,25 +648,20 @@
     from_west = along_lon(to_east, 1)
     from_east = along_lon(to_west, -1)
     from_far = from_east if lon_count == 4 else along_lon(to_west, 3)
-    pole_one = along_lon(pole, 1, False)
+    pole_one = along_lon(pole_rest, 1, False)
     pole_two = along_lon(pole, 2, False)
 
     flux, seam_index, seam_part, block_matrix, seam_matrix = in_vmem(
         *pl.pallas_call(
             functools.partial(own_kernel, lat_count),
-            out_shape=[
-                VMEM(stack, f32),
-                VMEM((2, *shape), i32),
-                VMEM((2, *shape), f32),
-                VMEM((4 * cells, 4 * cells), bf16),
-                VMEM((2 * cells, 3 * cells), bf16),
-            ],
-            in_specs=whole(3),
+            out_shape=own_shapes,
+            in_specs=whole(8),
             out_specs=whole(5),
-            scratch_shapes=[VMEM((2 * cells, 3 * cells), bf16)],
+            scratch_shapes=[own_matrix],
+            input_output_aliases={3 + i: i for i in range(5)},
             cost_estimate=cost(2.0),
             name="own",
-        )(field, offset, part)
+        )(field, offset, part, *own)
     )
     from_west, from_east, from_far, pole_one, pole_two = in_vmem(
         from_west, from_east, from_far, pole_one, pole_two
@@ -663,7 +700,15 @@
         )
     )
 
-    message_a, message_b = in_vmem(message_a, message_b)
+    pole_one = pl.pallas_call(
+        join_kernel,
+        out_shape=VMEM((depth * POLAR, cells), f32),
+        in_specs=whole(3),
+        out_specs=pl.BlockSpec(memory_space=VMEM),
+        cost_estimate=cost(0.3),
+        name="join",
+    )(from_west, pole_one, far)
+    pole_one, message_a, message_b = in_vmem(pole_one, message_a, message_b)
     scratch = [
         VMEM((depth, 3 * EDGE, cells), f32),
         VMEM((depth, 3 * EDGE, cells), f32),

time: 14.1 us -> 13.9 us (0.986)
  starting transfers between devices: 9.16 us -> 8.7 us
  waiting for transfers between devices: 0.1 us -> 0.42 us
    ppermute x4, starting transfers between devices: 7.69 us -> 7.15 us  [along_lon(): return lax.ppermute(value, ('lat', 'lon'), pairs)]
    pallas_call x1, Pallas kernels: 1.33 us -> 1.87 us  [on_device(): pl.pallas_call(functools.partial(pack_kernel, lat_count), out_shape=[VMEM...]
    pallas_call x1 -> x2, Pallas kernels: 0.53 us -> 0.01 us  [the longest x1 0.01 us: on_device(): pl.pallas_call(join_kernel, out_shape=VMEM((depth * POLAR, cells), f32),...]
    ppermute x4, waiting for transfers between devices: 0.1 us -> 0.37 us  [along_lon(): return lax.ppermute(value, ('lat', 'lon'), pairs)]
  transfers between devices with their start and end apart: 6 -> 6, of which waited for: 1 -> 2; matrix products, arithmetic and copies ran while one was open for 0% -> 0% of each run, Pallas kernels for 23% -> 19%
where the time goes in v7:
time: 13.9 us; the launch traced here: 13.7 us
  starting transfers between devices  8.7 us (63%)
  Pallas kernels  4.57 us (33%)
  waiting for transfers between devices  0.42 us (3%)
    ppermute x4, starting transfers between devices, along_lon(): return lax.ppermute(value, ('lat', 'lon'), pairs)  7.15 us
    pallas_call x1, Pallas kernels, on_device(): pl.pallas_call(functools.partial(pack_kernel, lat_count), out_shape=[VMEM...  1.87 us
    ppermute x2, starting transfers between devices, along_lat(): return lax.ppermute(value, ('lat', 'lon'), pairs)  1.55 us
    pallas_call x1, Pallas kernels, on_device(): pl.pallas_call(functools.partial(poles_kernel, lat_count), out_shape=[VME...  1.36 us
    pallas_call x1, Pallas kernels, on_device(): pl.pallas_call(functools.partial(middle_kernel, lat_count), out_shape=[VM...  0.83 us
    pallas_call x1, Pallas kernels, on_device(): pl.pallas_call(functools.partial(edge_kernel, lat_count), out_shape=[VMEM...  0.48 us
    ppermute x4, waiting for transfers between devices, along_lon(): return lax.ppermute(value, ('lat', 'lon'), pairs)  0.37 us
  transfers between devices with their start and end apart: 6, of which 2 were waited for; matrix products, arithmetic and copies ran while one was open for 0% of the time, Pallas kernels for 19%

profile of v7, /device:TPU:0, one launch (start us, length us, event | category | flops | bytes accessed | tf_op | source)
XLA Modules:
  0.0 13.7 jit_solution(11386103221728666179)
XLA Ops:
  0.0 1.9 %pack.1 = (f32[5,96,128]{2,1,0:T(8,128)S(1)}, s32[96,128]{1,0:T(8,128)S(1)}, f32[96,128]{1,0:T(8,128)S(1)}, f32[96,128]{1,0:T(8,128)S(1)}, f32[96,128]{1,0:T(8,1...) custom-call(f32[5,96,128]{2,1,0:T(8,128)} %bitcast.4, ...), custom_call_target="tpu_custom_call" | custom-call | flops 100000000 | bytes 3000000 | tf_op jit(solution)/shard_map/pack/pallas_call | solution.py:627
  1.9 2.5 %collective-permute-start.1 = (f32[144,128]{1,0:T(8,128)S(1)}, f32[144,128]{1,0:T(8,128)S(1)}, u32[]{:S(2)}, u32[]{:S(2)}) collective-permute-start(f32[144,128]{1,0:T(8,128)S(1)} %get-tuple-element.51), channel_id=1, source_target_pairs={{0,1},{1,2},{2,3},{3,0},{4,5},{5,6},{6,7},{7,4},{8,9},{9,10},{10,1... | collective-permute-start | bytes 221192 | tf_op jit(solution)/shard_map/ppermute | solution.py:599
  4.4 2.1 %collective-permute-start = (f32[48,128]{1,0:T(8,128)S(1)}, f32[48,128]{1,0:T(8,128)S(1)}, u32[]{:S(2)}, u32[]{:S(2)}) collective-permute-start(f32[48,128]{1,0:T(8,128)S(1)} %get-tuple-element.50), channel_id=1, source_target_pairs={{0,3},{1,0},{2,1},{3,2},{4,7},{5,4},{6,5},{7,6},{8,11},{9,8},{10,9... | collective-permute-start | bytes 73736 | tf_op jit(solution)/shard_map/ppermute | solution.py:599
  6.5 0.0 collective-permute-start.2
  6.5 2.5 %collective-permute-start.3 = (f32[120,128]{1,0:T(8,128)S(1)}, f32[120,128]{1,0:T(8,128)S(1)}, u32[]{:S(2)}, u32[]{:S(2)}) collective-permute-start(f32[120,128]{1,0:T(8,128)S(1)} %get-tuple-element.57), channel_id=1, source_target_pairs={{0,2},{1,3},{2,0},{3,1},{4,5},{5,4},{6,7},{7,6},{8,12},{9,13},{10,... | collective-permute-start | bytes 184328 | tf_op jit(solution)/shard_map/ppermute | solution.py:599
  9.0 0.1 %collective-permute-done.from_east.from_far = f32[48,128]{1,0:T(8,128)S(1)} collective-permute-done((f32[48,128]{1,0:T(8,128)S(1)}, f32[48,128]{1,0:T(8,128)S(1)}, u32[]{:S(2)}, u32[]{:S(2)}) %collective-permute-start) | collective-permute-done | bytes 24608 | tf_op jit(solution)/shard_map/ppermute | solution.py:599
  9.2 0.0 collective-permute-done.1.from_west
  9.2 0.5 %edge.1 = (f32[16,128]{1,0:T(8,128)S(1)}, f32[24,128]{1,0:T(8,128)S(1)}, f32[5,96,128]{2,1,0:T(8,128)S(1)}, f32[96,128]{1,0:T(8,128)S(1)}) custom-call(f32[5,96,128]{2,1,0:T(8,128)S(1)} %get-tuple-element.35.field, f32[5,96,128]{2,1,0:T(8,128)S(1)} %get-tuple-element.45.flux, f32[96,128]{1,0:T(8,128)S(1)} %get-tuple-element.46.packed, ...), custom_call_target="tpu_custom_call" | custom-call | flops 400000000 | bytes 12000000 | tf_op jit(solution)/shard_map/edge/pallas_call | solution.py:673
  9.7 1.2 %collective-permute-start.5 = (f32[24,128]{1,0:T(8,128)S(1)}, f32[24,128]{1,0:T(8,128)S(1)}, u32[]{:S(2)}, u32[]{:S(2)}) collective-permute-start(f32[24,128]{1,0:T(8,128)S(1)} %get-tuple-element.63), channel_id=1, source_target_pairs={{0,28},{1,0},{2,1},{3,2},{4,8},{5,9},{6,10},{7,11},{8,4},{9,5},{10... | collective-permute-start | bytes 36872 | tf_op jit(solution)/shard_map/ppermute | solution.py:616
  10.9 0.3 %collective-permute-start.4 = (f32[16,128]{1,0:T(8,128)S(1)}, f32[16,128]{1,0:T(8,128)S(1)}, u32[]{:S(2)}, u32[]{:S(2)}) collective-permute-start(f32[16,128]{1,0:T(8,128)S(1)} %get-tuple-element.58), channel_id=1, source_target_pairs={{0,4},{1,5},{2,6},{3,7},{4,0},{5,1},{6,2},{7,3},{8,12},{9,13},{10,... | collective-permute-start | bytes 24584 | tf_op jit(solution)/shard_map/ppermute | solution.py:616
  11.2 0.8 %middle.1 = (f32[5,96,128]{2,1,0:T(8,128)S(1)}, f32[96,128]{1,0:T(8,128)S(1)}, f32[5,80,128]{2,1,0:T(8,128)S(1)}, f32[96,128]{1,0:T(8,128)S(1)}) custom-call(f32[5,96,128]{2,1,0:T(8,128)S(1)} %get-tuple-element.35.field, s32[96,128]{1,0:T(8,128)S(1)} %get-tuple-element.36.offset, ...), custom_call_target="tpu_custom_call", output_to_operand_aliasing={{0}: (13, {}), {1}: (14, {})} | custom-call | tf_op jit(solution)/shard_map/middle/pallas_call | solution.py:688
  12.1 0.2 %collective-permute-done.2.rest = f32[72,128]{1,0:T(8,128)S(1)} collective-permute-done((f32[72,128]{1,0:T(8,128)S(1)}, f32[72,128]{1,0:T(8,128)S(1)}, u32[]{:S(2)}, u32[]{:S(2)}) %collective-permute-start.2) | collective-permute-done | bytes 36896 | tf_op jit(solution)/shard_map/ppermute | solution.py:599
  12.3 0.0 collective-permute-done.3.pole_two
  12.3 0.0 collective-permute-done.4.message_b.message_a
  12.3 1.4 %poles.1 = (f32[5,96,128]{2,1,0:T(8,128)S(1)}, f32[5,80,128]{2,1,0:T(8,128)S(1)}, f32[5,96,128]{2,1,0:T(8,128)}) custom-call(f32[5,96,128]{2,1,0:T(8,128)S(1)} %get-tuple-element.35.field, s32[96,128]{1,0:T(8,128)S(1)} %get-tuple-element.36.offset, f32[96,128]{1,0:T(8,128)S(1)} %get-tuple-element.37.part, ...), custom_call_target="tpu_custom_call", output_to_operand_aliasing={{0}: (11, {}), {1}: (12, {})} | custom-call | tf_op jit(solution)/shard_map/poles/pallas_call | solution.py:719
  13.7 0.0 collective-permute-done.5.message_b
  (3 shorter events, 0.0 us)
Async XLA Ops:
  1.9 7.3 %collective-permute-start.1 = (f32[144,128]{1,0:T(8,128)S(1)}, f32[144,128]{1,0:T(8,128)S(1)}, u32[]{:S(2)}, u32[]{:S(2)}) collective-permute-start(f32[144,128]{1,0:T(8,128)S(1)} %get-tuple-element.51), channel_id=1, source_target_pairs={{0,1},{1,2},{2,3},{3,0},{4,5},{5,6},{6,7},{7,4},{8,9},{9,10},{10,1... | collective-permute-start | bytes 221192 | tf_op jit(solution)/shard_map/ppermute | solution.py:599
  4.4 4.8 %collective-permute-start = (f32[48,128]{1,0:T(8,128)S(1)}, f32[48,128]{1,0:T(8,128)S(1)}, u32[]{:S(2)}, u32[]{:S(2)}) collective-permute-start(f32[48,128]{1,0:T(8,128)S(1)} %get-tuple-element.50), channel_id=1, source_target_pairs={{0,3},{1,0},{2,1},{3,2},{4,7},{5,4},{6,5},{7,6},{8,11},{9,8},{10,9... | collective-permute-start | bytes 73736 | tf_op jit(solution)/shard_map/ppermute | solution.py:599
  6.5 5.8 %collective-permute-start.2 = (f32[72,128]{1,0:T(8,128)S(1)}, f32[72,128]{1,0:T(8,128)S(1)}, u32[]{:S(2)}, u32[]{:S(2)}) collective-permute-start(f32[72,128]{1,0:T(8,128)S(1)} %get-tuple-element.56), channel_id=1, source_target_pairs={{0,1},{1,2},{2,3},{3,0},{4,5},{5,4},{6,7},{7,6},{8,12},{9,13},{10,... | collective-permute-start | bytes 110600 | tf_op jit(solution)/shard_map/ppermute | solution.py:599
  6.5 5.8 %collective-permute-start.3 = (f32[120,128]{1,0:T(8,128)S(1)}, f32[120,128]{1,0:T(8,128)S(1)}, u32[]{:S(2)}, u32[]{:S(2)}) collective-permute-start(f32[120,128]{1,0:T(8,128)S(1)} %get-tuple-element.57), channel_id=1, source_target_pairs={{0,2},{1,3},{2,0},{3,1},{4,5},{5,4},{6,7},{7,6},{8,12},{9,13},{10,... | collective-permute-start | bytes 184328 | tf_op jit(solution)/shard_map/ppermute | solution.py:599
  9.7 4.0 %collective-permute-start.5 = (f32[24,128]{1,0:T(8,128)S(1)}, f32[24,128]{1,0:T(8,128)S(1)}, u32[]{:S(2)}, u32[]{:S(2)}) collective-permute-start(f32[24,128]{1,0:T(8,128)S(1)} %get-tuple-element.63), channel_id=1, source_target_pairs={{0,28},{1,0},{2,1},{3,2},{4,8},{5,9},{6,10},{7,11},{8,4},{9,5},{10... | collective-permute-start | bytes 36872 | tf_op jit(solution)/shard_map/ppermute | solution.py:616
  10.9 1.4 %collective-permute-start.4 = (f32[16,128]{1,0:T(8,128)S(1)}, f32[16,128]{1,0:T(8,128)S(1)}, u32[]{:S(2)}, u32[]{:S(2)}) collective-permute-start(f32[16,128]{1,0:T(8,128)S(1)} %get-tuple-element.58), channel_id=1, source_target_pairs={{0,4},{1,5},{2,6},{3,7},{4,0},{5,1},{6,2},{7,3},{8,12},{9,13},{10,... | collective-permute-start | bytes 24584 | tf_op jit(solution)/shard_map/ppermute | solution.py:616

commit v8 on v7

--- a/solution.py
+++ b/solution.py
@@ -86,7 +86,7 @@
     ]
     for copy in copies:
         copy.start()
-    for copy in copies[:3]:
+    for copy in copies:
         copy.wait()
     shape = (row_count, cells)
     lane = lanes(shape)
@@ -133,7 +133,6 @@
             lat_count, field, offset, part, flux, seam_index, seam_part, block_matrix, seam_matrix, own_matrix
         )
     )
-    copies[3].wait()
 
 
 def pole_places(south, row_count):

time: 13.9 us -> 13.9 us (level)
  no operation moved by 1% of the time
where the time goes in v8:
time: 13.9 us; the launch traced here: 13.7 us
  starting transfers between devices  8.7 us (63%)
  Pallas kernels  4.58 us (33%)
  waiting for transfers between devices  0.42 us (3%)
    ppermute x4, starting transfers between devices, along_lon(): return lax.ppermute(value, ('lat', 'lon'), pairs)  7.15 us
    pallas_call x1, Pallas kernels, on_device(): pl.pallas_call(functools.partial(pack_kernel, lat_count), out_shape=[VMEM...  1.88 us
    ppermute x2, starting transfers between devices, along_lat(): return lax.ppermute(value, ('lat', 'lon'), pairs)  1.55 us
    pallas_call x1, Pallas kernels, on_device(): pl.pallas_call(functools.partial(poles_kernel, lat_count), out_shape=[VME...  1.35 us
    pallas_call x1, Pallas kernels, on_device(): pl.pallas_call(functools.partial(middle_kernel, lat_count), out_shape=[VM...  0.83 us
    pallas_call x1, Pallas kernels, on_device(): pl.pallas_call(functools.partial(edge_kernel, lat_count), out_shape=[VMEM...  0.48 us
    ppermute x4, waiting for transfers between devices, along_lon(): return lax.ppermute(value, ('lat', 'lon'), pairs)  0.37 us
  transfers between devices with their start and end apart: 6, of which 2 were waited for; matrix products, arithmetic and copies ran while one was open for 0% of the time, Pallas kernels for 19%

profile of v8, /device:TPU:0, one launch (start us, length us, event | category | flops | bytes accessed | tf_op | source)
XLA Modules:
  0.0 13.7 jit_solution(1829583653136832402)
XLA Ops:
  0.0 1.9 %pack.1 = (f32[5,96,128]{2,1,0:T(8,128)S(1)}, s32[96,128]{1,0:T(8,128)S(1)}, f32[96,128]{1,0:T(8,128)S(1)}, f32[96,128]{1,0:T(8,128)S(1)}, f32[96,128]{1,0:T(8,1...) custom-call(f32[5,96,128]{2,1,0:T(8,128)} %bitcast.4, ...), custom_call_target="tpu_custom_call" | custom-call | flops 100000000 | bytes 3000000 | tf_op jit(solution)/shard_map/pack/pallas_call | solution.py:626
  1.9 2.5 %collective-permute-start.1 = (f32[144,128]{1,0:T(8,128)S(1)}, f32[144,128]{1,0:T(8,128)S(1)}, u32[]{:S(2)}, u32[]{:S(2)}) collective-permute-start(f32[144,128]{1,0:T(8,128)S(1)} %get-tuple-element.51), channel_id=1, source_target_pairs={{0,1},{1,2},{2,3},{3,0},{4,5},{5,6},{6,7},{7,4},{8,9},{9,10},{10,1... | collective-permute-start | bytes 221192 | tf_op jit(solution)/shard_map/ppermute | solution.py:598
  4.4 2.1 %collective-permute-start = (f32[48,128]{1,0:T(8,128)S(1)}, f32[48,128]{1,0:T(8,128)S(1)}, u32[]{:S(2)}, u32[]{:S(2)}) collective-permute-start(f32[48,128]{1,0:T(8,128)S(1)} %get-tuple-element.50), channel_id=1, source_target_pairs={{0,3},{1,0},{2,1},{3,2},{4,7},{5,4},{6,5},{7,6},{8,11},{9,8},{10,9... | collective-permute-start | bytes 73736 | tf_op jit(solution)/shard_map/ppermute | solution.py:598
  6.5 0.0 collective-permute-start.2
  6.5 2.5 %collective-permute-start.3 = (f32[120,128]{1,0:T(8,128)S(1)}, f32[120,128]{1,0:T(8,128)S(1)}, u32[]{:S(2)}, u32[]{:S(2)}) collective-permute-start(f32[120,128]{1,0:T(8,128)S(1)} %get-tuple-element.57), channel_id=1, source_target_pairs={{0,2},{1,3},{2,0},{3,1},{4,5},{5,4},{6,7},{7,6},{8,12},{9,13},{10,... | collective-permute-start | bytes 184328 | tf_op jit(solution)/shard_map/ppermute | solution.py:598
  9.0 0.1 %collective-permute-done.from_east.from_far = f32[48,128]{1,0:T(8,128)S(1)} collective-permute-done((f32[48,128]{1,0:T(8,128)S(1)}, f32[48,128]{1,0:T(8,128)S(1)}, u32[]{:S(2)}, u32[]{:S(2)}) %collective-permute-start) | collective-permute-done | bytes 24608 | tf_op jit(solution)/shard_map/ppermute | solution.py:598
  9.2 0.0 collective-permute-done.1.from_west
  9.2 0.5 %edge.1 = (f32[16,128]{1,0:T(8,128)S(1)}, f32[24,128]{1,0:T(8,128)S(1)}, f32[5,96,128]{2,1,0:T(8,128)S(1)}, f32[96,128]{1,0:T(8,128)S(1)}) custom-call(f32[5,96,128]{2,1,0:T(8,128)S(1)} %get-tuple-element.35.field, f32[5,96,128]{2,1,0:T(8,128)S(1)} %get-tuple-element.45.flux, f32[96,128]{1,0:T(8,128)S(1)} %get-tuple-element.46.packed, ...), custom_call_target="tpu_custom_call" | custom-call | flops 400000000 | bytes 12000000 | tf_op jit(solution)/shard_map/edge/pallas_call | solution.py:672
  9.7 1.2 %collective-permute-start.5 = (f32[24,128]{1,0:T(8,128)S(1)}, f32[24,128]{1,0:T(8,128)S(1)}, u32[]{:S(2)}, u32[]{:S(2)}) collective-permute-start(f32[24,128]{1,0:T(8,128)S(1)} %get-tuple-element.63), channel_id=1, source_target_pairs={{0,28},{1,0},{2,1},{3,2},{4,8},{5,9},{6,10},{7,11},{8,4},{9,5},{10... | collective-permute-start | bytes 36872 | tf_op jit(solution)/shard_map/ppermute | solution.py:615
  10.9 0.3 %collective-permute-start.4 = (f32[16,128]{1,0:T(8,128)S(1)}, f32[16,128]{1,0:T(8,128)S(1)}, u32[]{:S(2)}, u32[]{:S(2)}) collective-permute-start(f32[16,128]{1,0:T(8,128)S(1)} %get-tuple-element.58), channel_id=1, source_target_pairs={{0,4},{1,5},{2,6},{3,7},{4,0},{5,1},{6,2},{7,3},{8,12},{9,13},{10,... | collective-permute-start | bytes 24584 | tf_op jit(solution)/shard_map/ppermute | solution.py:615
  11.2 0.8 %middle.1 = (f32[5,96,128]{2,1,0:T(8,128)S(1)}, f32[96,128]{1,0:T(8,128)S(1)}, f32[5,80,128]{2,1,0:T(8,128)S(1)}, f32[96,128]{1,0:T(8,128)S(1)}) custom-call(f32[5,96,128]{2,1,0:T(8,128)S(1)} %get-tuple-element.35.field, s32[96,128]{1,0:T(8,128)S(1)} %get-tuple-element.36.offset, ...), custom_call_target="tpu_custom_call", output_to_operand_aliasing={{0}: (13, {}), {1}: (14, {})} | custom-call | tf_op jit(solution)/shard_map/middle/pallas_call | solution.py:687
  12.1 0.2 %collective-permute-done.2.rest = f32[72,128]{1,0:T(8,128)S(1)} collective-permute-done((f32[72,128]{1,0:T(8,128)S(1)}, f32[72,128]{1,0:T(8,128)S(1)}, u32[]{:S(2)}, u32[]{:S(2)}) %collective-permute-start.2) | collective-permute-done | bytes 36896 | tf_op jit(solution)/shard_map/ppermute | solution.py:598
  12.3 0.0 collective-permute-done.3.pole_two
  12.3 0.0 collective-permute-done.4.message_b.message_a
  12.3 1.4 %poles.1 = (f32[5,96,128]{2,1,0:T(8,128)S(1)}, f32[5,80,128]{2,1,0:T(8,128)S(1)}, f32[5,96,128]{2,1,0:T(8,128)}) custom-call(f32[5,96,128]{2,1,0:T(8,128)S(1)} %get-tuple-element.35.field, s32[96,128]{1,0:T(8,128)S(1)} %get-tuple-element.36.offset, f32[96,128]{1,0:T(8,128)S(1)} %get-tuple-element.37.part, ...), custom_call_target="tpu_custom_call", output_to_operand_aliasing={{0}: (11, {}), {1}: (12, {})} | custom-call | tf_op jit(solution)/shard_map/poles/pallas_call | solution.py:718
  13.7 0.0 collective-permute-done.5.message_b
  (3 shorter events, 0.0 us)
Async XLA Ops:
  1.9 7.3 %collective-permute-start.1 = (f32[144,128]{1,0:T(8,128)S(1)}, f32[144,128]{1,0:T(8,128)S(1)}, u32[]{:S(2)}, u32[]{:S(2)}) collective-permute-start(f32[144,128]{1,0:T(8,128)S(1)} %get-tuple-element.51), channel_id=1, source_target_pairs={{0,1},{1,2},{2,3},{3,0},{4,5},{5,6},{6,7},{7,4},{8,9},{9,10},{10,1... | collective-permute-start | bytes 221192 | tf_op jit(solution)/shard_map/ppermute | solution.py:598
  4.4 4.8 %collective-permute-start = (f32[48,128]{1,0:T(8,128)S(1)}, f32[48,128]{1,0:T(8,128)S(1)}, u32[]{:S(2)}, u32[]{:S(2)}) collective-permute-start(f32[48,128]{1,0:T(8,128)S(1)} %get-tuple-element.50), channel_id=1, source_target_pairs={{0,3},{1,0},{2,1},{3,2},{4,7},{5,4},{6,5},{7,6},{8,11},{9,8},{10,9... | collective-permute-start | bytes 73736 | tf_op jit(solution)/shard_map/ppermute | solution.py:598
  6.5 5.8 %collective-permute-start.2 = (f32[72,128]{1,0:T(8,128)S(1)}, f32[72,128]{1,0:T(8,128)S(1)}, u32[]{:S(2)}, u32[]{:S(2)}) collective-permute-start(f32[72,128]{1,0:T(8,128)S(1)} %get-tuple-element.56), channel_id=1, source_target_pairs={{0,1},{1,2},{2,3},{3,0},{4,5},{5,4},{6,7},{7,6},{8,12},{9,13},{10,... | collective-permute-start | bytes 110600 | tf_op jit(solution)/shard_map/ppermute | solution.py:598
  6.5 5.8 %collective-permute-start.3 = (f32[120,128]{1,0:T(8,128)S(1)}, f32[120,128]{1,0:T(8,128)S(1)}, u32[]{:S(2)}, u32[]{:S(2)}) collective-permute-start(f32[120,128]{1,0:T(8,128)S(1)} %get-tuple-element.57), channel_id=1, source_target_pairs={{0,2},{1,3},{2,0},{3,1},{4,5},{5,4},{6,7},{7,6},{8,12},{9,13},{10,... | collective-permute-start | bytes 184328 | tf_op jit(solution)/shard_map/ppermute | solution.py:598
  9.7 4.0 %collective-permute-start.5 = (f32[24,128]{1,0:T(8,128)S(1)}, f32[24,128]{1,0:T(8,128)S(1)}, u32[]{:S(2)}, u32[]{:S(2)}) collective-permute-start(f32[24,128]{1,0:T(8,128)S(1)} %get-tuple-element.63), channel_id=1, source_target_pairs={{0,28},{1,0},{2,1},{3,2},{4,8},{5,9},{6,10},{7,11},{8,4},{9,5},{10... | collective-permute-start | bytes 36872 | tf_op jit(solution)/shard_map/ppermute | solution.py:615
  10.9 1.4 %collective-permute-start.4 = (f32[16,128]{1,0:T(8,128)S(1)}, f32[16,128]{1,0:T(8,128)S(1)}, u32[]{:S(2)}, u32[]{:S(2)}) collective-permute-start(f32[16,128]{1,0:T(8,128)S(1)} %get-tuple-element.58), channel_id=1, source_target_pairs={{0,4},{1,5},{2,6},{3,7},{4,0},{5,1},{6,2},{7,3},{8,12},{9,13},{10,... | collective-permute-start | bytes 24584 | tf_op jit(solution)/shard_map/ppermute | solution.py:615

commit v9 on v7

--- a/solution.py
+++ b/solution.py
@@ -16,7 +16,7 @@
 OFF_LANE = 120
 FRAC_LANE = 121
 PAIR = 4
-WITH_WEST = 2
+WITH_WEST = 3
 EDGE = 8
 
 f32 = jnp.float32
@@ -705,7 +705,7 @@
         out_shape=VMEM((depth * POLAR, cells), f32),
         in_specs=whole(3),
         out_specs=pl.BlockSpec(memory_space=VMEM),
-        cost_estimate=cost(0.3),
+        cost_estimate=cost(0.8),
         name="join",
     )(from_west, pole_one, far)
     pole_one, message_a, message_b = in_vmem(pole_one, message_a, message_b)

time: 13.9 us -> 13.9 us (level)
  transfers between devices with their start and end apart: 6 -> 6, of which waited for: 2 -> 3; matrix products, arithmetic and copies ran while one was open for 0% -> 0% of each run, Pallas kernels for 19% -> 20%
where the time goes in v9:
time: 13.9 us; the launch traced here: 13.7 us
  starting transfers between devices  8.6 us (62%)
  Pallas kernels  4.58 us (33%)
  waiting for transfers between devices  0.49 us (4%)
    ppermute x4, starting transfers between devices, along_lon(): return lax.ppermute(value, ('lat', 'lon'), pairs)  7.15 us
    pallas_call x1, Pallas kernels, on_device(): pl.pallas_call(functools.partial(pack_kernel, lat_count), out_shape=[VMEM...  1.87 us
    ppermute x2, starting transfers between devices, along_lat(): return lax.ppermute(value, ('lat', 'lon'), pairs)  1.45 us
    pallas_call x1, Pallas kernels, on_device(): pl.pallas_call(functools.partial(poles_kernel, lat_count), out_shape=[VME...  1.36 us
    pallas_call x1, Pallas kernels, on_device(): pl.pallas_call(functools.partial(middle_kernel, lat_count), out_shape=[VM...  0.84 us
    pallas_call x1, Pallas kernels, on_device(): pl.pallas_call(functools.partial(edge_kernel, lat_count), out_shape=[VMEM...  0.48 us
    ppermute x4, waiting for transfers between devices, along_lon(): return lax.ppermute(value, ('lat', 'lon'), pairs)  0.41 us
  transfers between devices with their start and end apart: 6, of which 3 were waited for; matrix products, arithmetic and copies ran while one was open for 0% of the time, Pallas kernels for 20%

profile of v9, /device:TPU:0, one launch (start us, length us, event | category | flops | bytes accessed | tf_op | source)
XLA Modules:
  0.0 13.7 jit_solution(8143926235327441371)
XLA Ops:
  0.0 1.9 %pack.1 = (f32[5,96,128]{2,1,0:T(8,128)S(1)}, s32[96,128]{1,0:T(8,128)S(1)}, f32[96,128]{1,0:T(8,128)S(1)}, f32[96,128]{1,0:T(8,128)S(1)}, f32[96,128]{1,0:T(8,1...) custom-call(f32[5,96,128]{2,1,0:T(8,128)} %bitcast.4, ...), custom_call_target="tpu_custom_call" | custom-call | flops 100000000 | bytes 3000000 | tf_op jit(solution)/shard_map/pack/pallas_call | solution.py:627
  1.9 2.5 %collective-permute-start.1 = (f32[168,128]{1,0:T(8,128)S(1)}, f32[168,128]{1,0:T(8,128)S(1)}, u32[]{:S(2)}, u32[]{:S(2)}) collective-permute-start(f32[168,128]{1,0:T(8,128)S(1)} %get-tuple-element.51), channel_id=1, source_target_pairs={{0,1},{1,2},{2,3},{3,0},{4,5},{5,6},{6,7},{7,4},{8,9},{9,10},{10,1... | collective-permute-start | bytes 258056 | tf_op jit(solution)/shard_map/ppermute | solution.py:599
  4.4 2.1 %collective-permute-start = (f32[48,128]{1,0:T(8,128)S(1)}, f32[48,128]{1,0:T(8,128)S(1)}, u32[]{:S(2)}, u32[]{:S(2)}) collective-permute-start(f32[48,128]{1,0:T(8,128)S(1)} %get-tuple-element.50), channel_id=1, source_target_pairs={{0,3},{1,0},{2,1},{3,2},{4,7},{5,4},{6,5},{7,6},{8,11},{9,8},{10,9... | collective-permute-start | bytes 73736 | tf_op jit(solution)/shard_map/ppermute | solution.py:599
  6.5 0.0 collective-permute-start.2
  6.5 2.5 %collective-permute-start.3 = (f32[120,128]{1,0:T(8,128)S(1)}, f32[120,128]{1,0:T(8,128)S(1)}, u32[]{:S(2)}, u32[]{:S(2)}) collective-permute-start(f32[120,128]{1,0:T(8,128)S(1)} %get-tuple-element.57), channel_id=1, source_target_pairs={{0,2},{1,3},{2,0},{3,1},{4,5},{5,4},{6,7},{7,6},{8,12},{9,13},{10,... | collective-permute-start | bytes 184328 | tf_op jit(solution)/shard_map/ppermute | solution.py:599
  9.0 0.1 %collective-permute-done.from_east.from_far = f32[48,128]{1,0:T(8,128)S(1)} collective-permute-done((f32[48,128]{1,0:T(8,128)S(1)}, f32[48,128]{1,0:T(8,128)S(1)}, u32[]{:S(2)}, u32[]{:S(2)}) %collective-permute-start) | collective-permute-done | bytes 24608 | tf_op jit(solution)/shard_map/ppermute | solution.py:599
  9.2 0.3 %collective-permute-done.1.from_west = f32[168,128]{1,0:T(8,128)S(1)} collective-permute-done((f32[168,128]{1,0:T(8,128)S(1)}, f32[168,128]{1,0:T(8,128)S(1)}, u32[]{:S(2)}, u32[]{:S(2)}) %collective-permute-start.1) | collective-permute-done | bytes 86048 | tf_op jit(solution)/shard_map/ppermute | solution.py:599
  9.4 0.5 %edge.1 = (f32[16,128]{1,0:T(8,128)S(1)}, f32[24,128]{1,0:T(8,128)S(1)}, f32[5,96,128]{2,1,0:T(8,128)S(1)}, f32[96,128]{1,0:T(8,128)S(1)}) custom-call(f32[5,96,128]{2,1,0:T(8,128)S(1)} %get-tuple-element.35.field, f32[5,96,128]{2,1,0:T(8,128)S(1)} %get-tuple-element.45.flux, f32[96,128]{1,0:T(8,128)S(1)} %get-tuple-element.46.packed, ...), custom_call_target="tpu_custom_call" | custom-call | flops 400000000 | bytes 12000000 | tf_op jit(solution)/shard_map/edge/pallas_call | solution.py:673
  9.9 1.0 %collective-permute-start.5 = (f32[24,128]{1,0:T(8,128)S(1)}, f32[24,128]{1,0:T(8,128)S(1)}, u32[]{:S(2)}, u32[]{:S(2)}) collective-permute-start(f32[24,128]{1,0:T(8,128)S(1)} %get-tuple-element.63), channel_id=1, source_target_pairs={{0,28},{1,0},{2,1},{3,2},{4,8},{5,9},{6,10},{7,11},{8,4},{9,5},{10... | collective-permute-start | bytes 36872 | tf_op jit(solution)/shard_map/ppermute | solution.py:616
  10.9 0.5 %collective-permute-start.4 = (f32[16,128]{1,0:T(8,128)S(1)}, f32[16,128]{1,0:T(8,128)S(1)}, u32[]{:S(2)}, u32[]{:S(2)}) collective-permute-start(f32[16,128]{1,0:T(8,128)S(1)} %get-tuple-element.58), channel_id=1, source_target_pairs={{0,4},{1,5},{2,6},{3,7},{4,0},{5,1},{6,2},{7,3},{8,12},{9,13},{10,... | collective-permute-start | bytes 24584 | tf_op jit(solution)/shard_map/ppermute | solution.py:616
  11.4 0.8 %middle.1 = (f32[5,96,128]{2,1,0:T(8,128)S(1)}, f32[96,128]{1,0:T(8,128)S(1)}, f32[5,80,128]{2,1,0:T(8,128)S(1)}, f32[96,128]{1,0:T(8,128)S(1)}) custom-call(f32[5,96,128]{2,1,0:T(8,128)S(1)} %get-tuple-element.35.field, s32[96,128]{1,0:T(8,128)S(1)} %get-tuple-element.36.offset, ...), custom_call_target="tpu_custom_call", output_to_operand_aliasing={{0}: (13, {}), {1}: (14, {})} | custom-call | tf_op jit(solution)/shard_map/middle/pallas_call | solution.py:688
  12.2 0.0 collective-permute-done.2.rest
  12.2 0.0 collective-permute-done.3.pole_two
  12.2 0.0 collective-permute-done.4.message_b.message_a
  12.3 1.4 %poles.1 = (f32[5,96,128]{2,1,0:T(8,128)S(1)}, f32[5,80,128]{2,1,0:T(8,128)S(1)}, f32[5,96,128]{2,1,0:T(8,128)}) custom-call(f32[5,96,128]{2,1,0:T(8,128)S(1)} %get-tuple-element.35.field, s32[96,128]{1,0:T(8,128)S(1)} %get-tuple-element.36.offset, f32[96,128]{1,0:T(8,128)S(1)} %get-tuple-element.37.part, ...), custom_call_target="tpu_custom_call", output_to_operand_aliasing={{0}: (11, {}), {1}: (12, {})} | custom-call | tf_op jit(solution)/shard_map/poles/pallas_call | solution.py:719
  13.6 0.1 collective-permute-done.5.message_b
  (3 shorter events, 0.0 us)
Async XLA Ops:
  1.9 7.6 %collective-permute-start.1 = (f32[168,128]{1,0:T(8,128)S(1)}, f32[168,128]{1,0:T(8,128)S(1)}, u32[]{:S(2)}, u32[]{:S(2)}) collective-permute-start(f32[168,128]{1,0:T(8,128)S(1)} %get-tuple-element.51), channel_id=1, source_target_pairs={{0,1},{1,2},{2,3},{3,0},{4,5},{5,6},{6,7},{7,4},{8,9},{9,10},{10,1... | collective-permute-start | bytes 258056 | tf_op jit(solution)/shard_map/ppermute | solution.py:599
  4.4 4.8 %collective-permute-start = (f32[48,128]{1,0:T(8,128)S(1)}, f32[48,128]{1,0:T(8,128)S(1)}, u32[]{:S(2)}, u32[]{:S(2)}) collective-permute-start(f32[48,128]{1,0:T(8,128)S(1)} %get-tuple-element.50), channel_id=1, source_target_pairs={{0,3},{1,0},{2,1},{3,2},{4,7},{5,4},{6,5},{7,6},{8,11},{9,8},{10,9... | collective-permute-start | bytes 73736 | tf_op jit(solution)/shard_map/ppermute | solution.py:599
  6.5 5.7 %collective-permute-start.2 = (f32[48,128]{1,0:T(8,128)S(1)}, f32[48,128]{1,0:T(8,128)S(1)}, u32[]{:S(2)}, u32[]{:S(2)}) collective-permute-start(f32[48,128]{1,0:T(8,128)S(1)} %get-tuple-element.56), channel_id=1, source_target_pairs={{0,1},{1,2},{2,3},{3,0},{4,5},{5,4},{6,7},{7,6},{8,12},{9,13},{10,... | collective-permute-start | bytes 73736 | tf_op jit(solution)/shard_map/ppermute | solution.py:599
  6.5 5.7 %collective-permute-start.3 = (f32[120,128]{1,0:T(8,128)S(1)}, f32[120,128]{1,0:T(8,128)S(1)}, u32[]{:S(2)}, u32[]{:S(2)}) collective-permute-start(f32[120,128]{1,0:T(8,128)S(1)} %get-tuple-element.57), channel_id=1, source_target_pairs={{0,2},{1,3},{2,0},{3,1},{4,5},{5,4},{6,7},{7,6},{8,12},{9,13},{10,... | collective-permute-start | bytes 184328 | tf_op jit(solution)/shard_map/ppermute | solution.py:599
  9.9 3.8 %collective-permute-start.5 = (f32[24,128]{1,0:T(8,128)S(1)}, f32[24,128]{1,0:T(8,128)S(1)}, u32[]{:S(2)}, u32[]{:S(2)}) collective-permute-start(f32[24,128]{1,0:T(8,128)S(1)} %get-tuple-element.63), channel_id=1, source_target_pairs={{0,28},{1,0},{2,1},{3,2},{4,8},{5,9},{6,10},{7,11},{8,4},{9,5},{10... | collective-permute-start | bytes 36872 | tf_op jit(solution)/shard_map/ppermute | solution.py:616
  10.9 1.3 %collective-permute-start.4 = (f32[16,128]{1,0:T(8,128)S(1)}, f32[16,128]{1,0:T(8,128)S(1)}, u32[]{:S(2)}, u32[]{:S(2)}) collective-permute-start(f32[16,128]{1,0:T(8,128)S(1)} %get-tuple-element.58), channel_id=1, source_target_pairs={{0,4},{1,5},{2,6},{3,7},{4,0},{5,1},{6,2},{7,3},{8,12},{9,13},{10,... | collective-permute-start | bytes 24584 | tf_op jit(solution)/shard_map/ppermute | solution.py:616

commit v10 on v7

--- a/solution.py
+++ b/solution.py
@@ -497,25 +497,14 @@
 
 
 def poles_kernel(
-    lat_count, field, offset, part, north, block_matrix, east, far, pole_one, pole_two, message_b, message_a,
-    given_wide, given_inner, wide, inner, out, faces, low, high, result, sems,
+    lat_count, field, offset, part, north, block_matrix, east, far, pole_one, pole_two, given_wide, given_inner,
+    wide, inner, faces,
 ):
     del given_wide, given_inner
 
     def polar_device(south):
         depth, row_count, cells = field.shape
-        near, beside = near_pole(south, row_count)
-        done = near + POLAR if south else EDGE
-        count = row_count - 2 * EDGE - POLAR
-        copies = [
-            pltpu.make_async_copy(
-                inner.at[:, pl.ds(first - EDGE, size)], out.at[:, pl.ds(first, size)], sems.at[2 + i]
-            )
-            for i, (first, size) in enumerate(((done, count), (near, beside)))
-        ]
-        copies[0].start()
-        first = static_places(south, row_count)[2]
-        rows = pl.ds(first, POLAR)
+        rows = pl.ds(static_places(south, row_count)[2], POLAR)
         own, west, west_two = stacked(field, rows), pole_one[...], pole_two[...]
         beyond = unpacked(far, rows, cells - WEST, depth)
         tables = jnp.concatenate(
@@ -527,14 +516,7 @@
             at = slice(t * POLAR, (t + 1) * POLAR)
             both = [split(tables[start : start + POLAR], cells) for start in (t * POLAR, (depth + t) * POLAR)]
             wide[t, rows] = rows_between(*both, west[at], west_two[at], -cells, *common)
-        inner_rows(wide, north, faces, inner, near, beside)
-        copies[1].start()
-        edge_rows(lat_count, wide, north, message_b, message_a, low, high, result)
-        copies += copy_edges(result, out, sems)
-        for copy in copies[2:]:
-            copy.start()
-        for copy in copies:
-            copy.wait()
+        inner_rows(wide, north, faces, inner, *near_pole(south, row_count))
 
     by_place(
         lat_count, None, functools.partial(polar_device, True), functools.partial(polar_device, False)
@@ -542,11 +524,11 @@
 
 
 def last_kernel(
-    lat_count, wide, inner, north, message_b, message_a, given_out, out, low, high, result, sems
+    lat_count, at_poles, wide, inner, north, message_b, message_a, given_out, out, low, high, result, sems
 ):
     del given_out
 
-    def away():
+    def finish():
         count = inner.shape[1]
         inner_copy = pltpu.make_async_copy(inner, out.at[:, pl.ds(EDGE, count)], sems.at[2])
         inner_copy.start()
@@ -558,7 +540,12 @@
             copy.wait()
 
     lat = lax.axis_index("lat")
-    pl.when((lat > 0) & (lat < lat_count - 1))(away)
+    polar = (lat == 0) | (lat == lat_count - 1)
+    pl.when(polar if at_poles else ~polar)(finish)
+
+
+def poles_output_kernel(lat_count, wide, inner, north, message_b, message_a, out, *scratch):
+    last_kernel(lat_count, True, wide, inner, north, message_b, message_a, None, out, *scratch)
 
 
 def cost(microseconds):
@@ -708,38 +695,47 @@
         cost_estimate=cost(0.3),
         name="join",
     )(from_west, pole_one, far)
-    pole_one, message_a, message_b = in_vmem(pole_one, message_a, message_b)
-    scratch = [
-        VMEM((depth, 3 * EDGE, cells), f32),
-        VMEM((depth, 3 * EDGE, cells), f32),
-        VMEM((2, depth, EDGE, cells), f32),
-        dma((4,)),
-    ]
+    (pole_one,) = in_vmem(pole_one)
+    wide, inner = in_vmem(
+        *pl.pallas_call(
+            functools.partial(poles_kernel, lat_count),
+            out_shape=[VMEM(stack, f32), inner],
+            in_specs=whole(11),
+            out_specs=whole(2),
+            scratch_shapes=[faces],
+            input_output_aliases={9: 0, 10: 1},
+            cost_estimate=cost(0.0),
+            name="poles",
+        )(field, offset, part, north, block_matrix, east, far, pole_one, pole_two, wide, inner_part)
+    )
+
+    message_a, message_b = in_vmem(message_a, message_b)
+    finish = dict(
+        out_shape=jax.ShapeDtypeStruct(stack, f32),
+        out_specs=pl.BlockSpec(memory_space=pl.ANY),
+        scratch_shapes=[
+            VMEM((depth, 3 * EDGE, cells), f32),
+            VMEM((depth, 3 * EDGE, cells), f32),
+            VMEM((2, depth, EDGE, cells), f32),
+            dma((3,)),
+        ],
+    )
     polar_b = message_b if lat_count % 2 else message_a
-    wide, inner, out = pl.pallas_call(
-        functools.partial(poles_kernel, lat_count),
-        out_shape=[VMEM(stack, f32), inner, jax.ShapeDtypeStruct(stack, f32)],
-        in_specs=whole(13),
-        out_specs=whole(2) + anywhere(1),
-        scratch_shapes=[faces, *scratch],
-        input_output_aliases={11: 0, 12: 1},
+    out = pl.pallas_call(
+        functools.partial(poles_output_kernel, lat_count),
+        in_specs=whole(5),
         cost_estimate=cost(0.0),
-        name="poles",
-    )(
-        field, offset, part, north, block_matrix, east, far, pole_one, pole_two, polar_b, message_a,
-        wide, inner_part,
-    )
-
+        name="poles_output",
+        **finish,
+    )(wide, inner, north, polar_b, message_a)
     out = pl.pallas_call(
-        functools.partial(last_kernel, lat_count),
-        out_shape=jax.ShapeDtypeStruct(stack, f32),
+        functools.partial(last_kernel, lat_count, False),
         in_specs=whole(5) + anywhere(1),
-        out_specs=pl.BlockSpec(memory_space=pl.ANY),
-        scratch_shapes=scratch,
         input_output_aliases={5: 0},
         cost_estimate=cost(0.7),
         name="last",
-    )(*in_vmem(wide, inner), north, message_b, message_a, out)
+        **finish,
+    )(wide, inner, north, message_b, message_a, out)
     return out.reshape(tracers.shape)
 
 

time: 13.9 us -> 13.9 us (level)
    pallas_call x1 -> x2, Pallas kernels: 0.04 us -> 0.77 us  [the longest x1 0.73 us: on_device(): pl.pallas_call(functools.partial(poles_output_kernel, lat_count), in_spec...]
    pallas_call x1, Pallas kernels: 1.36 us -> 0.67 us  [on_device(): pl.pallas_call(functools.partial(poles_kernel, lat_count), out_shape=[VME...]
  transfers between devices with their start and end apart: 6 -> 6, of which waited for: 2 -> 2; matrix products, arithmetic and copies ran while one was open for 0% -> 0% of each run, Pallas kernels for 19% -> 20%
where the time goes in v10:
time: 13.9 us; the launch traced here: 13.8 us
  starting transfers between devices  8.7 us (63%)
  Pallas kernels  4.62 us (33%)
  waiting for transfers between devices  0.38 us (3%)
    ppermute x4, starting transfers between devices, along_lon(): return lax.ppermute(value, ('lat', 'lon'), pairs)  7.15 us
    pallas_call x1, Pallas kernels, on_device(): pl.pallas_call(functools.partial(pack_kernel, lat_count), out_shape=[VMEM...  1.87 us
    ppermute x2, starting transfers between devices, along_lat(): return lax.ppermute(value, ('lat', 'lon'), pairs)  1.54 us
    pallas_call x1, Pallas kernels, on_device(): pl.pallas_call(functools.partial(middle_kernel, lat_count), out_shape=[VM...  0.83 us
    pallas_call x1, Pallas kernels, on_device(): pl.pallas_call(functools.partial(poles_output_kernel, lat_count), in_spec...  0.73 us
    pallas_call x1, Pallas kernels, on_device(): pl.pallas_call(functools.partial(poles_kernel, lat_count), out_shape=[VME...  0.67 us
    pallas_call x1, Pallas kernels, on_device(): pl.pallas_call(functools.partial(edge_kernel, lat_count), out_shape=[VMEM...  0.48 us
    ppermute x4, waiting for transfers between devices, along_lon(): return lax.ppermute(value, ('lat', 'lon'), pairs)  0.37 us
  transfers between devices with their start and end apart: 6, of which 2 were waited for; matrix products, arithmetic and copies ran while one was open for 0% of the time, Pallas kernels for 20%

profile of v10, /device:TPU:0, one launch (start us, length us, event | category | flops | bytes accessed | tf_op | source)
XLA Modules:
  0.0 13.8 jit_solution(7220372932947184290)
XLA Ops:
  0.0 1.9 %pack.1 = (f32[5,96,128]{2,1,0:T(8,128)S(1)}, s32[96,128]{1,0:T(8,128)S(1)}, f32[96,128]{1,0:T(8,128)S(1)}, f32[96,128]{1,0:T(8,128)S(1)}, f32[96,128]{1,0:T(8,1...) custom-call(f32[5,96,128]{2,1,0:T(8,128)} %bitcast.4, ...), custom_call_target="tpu_custom_call" | custom-call | flops 100000000 | bytes 3000000 | tf_op jit(solution)/shard_map/pack/pallas_call | solution.py:614
  1.9 2.5 %collective-permute-start.1 = (f32[144,128]{1,0:T(8,128)S(1)}, f32[144,128]{1,0:T(8,128)S(1)}, u32[]{:S(2)}, u32[]{:S(2)}) collective-permute-start(f32[144,128]{1,0:T(8,128)S(1)} %get-tuple-element.50), channel_id=1, source_target_pairs={{0,1},{1,2},{2,3},{3,0},{4,5},{5,6},{6,7},{7,4},{8,9},{9,10},{10,1... | collective-permute-start | bytes 221192 | tf_op jit(solution)/shard_map/ppermute | solution.py:586
  4.4 2.1 %collective-permute-start = (f32[48,128]{1,0:T(8,128)S(1)}, f32[48,128]{1,0:T(8,128)S(1)}, u32[]{:S(2)}, u32[]{:S(2)}) collective-permute-start(f32[48,128]{1,0:T(8,128)S(1)} %get-tuple-element.49), channel_id=1, source_target_pairs={{0,3},{1,0},{2,1},{3,2},{4,7},{5,4},{6,5},{7,6},{8,11},{9,8},{10,9... | collective-permute-start | bytes 73736 | tf_op jit(solution)/shard_map/ppermute | solution.py:586
  6.5 0.0 collective-permute-start.2
  6.5 2.5 %collective-permute-start.3 = (f32[120,128]{1,0:T(8,128)S(1)}, f32[120,128]{1,0:T(8,128)S(1)}, u32[]{:S(2)}, u32[]{:S(2)}) collective-permute-start(f32[120,128]{1,0:T(8,128)S(1)} %get-tuple-element.56), channel_id=1, source_target_pairs={{0,2},{1,3},{2,0},{3,1},{4,5},{5,4},{6,7},{7,6},{8,12},{9,13},{10,... | collective-permute-start | bytes 184328 | tf_op jit(solution)/shard_map/ppermute | solution.py:586
  9.0 0.1 %collective-permute-done.from_east.from_far = f32[48,128]{1,0:T(8,128)S(1)} collective-permute-done((f32[48,128]{1,0:T(8,128)S(1)}, f32[48,128]{1,0:T(8,128)S(1)}, u32[]{:S(2)}, u32[]{:S(2)}) %collective-permute-start) | collective-permute-done | bytes 24608 | tf_op jit(solution)/shard_map/ppermute | solution.py:586
  9.2 0.0 collective-permute-done.1.from_west
  9.2 0.5 %edge.1 = (f32[16,128]{1,0:T(8,128)S(1)}, f32[24,128]{1,0:T(8,128)S(1)}, f32[5,96,128]{2,1,0:T(8,128)S(1)}, f32[96,128]{1,0:T(8,128)S(1)}) custom-call(f32[5,96,128]{2,1,0:T(8,128)S(1)} %get-tuple-element.34.field, f32[5,96,128]{2,1,0:T(8,128)S(1)} %get-tuple-element.44.flux, f32[96,128]{1,0:T(8,128)S(1)} %get-tuple-element.45.packed, ...), custom_call_target="tpu_custom_call" | custom-call | flops 400000000 | bytes 12000000 | tf_op jit(solution)/shard_map/edge/pallas_call | solution.py:660
  9.7 1.2 %collective-permute-start.4 = (f32[24,128]{1,0:T(8,128)S(1)}, f32[24,128]{1,0:T(8,128)S(1)}, u32[]{:S(2)}, u32[]{:S(2)}) collective-permute-start(f32[24,128]{1,0:T(8,128)S(1)} %get-tuple-element.61), channel_id=1, source_target_pairs={{0,28},{1,0},{2,1},{3,2},{4,8},{5,9},{6,10},{7,11},{8,4},{9,5},{10... | collective-permute-start | bytes 36872 | tf_op jit(solution)/shard_map/ppermute | solution.py:603
  10.9 0.3 %collective-permute-start.5 = (f32[16,128]{1,0:T(8,128)S(1)}, f32[16,128]{1,0:T(8,128)S(1)}, u32[]{:S(2)}, u32[]{:S(2)}) collective-permute-start(f32[16,128]{1,0:T(8,128)S(1)} %get-tuple-element.62), channel_id=1, source_target_pairs={{0,4},{1,5},{2,6},{3,7},{4,0},{5,1},{6,2},{7,3},{8,12},{9,13},{10,... | collective-permute-start | bytes 24584 | tf_op jit(solution)/shard_map/ppermute | solution.py:603
  11.2 0.8 %middle.1 = (f32[5,96,128]{2,1,0:T(8,128)S(1)}, f32[96,128]{1,0:T(8,128)S(1)}, f32[5,80,128]{2,1,0:T(8,128)S(1)}, f32[96,128]{1,0:T(8,128)S(1)}) custom-call(f32[5,96,128]{2,1,0:T(8,128)S(1)} %get-tuple-element.34.field, s32[96,128]{1,0:T(8,128)S(1)} %get-tuple-element.35.offset, ...), custom_call_target="tpu_custom_call", output_to_operand_aliasing={{0}: (13, {}), {1}: (14, {})} | custom-call | tf_op jit(solution)/shard_map/middle/pallas_call | solution.py:675
  12.1 0.2 %collective-permute-done.2.rest = f32[72,128]{1,0:T(8,128)S(1)} collective-permute-done((f32[72,128]{1,0:T(8,128)S(1)}, f32[72,128]{1,0:T(8,128)S(1)}, u32[]{:S(2)}, u32[]{:S(2)}) %collective-permute-start.2) | collective-permute-done | bytes 36896 | tf_op jit(solution)/shard_map/ppermute | solution.py:586
  12.3 0.0 collective-permute-done.3.pole_two
  12.3 0.7 %poles.1 = (f32[5,96,128]{2,1,0:T(8,128)S(1)}, f32[5,80,128]{2,1,0:T(8,128)S(1)}) custom-call(f32[5,96,128]{2,1,0:T(8,128)S(1)} %get-tuple-element.34.field, s32[96,128]{1,0:T(8,128)S(1)} %get-tuple-element.35.offset, f32[96,128]{1,0:T(8,128)S(1)} %get-tuple-element.36.part, ...), custom_call_target="tpu_custom_call", output_to_operand_aliasing={{0}: (9, {}), {1}: (10, {})} | custom-call | tf_op jit(solution)/shard_map/poles/pallas_call | solution.py:700
  12.9 0.0 collective-permute-done.5.message_b.message_a
  13.0 0.7 %poles_output.1.given_out = f32[5,96,128]{2,1,0:T(8,128)} custom-call(f32[5,96,128]{2,1,0:T(8,128)S(1)} %get-tuple-element.59.wide, f32[5,80,128]{2,1,0:T(8,128)S(1)} %get-tuple-element.60.inner, f32[96,128]{1,0:T(8,128)S(1)} %get-tuple-element.37.north, f32[16,128]{1,0:T(8,128)S(1)} %collective-permute-done.5.message_b.message_a, ...), custom_call_target="tpu_custom_call" | custom-call | tf_op jit(solution)/shard_map/poles_output/pallas_call | solution.py:724
  13.7 0.0 collective-permute-done.4.message_b
  (3 shorter events, 0.1 us)
Async XLA Ops:
  1.9 7.3 %collective-permute-start.1 = (f32[144,128]{1,0:T(8,128)S(1)}, f32[144,128]{1,0:T(8,128)S(1)}, u32[]{:S(2)}, u32[]{:S(2)}) collective-permute-start(f32[144,128]{1,0:T(8,128)S(1)} %get-tuple-element.50), channel_id=1, source_target_pairs={{0,1},{1,2},{2,3},{3,0},{4,5},{5,6},{6,7},{7,4},{8,9},{9,10},{10,1... | collective-permute-start | bytes 221192 | tf_op jit(solution)/shard_map/ppermute | solution.py:586
  4.4 4.8 %collective-permute-start = (f32[48,128]{1,0:T(8,128)S(1)}, f32[48,128]{1,0:T(8,128)S(1)}, u32[]{:S(2)}, u32[]{:S(2)}) collective-permute-start(f32[48,128]{1,0:T(8,128)S(1)} %get-tuple-element.49), channel_id=1, source_target_pairs={{0,3},{1,0},{2,1},{3,2},{4,7},{5,4},{6,5},{7,6},{8,11},{9,8},{10,9... | collective-permute-start | bytes 73736 | tf_op jit(solution)/shard_map/ppermute | solution.py:586
  6.5 5.8 %collective-permute-start.2 = (f32[72,128]{1,0:T(8,128)S(1)}, f32[72,128]{1,0:T(8,128)S(1)}, u32[]{:S(2)}, u32[]{:S(2)}) collective-permute-start(f32[72,128]{1,0:T(8,128)S(1)} %get-tuple-element.55), channel_id=1, source_target_pairs={{0,1},{1,2},{2,3},{3,0},{4,5},{5,4},{6,7},{7,6},{8,12},{9,13},{10,... | collective-permute-start | bytes 110600 | tf_op jit(solution)/shard_map/ppermute | solution.py:586
  6.5 5.8 %collective-permute-start.3 = (f32[120,128]{1,0:T(8,128)S(1)}, f32[120,128]{1,0:T(8,128)S(1)}, u32[]{:S(2)}, u32[]{:S(2)}) collective-permute-start(f32[120,128]{1,0:T(8,128)S(1)} %get-tuple-element.56), channel_id=1, source_target_pairs={{0,2},{1,3},{2,0},{3,1},{4,5},{5,4},{6,7},{7,6},{8,12},{9,13},{10,... | collective-permute-start | bytes 184328 | tf_op jit(solution)/shard_map/ppermute | solution.py:586
  9.7 4.0 %collective-permute-start.4 = (f32[24,128]{1,0:T(8,128)S(1)}, f32[24,128]{1,0:T(8,128)S(1)}, u32[]{:S(2)}, u32[]{:S(2)}) collective-permute-start(f32[24,128]{1,0:T(8,128)S(1)} %get-tuple-element.61), channel_id=1, source_target_pairs={{0,28},{1,0},{2,1},{3,2},{4,8},{5,9},{6,10},{7,11},{8,4},{9,5},{10... | collective-permute-start | bytes 36872 | tf_op jit(solution)/shard_map/ppermute | solution.py:603
  10.9 2.0 %collective-permute-start.5 = (f32[16,128]{1,0:T(8,128)S(1)}, f32[16,128]{1,0:T(8,128)S(1)}, u32[]{:S(2)}, u32[]{:S(2)}) collective-permute-start(f32[16,128]{1,0:T(8,128)S(1)} %get-tuple-element.62), channel_id=1, source_target_pairs={{0,4},{1,5},{2,6},{3,7},{4,0},{5,1},{6,2},{7,3},{8,12},{9,13},{10,... | collective-permute-start | bytes 24584 | tf_op jit(solution)/shard_map/ppermute | solution.py:603
